TPU v7x, 32 devices: a whole 2x2x4 slice. The times are simulated.
32 devices in a mesh: rows: 16 (over z, x, core), dates: 2 (over y).
Axes of the slice: x: 2, y: 2, z: 4, core: 2. Of those that a mesh axis runs over, the one named last changes fastest.
Arguments:
- obs_mask: int32 [16, 128, 4096], P('dates', 'rows'), may hold values 0 or 1
- precision: float32 [16, 128, 4096], P('dates', 'rows'), may hold values from 0.5 to 4
- observed: float32 [16, 128, 4096], P('dates', 'rows')
- edge_class: int32 [2, 128, 4096], P(None, 'rows'), may hold values from 0 to 7
- temporal_weight: float32 [15], replicated, may hold values from 0.5 to 4
- inverse: bfloat16 [16, 16, 128, 4096], P(None, None, 'rows', 'dates'), as said below
Outputs:
- solution: float32 [16, 128, 4096], P('dates', 'rows')
- residual: float32 [16, 128, 4096], P('dates', 'rows')
Inputs may be any that keep to these rules, and one draw needn't show every extreme that they name: `inverse`: each pixel's matrix is symmetric with a diagonal larger than the sum of magnitudes of its row's other entries.
All inputs are finite; a program needn't handle non-finite values. No bound on the sum of `obs_mask` on one device may be relied on, other than what follows from the above.
Results may differ from a plain program's by a relative error of at most 0.0065.
Values sent between devices are 32-bit elements; how exact they have to be, the bound alone decides.
No kernel may reach another device: no remote copies, remote signals or barrier semaphores. Data moves between devices by JAX's collectives and lax.ppermute only.
A program may use at most 64 MiB of HBM per device.

v0:
```python
import jax
import jax.numpy as jnp
from jax import lax
from jax.sharding import PartitionSpec as P

ITERS = 2


mass_term = 0.1


def passed_along(value, axis, steps):
    count = lax.axis_size(axis)
    leading, last = (max(0, -steps), min(count, count - steps))
    return lax.ppermute(value, axis, [(source, source + steps) for source in range(leading, last)])


def padded_2(block, sides, width):
    for axis, dim in sides:
        count = lax.axis_size(axis)
        forward = [(i, i + 1) for i in range(count - 1)]
        backward = [(target, source) for source, target in forward]
        low = lax.ppermute(
            lax.slice_in_dim(block, block.shape[dim] - width, None, axis=dim), axis, forward
        )
        high = lax.ppermute(lax.slice_in_dim(block, 0, width, axis=dim), axis, backward)
        block = jnp.concatenate([low, block, high], axis=dim)
    return block


def edge_weights(edge_class, line_start, lines_total):
    classes = edge_class.astype(jnp.float32)
    rows_here = edge_class.shape[1]
    columns = edge_class.shape[2]
    col_ids = lax.broadcasted_iota(jnp.int32, (rows_here, columns), 1)
    row_ids = lax.broadcasted_iota(jnp.int32, (rows_here, columns), 0) + line_start
    across = jnp.where(col_ids == columns - 1, 0.0, 0.25 * (classes[0] + 1.0))
    downward = jnp.where(row_ids == lines_total - 1, 0.0, 0.25 * (classes[1] + 1.0))
    return (across, downward)


def operate(
    field, padded, data_weight, across, across_prev, downward, downward_prev, tau_up, tau_down
):
    total = (mass_term + data_weight) * field
    total = (
        total
        + across * (field - padded[1:-1, 1:-1, 2:])
        + across_prev * (field - padded[1:-1, 1:-1, :-2])
    )
    total = (
        total
        + downward * (field - padded[1:-1, 2:, 1:-1])
        + downward_prev * (field - padded[1:-1, :-2, 1:-1])
    )
    total = (
        total
        + tau_up * (field - padded[2:, 1:-1, 1:-1])
        + tau_down * (field - padded[:-2, 1:-1, 1:-1])
    )
    return total


def apply_inverse(inverse, values):
    total = inverse[:, 0].astype(jnp.float32) * values[0][None]
    for source in range(1, values.shape[0]):
        total = total + inverse[:, source].astype(jnp.float32) * values[source][None]
    return total


def norm_total(residual, precond):
    return lax.psum(jnp.sum(residual * precond), ("rows", "dates"))


def solve(rhs, operator, precondition):
    solution = jnp.zeros_like(rhs)
    residual = rhs
    precond = precondition(residual)
    search = precond
    rz_now = norm_total(residual, precond)
    for iteration in range(ITERS):
        image = operator(search)
        alpha = rz_now / lax.psum(jnp.sum(search * image), ("rows", "dates"))
        solution = solution + alpha * search
        residual = residual - alpha * image
        if iteration + 1 < ITERS:
            precond = precondition(residual)
            rz_next = norm_total(residual, precond)
            search = precond + rz_next / rz_now * search
            rz_now = rz_next
    return (solution, residual)


def body(obs_mask, precision, observed, edge_class, temporal_weight, inverse):
    dates_here, rows_here, columns = observed.shape
    line_start = lax.axis_index("rows") * rows_here
    lines_total = rows_here * lax.axis_size("rows")
    date_start = lax.axis_index("dates") * dates_here
    data_weight = obs_mask.astype(jnp.float32) * precision
    across, downward = edge_weights(edge_class, line_start, lines_total)
    zero_one = jnp.zeros((1,), jnp.float32)
    tau_ext = jnp.concatenate([zero_one, temporal_weight, zero_one])
    across_prev = jnp.pad(across, ((0, 0), (1, 0)))[:, :-1]
    above_row = passed_along(downward[-1:], "rows", 1)
    downward_prev = jnp.concatenate([above_row, downward[:-1]], axis=0)
    tau_up = lax.dynamic_slice_in_dim(tau_ext, date_start + 1, dates_here, 0)[:, None, None]
    tau_down = lax.dynamic_slice_in_dim(tau_ext, date_start, dates_here, 0)[:, None, None]

    def operator(field):
        padded = padded_2(field, (("rows", 1), ("dates", 0)), 1)
        padded = jnp.pad(padded, ((0, 0), (0, 0), (1, 1)))
        return operate(
            field,
            padded,
            data_weight,
            across,
            across_prev,
            downward,
            downward_prev,
            tau_up,
            tau_down,
        )

    def precondition(values):
        series = lax.all_to_all(values, "dates", split_axis=2, concat_axis=0, tiled=True)
        mapped = apply_inverse(inverse, series)
        return lax.all_to_all(mapped, "dates", split_axis=0, concat_axis=2, tiled=True)

    solution, residual = solve(data_weight * observed, operator, precondition)
    return (solution, residual)


def solution(mesh):
    return jax.shard_map(
        body,
        mesh=mesh,
        in_specs=(
            P("dates", "rows", None),
            P("dates", "rows", None),
            P("dates", "rows", None),
            P(None, "rows", None),
            P(),
            P(None, None, "rows", "dates"),
        ),
        out_specs=(P("dates", "rows", None), P("dates", "rows", None)),
        check_vma=False,
    )
```

profile of v0, /device:TPU:0, one launch (start us, length us, event | category | flops | bytes accessed | tf_op | source)
XLA Modules:
  0.0 373.7 jit_solution(12620194795726065900)
XLA Ops:
  0.6 2.0 fusion.65
  2.6 8.7 %copy.265 = f32[8,8,4096]{1,0,2:T(8,128)} copy(f32[8,8,4096]{2,1,0:T(8,128)S(1)} %fusion.65) | data formatting | bytes 2097152 | tf_op jit(solution)/shard_map/mul | solution.py:129
  11.4 17.2 %reshape.73 = f32[2,1,131072]{2,1,0:T(1,128)} reshape(f32[4096,8,8]{2,1,0:T(8,128)} %bitcast.187) | data formatting | bytes 2097152
  28.6 4.2 %all-to-all-start = ((f32[2,1,131072]{2,1,0:T(1,128)}), f32[2,1,131072]{2,1,0:T(1,128)S(1)}, u32[]{:S(2)}, u32[]{:S(2)}) async-start(f32[2,1,131072]{2,1,0:T(1,128)} %reshape.73), calls=%async_computation | async-start | bytes 2097152 | tf_op jit(solution)/shard_map/all_to_all | solution.py:125
  32.9 0.7 bitcast_select_fusion.1
  33.6 0.7 slice.350
  34.3 2.5 collective-permute-start.4
  36.8 10.5 %all-to-all-done = f32[2,1,131072]{2,1,0:T(1,128)S(1)} async-done(((f32[2,1,131072]{2,1,0:T(1,128)}), f32[2,1,131072]{2,1,0:T(1,128)S(1)}, u32[]{:S(2)}, u32[]{:S(2)}) %all-to-all-start) | async-done | bytes 1048608 | tf_op jit(solution)/shard_map/all_to_all | solution.py:125
  47.8 4.0 %reduce = f32[2,131072]{1,0:T(2,128)S(1)} reduce(f32[2,1,131072]{2,1,0:T(1,128)S(1)} %all-to-all-done, f32[]{:T(128)} %broadcast.99), dimensions={1}, to_apply=%all_to_all.52.reduce_sub_computation | reduce | bytes 2097156 | tf_op jit(solution)/shard_map/all_to_all | solution.py:125
  51.8 15.8 %reshape.74 = f32[4096,8,8]{2,1,0:T(8,128)} reshape(f32[2,131072]{1,0:T(2,128)S(1)} %reduce) | data formatting | bytes 2097152
  67.5 10.2 %copy.299 = f32[8,8,2,2048]{3,2,1,0:T(2,128)S(1)} copy(f32[8,8,2,2048]{1,0,3,2:T(8,128)} %bitcast.185) | data formatting | bytes 2097152 | tf_op jit(solution)/shard_map/all_to_all | solution.py:125
  78.5 5.2 %fusion.15 = f32[16,8,2048]{2,1,0:T(8,128)} fusion(f32[8,2048]{1,0:T(8,128)S(1)} %get-tuple-element.40, f32[8,2048]{1,0:T(8,128)S(1)} %get-tuple-element.41, f32[8,2048]{1,0:T(8,128)S(1)} %get-tuple-element.42, f32[8,2048]{1,0:T(8,128)S(1)} %get-tuple-element.43, f32[8,2048]{1,0:T(8,128)S(1)} %get-tuple-element.44, f32[8,2048]{1,0:T(8,128)S(1)} %get-tuple-element.45, ...), kind=kLoop, calls=%fused_computation.57 | loop fusion | flops 12320768 | bytes 10485760 | tf_op jit(solution)/shard_map/add | solution.py:67
  83.7 3.7 all-to-all-start.1
  87.5 0.7 select_bitcast_fusion.1
  88.3 12.5 %all-to-all-done.1 = f32[16,8,2048]{2,1,0:T(8,128)S(1)} async-done(((f32[16,8,2048]{2,1,0:T(8,128)}), f32[16,8,2048]{2,1,0:T(8,128)S(1)}, u32[]{:S(2)}, u32[]{:S(2)}) %all-to-all-start.1) | async-done | bytes 1048608 | tf_op jit(solution)/shard_map/all_to_all | solution.py:127
  101.2 1.3 collective-permute-start.1
  102.5 3.0 collective-permute-start
  106.8 1.4 collective-permute-start.3
  108.2 4.6 %collective-permute-start.2 = (f32[1,10,4096]{2,1,0:T(8,128)S(1)}, f32[1,10,4096]{2,1,0:T(8,128)S(1)}, u32[]{:S(2)}, u32[]{:S(2)}) collective-permute-start(f32[1,10,4096]{2,1,0:T(8,128)S(1)} %get-tuple-element.18), channel_id=1, source_target_pairs={{0,1},{2,3},{4,5},{6,7},{8,9},{10,11},{12,13},{14,15},{16,17},{18,... | collective-permute-start | bytes 491528 | tf_op jit(solution)/shard_map/ppermute | solution.py:23
  112.8 0.7 pad_maximum_fusion.22
  113.6 3.4 collective-permute-done.3
  117.0 1.8 collective-permute-done.2
  118.8 1.3 select_maximum_fusion.4
  120.2 3.3 multiply_reduce_fusion.2
  123.5 43.1 %all-reduce.3 = (f32[]{:T(128)}, f32[]{:T(128)}) all-reduce(f32[]{:T(128)} %get-tuple-element.9, f32[]{:T(128)} %get-tuple-element.8), channel_id=1, replica_groups=mesh['rows'=16,'dates'=2] {'rows','dates'}, use_global_device_ids=true, to_apply=%region_1.2 | all-reduce | flops 2 | bytes 16 | tf_op jit(solution)/shard_map/psum | solution.py:72
  167.9 1.3 multiply_subtract_fusion.1
  169.3 8.7 %copy.289 = f32[8,8,4096]{1,0,2:T(8,128)} copy(f32[8,8,4096]{2,1,0:T(8,128)S(1)} %multiply_subtract_fusion.1) | data formatting | bytes 2097152 | tf_op jit(solution)/shard_map/sub | solution.py:85
  178.0 15.6 %reshape.75 = f32[2,1,131072]{2,1,0:T(1,128)S(1)} reshape(f32[4096,8,8]{2,1,0:T(8,128)} %bitcast.188) | data formatting | bytes 2097152
  193.6 16.7 %all_to_all.72 = f32[2,1,131072]{2,1,0:T(1,128)} all-to-all(f32[2,1,131072]{2,1,0:T(1,128)S(1)} %reshape.75), channel_id=1, replica_groups=mesh['rows'=16,'dates'=2] {'dates'}, dimensions={0} | all-to-all | bytes 2097152 | tf_op jit(solution)/shard_map/all_to_all | solution.py:125
  210.3 4.9 %reduce.1 = f32[2,131072]{1,0:T(2,128)S(1)} reduce(f32[2,1,131072]{2,1,0:T(1,128)} %all_to_all.72, f32[]{:T(128)} %broadcast.99), dimensions={1}, to_apply=%all_to_all.60.reduce_sub_computation | reduce | bytes 2097156 | tf_op jit(solution)/shard_map/all_to_all | solution.py:125
  215.2 15.8 %reshape.76 = f32[4096,8,8]{2,1,0:T(8,128)} reshape(f32[2,131072]{1,0:T(2,128)S(1)} %reduce.1) | data formatting | bytes 2097152
  231.0 9.8 %copy.300 = f32[8,8,2,2048]{3,2,1,0:T(2,128)S(1)} copy(f32[8,8,2,2048]{1,0,3,2:T(8,128)} %bitcast.186) | data formatting | bytes 2097152 | tf_op jit(solution)/shard_map/all_to_all | solution.py:125
  241.5 4.7 %fusion.30 = f32[16,8,2048]{2,1,0:T(8,128)S(1)} fusion(f32[8,2048]{1,0:T(8,128)S(1)} %get-tuple-element.22, f32[8,2048]{1,0:T(8,128)S(1)} %get-tuple-element.23, f32[8,2048]{1,0:T(8,128)S(1)} %get-tuple-element.24, f32[8,2048]{1,0:T(8,128)S(1)} %get-tuple-element.25, f32[8,2048]{1,0:T(8,128)S(1)} %get-tuple-element.26, f32[8,2048]{1,0:T(8,128)S(1)} %get-tuple-element.27, ...), kind=kLoop, calls=%fused_computation.72 | loop fusion | flops 12320768 | bytes 10485760 | tf_op jit(solution)/shard_map/add | solution.py:67
  246.2 14.3 %all_to_all.73 = f32[16,8,2048]{2,1,0:T(8,128)S(1)} all-to-all(f32[16,8,2048]{2,1,0:T(8,128)S(1)} %fusion.30), channel_id=1, replica_groups=mesh['rows'=16,'dates'=2] {'dates'}, dimensions={0} | all-to-all | bytes 2097152 | tf_op jit(solution)/shard_map/all_to_all | solution.py:127
  260.7 0.9 multiply_reduce_fusion.1
  261.6 39.8 %psum.30 = f32[]{:T(128)} all-reduce(f32[]{:T(128)} %multiply_reduce_fusion.1), channel_id=1, replica_groups=mesh['rows'=16,'dates'=2] {'rows','dates'}, use_global_device_ids=true, to_apply=%region_5.6 | all-reduce | flops 1 | bytes 8 | tf_op jit(solution)/shard_map/psum | solution.py:72
  302.6 1.3 multiply_add_fusion.1
  304.3 1.3 collective-permute-start.6
  305.6 3.0 collective-permute-start.5
  308.8 0.8 collective-permute-done.5
  309.9 1.4 collective-permute-start.8
  311.4 4.6 %collective-permute-start.7 = (f32[1,10,4096]{2,1,0:T(8,128)S(1)}, f32[1,10,4096]{2,1,0:T(8,128)S(1)}, u32[]{:S(2)}, u32[]{:S(2)}) collective-permute-start(f32[1,10,4096]{2,1,0:T(8,128)S(1)} %get-tuple-element.16), channel_id=1, source_target_pairs={{0,1},{2,3},{4,5},{6,7},{8,9},{10,11},{12,13},{14,15},{16,17},{18,... | collective-permute-start | bytes 491528 | tf_op jit(solution)/shard_map/ppermute | solution.py:23
  315.9 3.2 collective-permute-done.8
  319.2 1.8 collective-permute-done.7
  320.9 1.3 select_maximum_fusion
  322.3 3.2 multiply_reduce_fusion
  325.5 43.9 %psum.31 = f32[]{:T(128)} all-reduce(f32[]{:T(128)} %get-tuple-element.12), channel_id=1, replica_groups=mesh['rows'=16,'dates'=2] {'rows','dates'}, use_global_device_ids=true, to_apply=%region_7.8 | all-reduce | flops 1 | bytes 8 | tf_op jit(solution)/shard_map/psum | solution.py:83
  370.7 2.8 multiply_subtract_fusion
  (55 shorter events, 4.5 us)
Async XLA Ops:
  11.4 21.5 %copy-start.11 = (s32[2,8,4096]{2,1,0:T(8,128)S(1)}, s32[2,8,4096]{2,1,0:T(8,128)}, u32[]{:S(2)}) copy-start(s32[2,8,4096]{2,1,0:T(8,128)} %param.9) | copy-start | bytes 786436
  28.6 18.7 %all-to-all-start = ((f32[2,1,131072]{2,1,0:T(1,128)}), f32[2,1,131072]{2,1,0:T(1,128)S(1)}, u32[]{:S(2)}, u32[]{:S(2)}) async-start(f32[2,1,131072]{2,1,0:T(1,128)} %reshape.73), calls=%async_computation | async-start | bytes 2097152 | tf_op jit(solution)/shard_map/all_to_all | solution.py:125
  33.6 0.7 copy-start.8
  34.3 78.6 %collective-permute-start.4 = (f32[1,4096]{1,0:T(1,128)}, f32[1,4096]{1,0:T(1,128)}, u32[]{:S(2)}, u32[]{:S(2)}) collective-permute-start(f32[1,4096]{1,0:T(1,128)} %slice.350), channel_id=1, source_target_pairs={{0,2},{2,4},{4,6},{6,8},{8,10},{10,12},{12,14},{14,16},{16,18},{18... | collective-permute-start | bytes 49160 | tf_op jit(solution)/shard_map/ppermute | solution.py:15
  83.7 4.5 %copy-start.10 = (f32[8,4096]{1,0:T(8,128)S(1)}, f32[8,4096]{1,0:T(8,128)}, u32[]{:S(2)}) copy-start(f32[8,4096]{1,0:T(8,128)} %get-tuple-element.57) | copy-start | bytes 393220
  83.7 21.9 %copy-start.12 = (f32[15]{0:T(128)S(1)}, f32[15]{0:T(128)}, u32[]{:S(2)}) copy-start(f32[15]{0:T(128)} %param.10) | copy-start | bytes 184
  83.7 17.0 %all-to-all-start.1 = ((f32[16,8,2048]{2,1,0:T(8,128)}), f32[16,8,2048]{2,1,0:T(8,128)S(1)}, u32[]{:S(2)}, u32[]{:S(2)}) async-start(f32[16,8,2048]{2,1,0:T(8,128)} %fusion.15), calls=%async_computation.1 | async-start | bytes 2097152 | tf_op jit(solution)/shard_map/all_to_all | solution.py:127
  100.9 12.0 %copy-start.9 = (f32[8,4096]{1,0:T(8,128)S(1)}, f32[8,4096]{1,0:T(8,128)}, u32[]{:S(2)}) copy-start(f32[8,4096]{1,0:T(8,128)} %copy-done.8) | copy-start | bytes 393220
  101.2 4.5 %collective-permute-start.1 = (f32[8,1,4096]{2,0,1:T(8,128)S(1)}, f32[8,1,4096]{2,0,1:T(8,128)S(1)}, u32[]{:S(2)}, u32[]{:S(2)}) collective-permute-start(f32[8,1,4096]{2,0,1:T(8,128)S(1)} %copy.284), channel_id=1, source_target_pairs={{2,0},{4,2},{6,4},{8,6},{10,8},{12,10},{14,12},{16,14},{18,16},{20... | collective-permute-start | bytes 393224 | tf_op jit(solution)/shard_map/ppermute | solution.py:26
  102.5 4.0 %collective-permute-start = (f32[8,1,4096]{2,0,1:T(8,128)S(1)}, f32[8,1,4096]{2,0,1:T(8,128)S(1)}, u32[]{:S(2)}, u32[]{:S(2)}) collective-permute-start(f32[8,1,4096]{2,0,1:T(8,128)S(1)} %copy.283), channel_id=1, source_target_pairs={{0,2},{2,4},{4,6},{6,8},{8,10},{10,12},{12,14},{14,16},{16,18},{18... | collective-permute-start | bytes 393224 | tf_op jit(solution)/shard_map/ppermute | solution.py:23
  106.8 13.4 %copy-start.1 = (f32[8,8,4096]{2,1,0:T(8,128)S(1)}, f32[8,8,4096]{2,1,0:T(8,128)}, u32[]{:S(2)}) copy-start(f32[8,8,4096]{2,1,0:T(8,128)} %param.7) | copy-start | bytes 3145732
  106.8 13.4 %copy-start.3 = (s32[8,8,4096]{2,1,0:T(8,128)S(1)}, s32[8,8,4096]{2,1,0:T(8,128)}, u32[]{:S(2)}) copy-start(s32[8,8,4096]{2,1,0:T(8,128)} %param.6) | copy-start | bytes 3145732
  106.8 13.4 %copy-start.5 = (f32[8,4096]{1,0:T(8,128)S(1)}, f32[8,4096]{1,0:T(8,128)}, u32[]{:S(2)}) copy-start(f32[8,4096]{1,0:T(8,128)} %get-tuple-element.56) | copy-start | bytes 393220
  106.8 10.2 %collective-permute-start.3 = (f32[1,10,4096]{2,1,0:T(8,128)S(1)}, f32[1,10,4096]{2,1,0:T(8,128)S(1)}, u32[]{:S(2)}, u32[]{:S(2)}) collective-permute-start(f32[1,10,4096]{2,1,0:T(8,128)S(1)} %get-tuple-element.17), channel_id=1, source_target_pairs={{1,0},{3,2},{5,4},{7,6},{9,8},{11,10},{13,12},{15,14},{17,16},{19,... | collective-permute-start | bytes 491528 | tf_op jit(solution)/shard_map/ppermute | solution.py:26
  108.2 10.6 %collective-permute-start.2 = (f32[1,10,4096]{2,1,0:T(8,128)S(1)}, f32[1,10,4096]{2,1,0:T(8,128)S(1)}, u32[]{:S(2)}, u32[]{:S(2)}) collective-permute-start(f32[1,10,4096]{2,1,0:T(8,128)S(1)} %get-tuple-element.18), channel_id=1, source_target_pairs={{0,1},{2,3},{4,5},{6,7},{8,9},{10,11},{12,13},{14,15},{16,17},{18,... | collective-permute-start | bytes 491528 | tf_op jit(solution)/shard_map/ppermute | solution.py:23
  113.6 9.9 %copy-start.6 = (f32[8,4096]{1,0:T(8,128)}, f32[8,4096]{1,0:T(8,128)S(1)}, u32[]{:S(2)}) copy-start(f32[8,4096]{1,0:T(8,128)S(1)} %pad_maximum_fusion.22) | copy-start | bytes 393220
  260.6 40.7 %copy-start = (f32[2,8,8,2048]{3,2,0,1:T(8,128)}, f32[2,8,8,2048]{3,2,0,1:T(8,128)S(1)}, u32[]{:S(2)}) copy-start(f32[2,8,8,2048]{3,2,0,1:T(8,128)S(1)} %copy.292) | copy-start | bytes 3145732
  304.3 4.4 %collective-permute-start.6 = (f32[8,1,4096]{2,0,1:T(8,128)S(1)}, f32[8,1,4096]{2,0,1:T(8,128)S(1)}, u32[]{:S(2)}, u32[]{:S(2)}) collective-permute-start(f32[8,1,4096]{2,0,1:T(8,128)S(1)} %copy.294), channel_id=1, source_target_pairs={{2,0},{4,2},{6,4},{8,6},{10,8},{12,10},{14,12},{16,14},{18,16},{20... | collective-permute-start | bytes 393224 | tf_op jit(solution)/shard_map/ppermute | solution.py:26
  305.6 4.0 %collective-permute-start.5 = (f32[8,1,4096]{2,0,1:T(8,128)S(1)}, f32[8,1,4096]{2,0,1:T(8,128)S(1)}, u32[]{:S(2)}, u32[]{:S(2)}) collective-permute-start(f32[8,1,4096]{2,0,1:T(8,128)S(1)} %copy.293), channel_id=1, source_target_pairs={{0,2},{2,4},{4,6},{6,8},{8,10},{10,12},{12,14},{14,16},{16,18},{18... | collective-permute-start | bytes 393224 | tf_op jit(solution)/shard_map/ppermute | solution.py:23
  309.9 12.4 %copy-start.2 = (f32[8,8,4096]{2,1,0:T(8,128)S(1)}, f32[8,8,4096]{2,1,0:T(8,128)}, u32[]{:S(2)}) copy-start(f32[8,8,4096]{2,1,0:T(8,128)} %param.7) | copy-start | bytes 3145732
  309.9 12.4 %copy-start.4 = (s32[8,8,4096]{2,1,0:T(8,128)S(1)}, s32[8,8,4096]{2,1,0:T(8,128)}, u32[]{:S(2)}) copy-start(s32[8,8,4096]{2,1,0:T(8,128)} %param.6) | copy-start | bytes 3145732
  309.9 12.4 %copy-start.7 = (f32[8,4096]{1,0:T(8,128)S(1)}, f32[8,4096]{1,0:T(8,128)}, u32[]{:S(2)}) copy-start(f32[8,4096]{1,0:T(8,128)} %copy-done.6) | copy-start | bytes 393220
  309.9 9.3 %collective-permute-start.8 = (f32[1,10,4096]{2,1,0:T(8,128)S(1)}, f32[1,10,4096]{2,1,0:T(8,128)S(1)}, u32[]{:S(2)}, u32[]{:S(2)}) collective-permute-start(f32[1,10,4096]{2,1,0:T(8,128)S(1)} %get-tuple-element.15), channel_id=1, source_target_pairs={{1,0},{3,2},{5,4},{7,6},{9,8},{11,10},{13,12},{15,14},{17,16},{19,... | collective-permute-start | bytes 491528 | tf_op jit(solution)/shard_map/ppermute | solution.py:26
  311.4 9.6 %collective-permute-start.7 = (f32[1,10,4096]{2,1,0:T(8,128)S(1)}, f32[1,10,4096]{2,1,0:T(8,128)S(1)}, u32[]{:S(2)}, u32[]{:S(2)}) collective-permute-start(f32[1,10,4096]{2,1,0:T(8,128)S(1)} %get-tuple-element.16), channel_id=1, source_target_pairs={{0,1},{2,3},{4,5},{6,7},{8,9},{10,11},{12,13},{14,15},{16,17},{18,... | collective-permute-start | bytes 491528 | tf_op jit(solution)/shard_map/ppermute | solution.py:23
where the time goes:
time: 380 us; the launch traced here: 374 us
  blocking collectives  158 us (42%)
  local copies, waits for them, and re-layouts  106 us (28%)
  other arithmetic  38.8 us (10%)
  waiting for transfers between devices  34.6 us (9%)
  starting transfers between devices  31.1 us (8%)
  between operations  5.25 us (1%)
    psum x2, blocking collectives, norm_total(): return lax.psum(jnp.sum(residual * precond), ('rows', 'dates'))  82.9 us
    unnamed x30, local copies, waits for them, and re-layouts  64.5 us
    psum x1, blocking collectives, solve(): alpha = rz_now / lax.psum(jnp.sum(search * image), ('rows', 'dates'))  43.9 us
    all_to_all x5, local copies, waits for them, and re-layouts, precondition(): lax.all_to_all(values, 'dates', split_axis=2, concat_axis=0, tiled=True)  21.8 us
    all_to_all x1, blocking collectives, precondition(): lax.all_to_all(values, 'dates', split_axis=2, concat_axis=0, tiled=True)  16.7 us
    ppermute x4, starting transfers between devices, padded_2(): lax.ppermute(lax.slice_in_dim(block, block.shape[dim] - width, None, axis...  15.2 us
    all_to_all x1, blocking collectives, precondition(): lax.all_to_all(mapped, 'dates', split_axis=0, concat_axis=2, tiled=True)  14.3 us
    all_to_all x1, waiting for transfers between devices, precondition(): lax.all_to_all(mapped, 'dates', split_axis=0, concat_axis=2, tiled=True)  12.5 us
  transfers between devices with their start and end apart: 11, of which 8 were waited for; matrix products, arithmetic and copies ran while one was open for 11% of the time, Pallas kernels for 0%

commit v1 on v0

v1 whole, which is shorter than its diff:
```python
import functools

import jax
import jax.numpy as jnp
from jax import lax
from jax.experimental import pallas as pl
from jax.experimental.pallas import tpu as pltpu
from jax.sharding import PartitionSpec as P

MASS = 0.1
LANES = 128
VMEM = pl.BlockSpec(memory_space=pltpu.VMEM)
SMEM = pl.BlockSpec(memory_space=pltpu.SMEM)
PARAMS = pltpu.CompilerParams(vmem_limit_bytes=32 * 1024 * 1024)


def call(kernel, out_shapes, scratch, scalars, arrays):
    return pl.pallas_call(
        kernel,
        out_shape=[jax.ShapeDtypeStruct(shape, jnp.float32) for shape in out_shapes],
        in_specs=[SMEM] * len(scalars) + [VMEM] * len(arrays),
        out_specs=[VMEM] * len(out_shapes),
        scratch_shapes=[pltpu.VMEM(shape, jnp.float32) for shape in scratch],
        compiler_params=PARAMS,
    )(*scalars, *arrays)


def tile(index):
    return pl.ds(pl.multiple_of(index * LANES, LANES), LANES)


def columns(block, width):
    return pl.ds(pl.multiple_of(block * width, LANES), width)


def row_ids(width):
    return lax.broadcasted_iota(jnp.int32, (8, width), 0)


def lane_ids(width):
    return lax.broadcasted_iota(jnp.int32, (8, width), 1)


def window_start(block, dates_here, length, dates):
    return jnp.clip(block * dates_here - 1, 0, dates - length)


def edge_rows(value, parity):
    top, bottom = value[0:1], value[7:8]
    return jnp.where(parity == 0, bottom, top), jnp.where(parity == 0, top, bottom)


def halo_rows(first, second, parity):
    above = jnp.where(parity == 0, second, first)
    below = jnp.where(parity == 0, first, second)
    return above, below


def stencil(value, above, below, left, right, later, earlier, weights, diagonal, tau_up, tau_down):
    across, across_prev, downward, downward_prev = weights
    width = value.shape[1]
    rows, lanes = row_ids(width), lane_ids(width)
    next_column = jnp.where(lanes == width - 1, right, pltpu.roll(value, width - 1, 1))
    prev_column = jnp.where(lanes == 0, left, pltpu.roll(value, 1, 1))
    next_row = jnp.where(rows == 7, below, pltpu.roll(value, 7, 0))
    prev_row = jnp.where(rows == 0, above, pltpu.roll(value, 1, 0))
    away = across * next_column + across_prev * prev_column
    away = away + downward * next_row + downward_prev * prev_row
    return diagonal * value - (away + tau_up * later + tau_down * earlier)


def apply_inverse(inverse, source, store, first_total):
    dates = inverse.shape[0]

    def step(index, total):
        lanes = tile(index)
        values = [source[s, :, lanes] for s in range(dates)]
        for t in range(dates):
            mapped = inverse[t, 0, :, lanes].astype(jnp.float32) * values[0]
            for s in range(1, dates):
                mapped = mapped + inverse[t, s, :, lanes].astype(jnp.float32) * values[s]
            total = total + values[t] * mapped
            store(t, lanes, mapped)
        return total

    return lax.fori_loop(0, source.shape[2] // LANES, step, first_total)


def pack_edges(field, parity, first, second, ends):
    dates, _, width = field.shape
    lanes = lane_ids(LANES)
    begin = jnp.zeros((8, LANES), jnp.float32)
    end = begin
    for t in range(dates):
        value = field[t]
        send_1, send_2 = edge_rows(value, parity)
        first[t : t + 1, :] = send_1
        second[t : t + 1, :] = send_2
        begin = jnp.where(lanes == t, value[:, 0:1], begin)
        end = jnp.where(lanes == t, value[:, width - 1 : width], end)
    ends[0:8, :] = begin
    ends[8:16, :] = end


def gather_dates(target, own, received, date_block, blocks, dates_here):
    for j in range(dates_here):
        target[date_block * dates_here + j] = own(j)
    for k in range(1, blocks):
        source = lax.rem(date_block + blocks - k, blocks)
        for j in range(dates_here):
            target[source * dates_here + j] = received[k - 1, j]


def send_windows(field, windows, date_block, blocks, dates_here):
    length = windows.shape[1]
    for k in range(1, blocks):
        target = lax.rem(date_block + k, blocks)
        start = window_start(target, dates_here, length, field.shape[0])
        for j in range(length):
            windows[k - 1, j] = field[start + j]


def first_kernel(blocks, place, mask, precision, observed, received, inverse, precond, first, second, ends, windows, dot, rhs):
    date_block, parity = place[0], place[1]
    dates_here = observed.shape[0]
    here = columns(date_block, rhs.shape[2])

    def own(j):
        return mask[j, :, here].astype(jnp.float32) * precision[j, :, here] * observed[j, :, here]

    gather_dates(rhs, own, received, date_block, blocks, dates_here)

    def store(t, lanes, value):
        precond[t, :, lanes] = value

    dot[...] = apply_inverse(inverse, rhs, store, jnp.zeros((8, LANES), jnp.float32))
    pack_edges(precond, parity, first, second, ends)
    send_windows(precond, windows, date_block, blocks, dates_here)


def pixel_image(place, tau, weights_all, field, halo_1, halo_2, ends_left, ends_right, data_weight, use):
    date_block, parity = place[0], place[1]
    dates, _, width = field.shape
    here = columns(date_block, width)
    weights = [weights_all[k, :, here] for k in range(4)]
    weight_sum = weights_all[4, :, here]
    for t in range(dates):
        above, below = halo_rows(halo_1[t : t + 1, :], halo_2[t : t + 1, :], parity)
        tau_up, tau_down = tau[t + 1], tau[t]
        value = field[t]
        diagonal = weight_sum + data_weight[t] + (tau_up + tau_down)
        image = stencil(
            value,
            above,
            below,
            ends_left[:, t : t + 1],
            ends_right[:, t : t + 1],
            field[min(t + 1, dates - 1)],
            field[max(t - 1, 0)],
            weights,
            diagonal,
            tau_up,
            tau_down,
        )
        use(t, value, image)


def fold(value):
    total = value[:, :LANES]
    for index in range(1, value.shape[1] // LANES):
        total = total + value[:, index * LANES : (index + 1) * LANES]
    return total


def second_kernel(
    blocks, place, tau, weights, precond, halo_1, halo_2, ends_left, ends_right, mask, precision, received, inverse,
    mapped, first, second, ends, windows, edges, data_weight, dot_image, dot_mapped, image_all, total,
):
    date_block, parity = place[0], place[1]
    dates_here = mask.shape[0]
    here = columns(date_block, precond.shape[2])

    def own(j):
        return mask[j, :, here].astype(jnp.float32) * precision[j, :, here]

    gather_dates(data_weight, own, received, date_block, blocks, dates_here)
    total[...] = jnp.zeros_like(total)

    def use(t, value, image):
        image_all[t] = image
        total[...] = total[...] + fold(value * image)

    pixel_image(place, tau, weights, precond, halo_1, halo_2, ends_left, ends_right, data_weight, use)
    dot_image[...] = total[...]

    def store(t, lanes, value):
        mapped[t, :, lanes] = value

    dot_mapped[...] = apply_inverse(inverse, image_all, store, jnp.zeros((8, LANES), jnp.float32))
    pack_edges(mapped, parity, first, second, ends)
    send_windows(mapped, windows, date_block, blocks, dates_here)
    for k in range(1, blocks):
        target = lax.rem(date_block + k, blocks)
        for j in range(dates_here):
            send_1, send_2 = edge_rows(mapped[target * dates_here + j], parity)
            edges[k - 1, j : j + 1, :] = send_1
            edges[k - 1, dates_here + j : dates_here + j + 1, :] = send_2


def third_kernel(place, tau, weights, mapped, halo_1, halo_2, ends_left, ends_right, data_weight, dot_1, dot_2, dot_3, sums, total):
    total[...] = jnp.zeros_like(total)

    def use(t, value, image):
        total[...] = total[...] + fold(value * image)

    pixel_image(place, tau, weights, mapped, halo_1, halo_2, ends_left, ends_right, data_weight, use)
    rows = row_ids(LANES)
    result = jnp.zeros((8, LANES), jnp.float32)
    for index, dot in enumerate((dot_1, dot_2, dot_3, total)):
        result = jnp.where(rows == index, jnp.sum(dot[...]), result)
    sums[...] = result


def last_kernel(
    blocks, place, tau, weights_all, sums, precond, mapped, precond_other, mapped_other, own_p1, own_p2, own_m1, own_m2,
    other_1, other_2, mask, precision, observed, solution, residual, field, above_all, below_all,
):
    date_block, parity = place[0], place[1]
    dates, _, width = precond.shape
    dates_here, _, all_columns = observed.shape
    length = field.shape[0]
    one = sums[0:1, :]
    two = sums[1:2, :]
    three = sums[2:3, :]
    four = sums[3:4, :]
    alpha = one / two
    rz = alpha * alpha * three - one
    ahead = 1.0 + rz / one
    curve = ahead * ahead * two - 2.0 * ahead * alpha * three + alpha * alpha * four
    alpha_last = rz / curve
    scale_p = jnp.tile(alpha + alpha_last * ahead, (1, width // LANES))
    scale_m = jnp.tile(-alpha_last * alpha, (1, width // LANES))

    def mix(p, m):
        return scale_p * p + scale_m * m

    start = window_start(date_block, dates_here, length, dates)
    offset = date_block * dates_here - start
    here = columns(date_block, width)
    for j in range(length):
        field[j, :, here] = mix(precond[start + j], mapped[start + j])
    for j in range(dates_here):
        date = pl.ds(date_block * dates_here + j, 1)
        above, below = halo_rows(mix(own_p1[date, :], own_m1[date, :]), mix(own_p2[date, :], own_m2[date, :]), parity)
        above_all[j : j + 1, here] = above
        below_all[j : j + 1, here] = below
    for k in range(1, blocks):
        there = columns(lax.rem(date_block + blocks - k, blocks), width)
        for j in range(length):
            field[j, :, there] = mix(precond_other[k - 1, j], mapped_other[k - 1, j])
        for j in range(dates_here):
            p, m = slice(j, j + 1), slice(dates_here + j, dates_here + j + 1)
            above, below = halo_rows(
                mix(other_1[k - 1, p, :], other_1[k - 1, m, :]), mix(other_2[k - 1, p, :], other_2[k - 1, m, :]), parity
            )
            above_all[j : j + 1, there] = above
            below_all[j : j + 1, there] = below
    weights = [weights_all[k] for k in range(4)]
    weight_sum = weights_all[4]
    for j in range(dates_here):
        tau_up, tau_down = tau[date_block * dates_here + j + 1], tau[date_block * dates_here + j]
        data_weight = mask[j].astype(jnp.float32) * precision[j]
        place_j = offset + j
        value = field[place_j]
        image = stencil(
            value,
            above_all[j : j + 1, :],
            below_all[j : j + 1, :],
            0.0,
            0.0,
            field[jnp.minimum(place_j + 1, length - 1)],
            field[jnp.maximum(place_j - 1, 0)],
            weights,
            weight_sum + data_weight + (tau_up + tau_down),
            tau_up,
            tau_down,
        )
        solution[j] = value
        residual[j] = data_weight * observed[j] - image


def body(blocks, slabs, obs_mask, precision, observed, edge_class, temporal_weight, inverse):
    dates_here, lines, all_columns = observed.shape
    dates = inverse.shape[0]
    width = all_columns // blocks
    length = min(dates_here + (1 if blocks == 2 else 2), dates)
    line_block = lax.axis_index("rows")
    date_block = lax.axis_index("dates")
    parity = lax.rem(line_block, 2)
    place = jnp.stack([date_block, parity]).astype(jnp.int32)

    pairs = [(i, i ^ 1) for i in range(slabs)]
    across_pairs = [(i, i + 1) for i in range(1, slabs - 1, 2)]
    across_pairs = across_pairs + [(b, a) for a, b in across_pairs]

    def rotate(value, k):
        return lax.ppermute(value, "dates", [(i, (i + k) % blocks) for i in range(blocks)])

    def swap_rows(first, second):
        return lax.ppermute(first, "rows", pairs), lax.ppermute(second, "rows", across_pairs)

    def swap_ends(ends):
        if blocks == 2:
            other = rotate(ends, 1)
            return other[8:16], other[0:8]
        forward = [(i, i + 1) for i in range(blocks - 1)]
        backward = [(b, a) for a, b in forward]
        return lax.ppermute(ends[8:16], "dates", forward), lax.ppermute(ends[0:8], "dates", backward)

    def send(stack):
        return jnp.stack([rotate(stack[k - 1], k) for k in range(1, blocks)])

    def part(value, k):
        there = lax.rem(date_block + k, blocks) * width
        return lax.dynamic_slice_in_dim(value, there, width, 2)

    def weight(k):
        return part(obs_mask, k).astype(jnp.float32) * part(precision, k)

    rhs_other = jnp.stack([rotate(weight(k) * part(observed, k), k) for k in range(1, blocks)])
    weight_other = jnp.stack([rotate(weight(k), k) for k in range(1, blocks)])

    classes = edge_class.astype(jnp.float32)
    col_ids = lax.broadcasted_iota(jnp.int32, (lines, all_columns), 1)
    line_ids = lax.broadcasted_iota(jnp.int32, (lines, all_columns), 0) + line_block * lines
    across = jnp.where(col_ids == all_columns - 1, 0.0, 0.25 * (classes[0] + 1.0))
    downward = jnp.where(line_ids == lines * slabs - 1, 0.0, 0.25 * (classes[1] + 1.0))
    across_prev = jnp.pad(across, ((0, 0), (1, 0)))[:, :-1]
    above_row = lax.ppermute(downward[-1:], "rows", [(i, i + 1) for i in range(slabs - 1)])
    downward_prev = jnp.concatenate([above_row, downward[:-1]], axis=0)
    weights = jnp.stack([across, across_prev, downward, downward_prev, MASS + across + across_prev + downward + downward_prev])
    zero_one = jnp.zeros((1,), jnp.float32)
    tau = jnp.concatenate([zero_one, temporal_weight, zero_one])

    pixel = (dates, lines, width)
    rows = (dates, width)
    ends_shape = (16, LANES)
    vector = (8, LANES)
    window_shape = (blocks - 1, length, lines, width)

    precond, p_first, p_second, p_ends, p_windows, dot_1 = call(
        functools.partial(first_kernel, blocks),
        [pixel, rows, rows, ends_shape, window_shape, vector],
        [pixel],
        [place],
        [obs_mask, precision, observed, rhs_other, inverse],
    )
    p_halo_1, p_halo_2 = swap_rows(p_first, p_second)
    p_left, p_right = swap_ends(p_ends)
    mapped, m_first, m_second, m_ends, m_windows, m_edges, data_weight, dot_2, dot_3 = call(
        functools.partial(second_kernel, blocks),
        [pixel, rows, rows, ends_shape, window_shape, (blocks - 1, 2 * dates_here, width), pixel, vector, vector],
        [pixel, vector],
        [place, tau],
        [weights, precond, p_halo_1, p_halo_2, p_left, p_right, obs_mask, precision, weight_other, inverse],
    )
    m_halo_1, m_halo_2 = swap_rows(m_first, m_second)
    m_left, m_right = swap_ends(m_ends)
    (sums,) = call(
        third_kernel,
        [vector],
        [vector],
        [place, tau],
        [weights, mapped, m_halo_1, m_halo_2, m_left, m_right, data_weight, dot_1, dot_2, dot_3],
    )
    edges_other = send(m_edges)
    precond_other = send(p_windows)
    mapped_other = send(m_windows)
    steps = 1
    while steps < slabs:
        sums = sums + lax.ppermute(sums, "rows", [(i, i ^ steps) for i in range(slabs)])
        steps *= 2
    steps = 1
    while steps < blocks:
        sums = sums + lax.ppermute(sums, "dates", [(i, i ^ steps) for i in range(blocks)])
        steps *= 2

    start = window_start(date_block, dates_here, length, dates)
    own_dates = lax.dynamic_slice_in_dim(precond_other, date_block * dates_here - start, dates_here, 1)
    top, bottom = own_dates[:, :, 0], own_dates[:, :, 7]
    p_edge_1 = jnp.where(parity == 0, bottom, top)
    p_edge_2 = jnp.where(parity == 0, top, bottom)
    other_1, other_2 = swap_rows(
        jnp.concatenate([p_edge_1, edges_other[:, :dates_here]], axis=1),
        jnp.concatenate([p_edge_2, edges_other[:, dates_here:]], axis=1),
    )
    out = (dates_here, lines, all_columns)
    return tuple(
        call(
            functools.partial(last_kernel, blocks),
            [out, out],
            [(length, lines, all_columns), (dates_here, all_columns), (dates_here, all_columns)],
            [place, tau],
            [
                weights, sums, precond, mapped, precond_other, mapped_other, p_halo_1, p_halo_2, m_halo_1, m_halo_2,
                other_1, other_2, obs_mask, precision, observed,
            ],
        )
    )


def solution(mesh):
    return jax.shard_map(
        functools.partial(body, mesh.shape["dates"], mesh.shape["rows"]),
        mesh=mesh,
        in_specs=(
            P("dates", "rows", None),
            P("dates", "rows", None),
            P("dates", "rows", None),
            P(None, "rows", None),
            P(),
            P(None, None, "rows", "dates"),
        ),
        out_specs=(P("dates", "rows", None), P("dates", "rows", None)),
        check_vma=False,
    )
```

time: 380 us -> 94.9 us (0.25); the launches traced: 374 us -> 94.2 us
  blocking collectives: 158 us -> 0 us
  local copies, waits for them, and re-layouts: 106 us -> 21.4 us
  other arithmetic: 38.8 us -> 4.43 us
  waiting for transfers between devices: 34.6 us -> 18.8 us
  Pallas kernels: 0 us -> 15.5 us
  between operations: 5.25 us -> 0.94 us
    psum x3 -> x0, blocking collectives: 127 us -> none  [the longest x2 82.9 us: norm_total(): return lax.psum(jnp.sum(residual * precond), ('rows', 'dates'))]
    unnamed x30 -> x45, local copies, waits for them, and re-layouts: 64.5 us -> 20.1 us
    all_to_all x2 -> x0, blocking collectives: 31 us -> none  [the longest x1 16.7 us: precondition(): lax.all_to_all(values, 'dates', split_axis=2, concat_axis=0, tiled=True)]
    all_to_all x2 -> x0, waiting for transfers between devices: 23 us -> none  [the longest x1 12.5 us: precondition(): lax.all_to_all(mapped, 'dates', split_axis=0, concat_axis=2, tiled=True)]
    all_to_all x7 -> x0, local copies, waits for them, and re-layouts: 22 us -> none  [the longest x5 21.8 us: precondition(): lax.all_to_all(values, 'dates', split_axis=2, concat_axis=0, tiled=True)]
    pallas_call x0 -> x4, Pallas kernels: none -> 15.5 us  [call(): pl.pallas_call(kernel, out_shape=[jax.ShapeDtypeStruct(shape, jnp.float32...]
    add x3 -> x5, other arithmetic: 11.3 us -> 0.02 us  [the longest x4 0.01 us: body(): sums + lax.ppermute(sums, 'rows', [(i, i ^ steps) for i in range(slabs)])]
    ppermute x9 -> x19, starting transfers between devices: 23.2 us -> 33.1 us  [the longest x3 9.61 us: swap_rows(): lax.ppermute(first, 'rows', pairs)]
  transfers between devices with their start and end apart: 11 -> 19, of which waited for: 8 -> 6; matrix products, arithmetic and copies ran while one was open for 11% -> 5% of each run, Pallas kernels for 0% -> 12%
where the time goes in v1:
time: 94.9 us; the launch traced here: 94.2 us
  starting transfers between devices  33.1 us (35%)
  local copies, waits for them, and re-layouts  21.4 us (23%)
  waiting for transfers between devices  18.8 us (20%)
  Pallas kernels  15.5 us (16%)
  other arithmetic  4.43 us (5%)
    unnamed x45, local copies, waits for them, and re-layouts  20.1 us
    pallas_call x4, Pallas kernels, call(): pl.pallas_call(kernel, out_shape=[jax.ShapeDtypeStruct(shape, jnp.float32...  15.5 us
    ppermute x7, waiting for transfers between devices, rotate(): lax.ppermute(value, 'dates', [(i, (i + k) % blocks) for i in range(blocks)])  10.5 us
    ppermute x3, starting transfers between devices, swap_rows(): lax.ppermute(first, 'rows', pairs)  9.61 us
    ppermute x4, starting transfers between devices, body(): lax.ppermute(sums, 'rows', [(i, i ^ steps) for i in range(slabs)])  9.48 us
    ppermute x7, starting transfers between devices, rotate(): lax.ppermute(value, 'dates', [(i, (i + k) % blocks) for i in range(blocks)])  8.17 us
    ppermute x4, waiting for transfers between devices, body(): lax.ppermute(sums, 'rows', [(i, i ^ steps) for i in range(slabs)])  6.24 us
    ppermute x1, starting transfers between devices, body(): lax.ppermute(downward[-1:], 'rows', [(i, i + 1) for i in range(slabs - 1)])  2.36 us
  transfers between devices with their start and end apart: 19, of which 6 were waited for; matrix products, arithmetic and copies ran while one was open for 5% of the time, Pallas kernels for 12%

profile of v1, /device:TPU:0, one launch (start us, length us, event | category | flops | bytes accessed | tf_op | source)
XLA Modules:
  0.0 94.2 jit_solution(10458641905118748466)
XLA Ops:
  0.7 1.0 %convert_element_type.9 = f32[2,8,4096]{2,1,0:T(8,128)S(1)} convert(s32[2,8,4096]{2,1,0:T(8,128)} %param.9) | non-fusion elementwise | flops 65536 | bytes 524288 | tf_op jit(solution)/shard_map/convert_element_type | solution.py:333
  1.7 2.4 %collective-permute-start = (f32[1,4096]{1,0:T(1,128)S(1)}, f32[1,4096]{1,0:T(1,128)S(1)}, u32[]{:S(2)}, u32[]{:S(2)}) collective-permute-start(f32[1,4096]{1,0:T(1,128)S(1)} %slice.54), channel_id=1, source_target_pairs={{0,2},{2,4},{4,6},{6,8},{8,10},{10,12},{12,14},{14,16},{16,18},{18... | collective-permute-start | bytes 49160 | tf_op jit(solution)/shard_map/ppermute | solution.py:339
  4.1 2.3 %dynamic-slice_multiply_fusion = (f32[8,8,2048]{2,1,0:T(8,128)S(1)}, f32[8,8,2048]{2,1,0:T(8,128)}) fusion(f32[8,8,4096]{2,1,0:T(8,128)} %observed.3, s32[]{:T(128)S(6)} %select_n.61, f32[8,8,4096]{2,1,0:T(8,128)} %precision.5, s32[8,8,4096]{2,1,0:T(8,128)} %mask.5), kind=kLoop, calls=%fused_computation.1 | loop fusion | flops 393216 | bytes 2621444 | tf_op jit(solution)/shard_map/mul | solution.py:330
  6.4 2.3 %collective-permute-start.1 = (f32[8,8,2048]{2,1,0:T(8,128)S(1)}, f32[8,8,2048]{2,1,0:T(8,128)S(1)}, u32[]{:S(2)}, u32[]{:S(2)}) collective-permute-start(f32[8,8,2048]{2,1,0:T(8,128)S(1)} %get-tuple-element.32), channel_id=1, source_target_pairs={{0,1},{1,0},{2,3},{3,2},{4,5},{5,4},{6,7},{7,6},{8,9},{9,8},{10,11... | collective-permute-start | bytes 1572872 | tf_op jit(solution)/shard_map/ppermute | solution.py:307
  9.1 0.7 pad_maximum_fusion.3.tau
  9.8 10.4 %collective-permute-done.1 = f32[8,8,2048]{2,1,0:T(8,128)S(1)} collective-permute-done((f32[8,8,2048]{2,1,0:T(8,128)S(1)}, f32[8,8,2048]{2,1,0:T(8,128)S(1)}, u32[]{:S(2)}, u32[]{:S(2)}) %collective-permute-start.1) | collective-permute-done | bytes 524320 | tf_op jit(solution)/shard_map/ppermute | solution.py:307
  20.3 3.4 %copy-done = bf16[16,16,8,2048]{3,2,1,0:T(8,128)(2,1)S(1)} copy-done((bf16[16,16,8,2048]{3,2,1,0:T(8,128)(2,1)S(1)}, bf16[16,16,8,2048]{3,2,1,0:T(8,128)(2,1)}, u32[]{:S(2)}) %copy-start) | copy-done | bytes 8388632
  23.7 1.2 %copy-done.2 = s32[8,8,4096]{2,1,0:T(8,128)S(1)} copy-done((s32[8,8,4096]{2,1,0:T(8,128)S(1)}, s32[8,8,4096]{2,1,0:T(8,128)}, u32[]{:S(2)}) %copy-start.2) | copy-done | bytes 1048600
  24.9 1.2 %copy-done.4 = f32[8,8,4096]{2,1,0:T(8,128)S(1)} copy-done((f32[8,8,4096]{2,1,0:T(8,128)S(1)}, f32[8,8,4096]{2,1,0:T(8,128)}, u32[]{:S(2)}) %copy-start.4) | copy-done | bytes 1048600
  26.1 1.2 %copy-done.6 = f32[8,8,4096]{2,1,0:T(8,128)S(1)} copy-done((f32[8,8,4096]{2,1,0:T(8,128)S(1)}, f32[8,8,4096]{2,1,0:T(8,128)}, u32[]{:S(2)}) %copy-start.6) | copy-done | bytes 1048600
  27.3 4.4 %shard_map.77 = (f32[16,8,2048]{2,1,0:T(8,128)S(1)}, f32[16,2048]{1,0:T(8,128)S(1)}, f32[16,2048]{1,0:T(8,128)S(1)}, f32[16,128]{1,0:T(8,128)S(1)}, f32[1,9,8,2048]{3,2,1,0:T(8,128)}, /*index=5*/f32[8,128]{1,0:T(8,128)S(1)}) custom-call(s32[2]{0:T(128)S(1)} %pad_add_fusion.place, s32[8,8,4096]{2,1,0:T(8,128)S(1)} %copy-done.2, f32[8,8,4096]{2,1,0:T(8,128)S(1)} %copy-done.4, ...), custom_call_target="tpu_custom_call" | custom-call | tf_op jit(solution)/shard_map/pallas_call | solution.py:18
  31.7 2.5 %collective-permute-start.4 = (f32[16,128]{1,0:T(8,128)S(1)}, f32[16,128]{1,0:T(8,128)S(1)}, u32[]{:S(2)}, u32[]{:S(2)}) collective-permute-start(f32[16,128]{1,0:T(8,128)S(1)} %get-tuple-element.20), channel_id=1, source_target_pairs={{0,1},{1,0},{2,3},{3,2},{4,5},{5,4},{6,7},{7,6},{8,9},{9,8},{10,11... | collective-permute-start | bytes 24584 | tf_op jit(solution)/shard_map/ppermute | solution.py:307
  34.3 1.5 %collective-permute-start.2 = (f32[16,2048]{1,0:T(8,128)S(1)}, f32[16,2048]{1,0:T(8,128)S(1)}, u32[]{:S(2)}, u32[]{:S(2)}) collective-permute-start(f32[16,2048]{1,0:T(8,128)S(1)} %get-tuple-element.18), channel_id=1, source_target_pairs={{0,2},{2,0},{4,6},{6,4},{8,10},{10,8},{12,14},{14,12},{16,18},{18,... | collective-permute-start | bytes 393224 | tf_op jit(solution)/shard_map/ppermute | solution.py:310
  35.8 0.7 collective-permute-start.3
  36.4 0.6 collective-permute-start.14
  37.1 0.8 copy-done.15
  37.9 1.1 %copy-done.16 = f32[8,8,2048]{2,1,0:T(8,128)S(1)} copy-done((f32[8,8,2048]{2,1,0:T(8,128)S(1)}, f32[8,8,2048]{2,1,0:T(8,128)}, u32[]{:S(2)}) %copy-start.16) | copy-done | bytes 524312
  39.0 5.5 %shard_map.78 = (f32[16,8,2048]{2,1,0:T(8,128)S(1)}, f32[16,2048]{1,0:T(8,128)S(1)}, f32[16,2048]{1,0:T(8,128)S(1)}, f32[16,128]{1,0:T(8,128)S(1)}, f32[1,9,8,20...) custom-call(s32[2]{0:T(128)S(1)} %pad_add_fusion.place, ...), custom_call_target="tpu_custom_call" | custom-call | tf_op jit(solution)/shard_map/pallas_call | solution.py:18
  44.5 1.0 %copy-done.10 = f32[16,8,2048]{2,1,0:T(8,128)} copy-done((f32[16,8,2048]{2,1,0:T(8,128)}, f32[16,8,2048]{2,1,0:T(8,128)S(1)}, u32[]{:S(2)}) %copy-start.10) | copy-done | bytes 1048600
  45.4 1.0 %copy-done.13 = f32[16,8,2048]{2,1,0:T(8,128)} copy-done((f32[16,8,2048]{2,1,0:T(8,128)}, f32[16,8,2048]{2,1,0:T(8,128)S(1)}, u32[]{:S(2)}) %copy-start.13) | copy-done | bytes 1048600
  46.4 0.8 copy-done.19
  47.2 0.6 copy-done.20
  47.9 0.7 copy-done.21
  48.5 1.5 %collective-permute-start.16 = (f32[16,2048]{1,0:T(8,128)}, f32[16,2048]{1,0:T(8,128)}, u32[]{:S(2)}, u32[]{:S(2)}) collective-permute-start(f32[16,2048]{1,0:T(8,128)} %bitcast.15), channel_id=1, source_target_pairs={{0,1},{1,0},{2,3},{3,2},{4,5},{5,4},{6,7},{7,6},{8,9},{9,8},{10,11... | collective-permute-start | bytes 393224 | tf_op jit(solution)/shard_map/ppermute | solution.py:307
  50.6 3.9 %collective-permute-start.6 = (f32[16,2048]{1,0:T(8,128)}, f32[16,2048]{1,0:T(8,128)S(1)}, u32[]{:S(2)}, u32[]{:S(2)}) collective-permute-start(f32[16,2048]{1,0:T(8,128)} %copy-done.21), channel_id=1, source_target_pairs={{0,2},{2,0},{4,6},{6,4},{8,10},{10,8},{12,14},{14,12},{16,18},{18,... | collective-permute-start | bytes 393224 | tf_op jit(solution)/shard_map/ppermute | solution.py:310
  54.5 0.7 collective-permute-start.7
  55.1 0.6 collective-permute-start.15
  55.8 0.9 fusion.2
  57.1 4.2 %collective-permute-start.17 = (f32[1,16,2048]{2,1,0:T(8,128)S(1)}, f32[1,16,2048]{2,1,0:T(8,128)S(1)}, u32[]{:S(2)}, u32[]{:S(2)}) collective-permute-start(f32[1,16,2048]{2,1,0:T(8,128)S(1)} %pad_maximum_fusion.1), channel_id=1, source_target_pairs={{0,2},{2,0},{4,6},{6,4},{8,10},{10,8},{12,14},{14,12},{16,18},{18,... | collective-permute-start | bytes 393224 | tf_op jit(solution)/shard_map/ppermute | solution.py:310
  61.4 0.7 collective-permute-start.18
  62.1 1.2 %copy-done.11 = f32[16,8,2048]{2,1,0:T(8,128)S(1)} copy-done((f32[16,8,2048]{2,1,0:T(8,128)S(1)}, f32[16,8,2048]{2,1,0:T(8,128)}, u32[]{:S(2)}) %copy-start.11) | copy-done | bytes 1048600
  63.3 1.2 %copy-done.14 = f32[16,8,2048]{2,1,0:T(8,128)S(1)} copy-done((f32[16,8,2048]{2,1,0:T(8,128)S(1)}, f32[16,8,2048]{2,1,0:T(8,128)}, u32[]{:S(2)}) %copy-start.14) | copy-done | bytes 1048600
  64.5 1.8 %shard_map.79 = f32[8,128]{1,0:T(8,128)S(1)} custom-call(s32[2]{0:T(128)S(1)} %pad_add_fusion.place, f32[17]{0:T(128)S(1)} %pad_maximum_fusion.3.tau, f32[5,8,4096]{2,1,0:T(8,128)S(1)} %bitcast_dynamic-update-slice_fusion.weights.weights_all, f32[16,8,2048]{2,1,0:T(8,128)S(1)} %copy-done.11, f32[16,2048]{1,0:T(8,128)S(1)} %collective-permute-done.6.halo_1.own_m1, ...), custom_call_target="tpu_custom_call" | custom-call | tf_op jit(solution)/shard_map/pallas_call | solution.py:18
  66.4 3.0 %collective-permute-start.9 = (f32[8,128]{1,0:T(8,128)S(1)}, f32[8,128]{1,0:T(8,128)S(1)}, u32[]{:S(2)}, u32[]{:S(2)}) collective-permute-start(f32[8,128]{1,0:T(8,128)S(1)} %shard_map.79), channel_id=1, source_target_pairs={{0,2},{2,0},{4,6},{6,4},{8,10},{10,8},{12,14},{14,12},{16,18},{18,... | collective-permute-start | bytes 12296 | tf_op jit(solution)/shard_map/ppermute | solution.py:381
  69.4 0.8 collective-permute-done.9
  70.2 2.2 %collective-permute-start.10 = (f32[8,128]{1,0:T(8,128)S(1)}, f32[8,128]{1,0:T(8,128)S(1)}, u32[]{:S(2)}, u32[]{:S(2)}) collective-permute-start(f32[8,128]{1,0:T(8,128)S(1)} %add.78), channel_id=1, source_target_pairs={{0,4},{2,6},{4,0},{6,2},{8,12},{10,14},{12,8},{14,10},{16,20},{18,... | collective-permute-start | bytes 12296 | tf_op jit(solution)/shard_map/ppermute | solution.py:381
  72.4 1.6 %collective-permute-done.10 = f32[8,128]{1,0:T(8,128)S(1)} collective-permute-done((f32[8,128]{1,0:T(8,128)S(1)}, f32[8,128]{1,0:T(8,128)S(1)}, u32[]{:S(2)}, u32[]{:S(2)}) %collective-permute-start.10) | collective-permute-done | bytes 4128 | tf_op jit(solution)/shard_map/ppermute | solution.py:381
  74.0 1.6 %collective-permute-start.11 = (f32[8,128]{1,0:T(8,128)S(1)}, f32[8,128]{1,0:T(8,128)S(1)}, u32[]{:S(2)}, u32[]{:S(2)}) collective-permute-start(f32[8,128]{1,0:T(8,128)S(1)} %add.79), channel_id=1, source_target_pairs={{0,8},{2,10},{4,12},{6,14},{8,0},{10,2},{12,4},{14,6},{16,24},{18,... | collective-permute-start | bytes 12296 | tf_op jit(solution)/shard_map/ppermute | solution.py:381
  75.6 2.0 %collective-permute-done.11 = f32[8,128]{1,0:T(8,128)S(1)} collective-permute-done((f32[8,128]{1,0:T(8,128)S(1)}, f32[8,128]{1,0:T(8,128)S(1)}, u32[]{:S(2)}, u32[]{:S(2)}) %collective-permute-start.11) | collective-permute-done | bytes 4128 | tf_op jit(solution)/shard_map/ppermute | solution.py:381
  77.6 2.6 %collective-permute-start.12 = (f32[8,128]{1,0:T(8,128)S(1)}, f32[8,128]{1,0:T(8,128)S(1)}, u32[]{:S(2)}, u32[]{:S(2)}) collective-permute-start(f32[8,128]{1,0:T(8,128)S(1)} %add.80), channel_id=1, source_target_pairs={{0,16},{2,18},{4,20},{6,22},{8,24},{10,26},{12,28},{14,30},{16,0},... | collective-permute-start | bytes 12296 | tf_op jit(solution)/shard_map/ppermute | solution.py:381
  80.3 1.9 %collective-permute-done.12 = f32[8,128]{1,0:T(8,128)S(1)} collective-permute-done((f32[8,128]{1,0:T(8,128)S(1)}, f32[8,128]{1,0:T(8,128)S(1)}, u32[]{:S(2)}, u32[]{:S(2)}) %collective-permute-start.12) | collective-permute-done | bytes 4128 | tf_op jit(solution)/shard_map/ppermute | solution.py:381
  82.1 1.5 %collective-permute-start.13 = (f32[8,128]{1,0:T(8,128)S(1)}, f32[8,128]{1,0:T(8,128)S(1)}, u32[]{:S(2)}, u32[]{:S(2)}) collective-permute-start(f32[8,128]{1,0:T(8,128)S(1)} %add.81), channel_id=1, source_target_pairs={{0,1},{1,0},{2,3},{3,2},{4,5},{5,4},{6,7},{7,6},{8,9},{9,8},{10,11... | collective-permute-start | bytes 12296 | tf_op jit(solution)/shard_map/ppermute | solution.py:385
  83.6 2.1 %collective-permute-done.13 = f32[8,128]{1,0:T(8,128)S(1)} collective-permute-done((f32[8,128]{1,0:T(8,128)S(1)}, f32[8,128]{1,0:T(8,128)S(1)}, u32[]{:S(2)}, u32[]{:S(2)}) %collective-permute-start.13) | collective-permute-done | bytes 4128 | tf_op jit(solution)/shard_map/ppermute | solution.py:385
  85.8 1.2 %copy-done.7 = f32[8,8,4096]{2,1,0:T(8,128)S(1)} copy-done((f32[8,8,4096]{2,1,0:T(8,128)S(1)}, f32[8,8,4096]{2,1,0:T(8,128)}, u32[]{:S(2)}) %copy-start.7) | copy-done | bytes 1048600
  87.0 1.2 %copy-done.9 = f32[16,8,2048]{2,1,0:T(8,128)S(1)} copy-done((f32[16,8,2048]{2,1,0:T(8,128)S(1)}, f32[16,8,2048]{2,1,0:T(8,128)}, u32[]{:S(2)}) %copy-start.9) | copy-done | bytes 1048600
  88.2 1.2 %copy-done.12 = f32[16,8,2048]{2,1,0:T(8,128)S(1)} copy-done((f32[16,8,2048]{2,1,0:T(8,128)S(1)}, f32[16,8,2048]{2,1,0:T(8,128)}, u32[]{:S(2)}) %copy-start.12) | copy-done | bytes 1048600
  89.4 0.9 copy-done.18
  90.3 3.8 %shard_map.80 = (f32[8,8,4096]{2,1,0:T(8,128)}, f32[8,8,4096]{2,1,0:T(8,128)}) custom-call(s32[2]{0:T(128)S(1)} %pad_add_fusion.place, f32[17]{0:T(128)S(1)} %pad_maximum_fusion.3.tau, f32[5,8,4096]{2,1,0:T(8,128)S(1)} %bitcast_dynamic-update-slice_fusion.weights.weights_all, f32[8,128]{1,0:T(8,128)S(1)} %add.82.sums, f32[16,8,2048]{2,1,0:T(8,128)S(1)} %copy-done.9, ...), custom_call_target="tpu_custom_call" | custom-call | tf_op jit(solution)/shard_map/pallas_call | solution.py:18
  (64 shorter events, 1.6 us)
Async XLA Ops:
  1.7 8.1 %collective-permute-start = (f32[1,4096]{1,0:T(1,128)S(1)}, f32[1,4096]{1,0:T(1,128)S(1)}, u32[]{:S(2)}, u32[]{:S(2)}) collective-permute-start(f32[1,4096]{1,0:T(1,128)S(1)} %slice.54), channel_id=1, source_target_pairs={{0,2},{2,4},{4,6},{6,8},{8,10},{10,12},{12,14},{14,16},{16,18},{18... | collective-permute-start | bytes 49160 | tf_op jit(solution)/shard_map/ppermute | solution.py:339
  6.4 13.9 %collective-permute-start.1 = (f32[8,8,2048]{2,1,0:T(8,128)S(1)}, f32[8,8,2048]{2,1,0:T(8,128)S(1)}, u32[]{:S(2)}, u32[]{:S(2)}) collective-permute-start(f32[8,8,2048]{2,1,0:T(8,128)S(1)} %get-tuple-element.32), channel_id=1, source_target_pairs={{0,1},{1,0},{2,3},{3,2},{4,5},{5,4},{6,7},{7,6},{8,9},{9,8},{10,11... | collective-permute-start | bytes 1572872 | tf_op jit(solution)/shard_map/ppermute | solution.py:307
  8.7 28.3 %collective-permute-start.5 = (f32[8,8,2048]{2,1,0:T(8,128)}, f32[8,8,2048]{2,1,0:T(8,128)S(1)}, u32[]{:S(2)}, u32[]{:S(2)}) collective-permute-start(f32[8,8,2048]{2,1,0:T(8,128)} %get-tuple-element.33), channel_id=1, source_target_pairs={{0,1},{1,0},{2,3},{3,2},{4,5},{5,4},{6,7},{7,6},{8,9},{9,8},{10,11... | collective-permute-start | bytes 1572872 | tf_op jit(solution)/shard_map/ppermute | solution.py:307
  20.3 3.4 %copy-start = (bf16[16,16,8,2048]{3,2,1,0:T(8,128)(2,1)S(1)}, bf16[16,16,8,2048]{3,2,1,0:T(8,128)(2,1)}, u32[]{:S(2)}) copy-start(bf16[16,16,8,2048]{3,2,1,0:T(8,128)(2,1)} %inverse.3) | copy-start | bytes 25165828
  23.7 1.2 %copy-start.2 = (s32[8,8,4096]{2,1,0:T(8,128)S(1)}, s32[8,8,4096]{2,1,0:T(8,128)}, u32[]{:S(2)}) copy-start(s32[8,8,4096]{2,1,0:T(8,128)} %mask.5) | copy-start | bytes 3145732
  24.9 1.2 %copy-start.4 = (f32[8,8,4096]{2,1,0:T(8,128)S(1)}, f32[8,8,4096]{2,1,0:T(8,128)}, u32[]{:S(2)}) copy-start(f32[8,8,4096]{2,1,0:T(8,128)} %precision.5) | copy-start | bytes 3145732
  26.1 1.2 %copy-start.6 = (f32[8,8,4096]{2,1,0:T(8,128)S(1)}, f32[8,8,4096]{2,1,0:T(8,128)}, u32[]{:S(2)}) copy-start(f32[8,8,4096]{2,1,0:T(8,128)} %observed.3) | copy-start | bytes 3145732
  27.3 10.6 %copy-start.1 = (bf16[16,16,8,2048]{3,2,1,0:T(8,128)(2,1)S(1)}, bf16[16,16,8,2048]{3,2,1,0:T(8,128)(2,1)}, u32[]{:S(2)}) copy-start(bf16[16,16,8,2048]{3,2,1,0:T(8,128)(2,1)} %inverse.3) | copy-start | bytes 25165828
  31.7 12.7 %copy-start.8 = (f32[16,8,2048]{2,1,0:T(8,128)}, f32[16,8,2048]{2,1,0:T(8,128)S(1)}, u32[]{:S(2)}) copy-start(f32[16,8,2048]{2,1,0:T(8,128)S(1)} %get-tuple-element.17.precond) | copy-start | bytes 3145732
  31.7 5.3 %collective-permute-start.4 = (f32[16,128]{1,0:T(8,128)S(1)}, f32[16,128]{1,0:T(8,128)S(1)}, u32[]{:S(2)}, u32[]{:S(2)}) collective-permute-start(f32[16,128]{1,0:T(8,128)S(1)} %get-tuple-element.20), channel_id=1, source_target_pairs={{0,1},{1,0},{2,3},{3,2},{4,5},{5,4},{6,7},{7,6},{8,9},{9,8},{10,11... | collective-permute-start | bytes 24584 | tf_op jit(solution)/shard_map/ppermute | solution.py:307
  34.3 3.6 %collective-permute-start.2 = (f32[16,2048]{1,0:T(8,128)S(1)}, f32[16,2048]{1,0:T(8,128)S(1)}, u32[]{:S(2)}, u32[]{:S(2)}) collective-permute-start(f32[16,2048]{1,0:T(8,128)S(1)} %get-tuple-element.18), channel_id=1, source_target_pairs={{0,2},{2,0},{4,6},{6,4},{8,10},{10,8},{12,14},{14,12},{16,18},{18,... | collective-permute-start | bytes 393224 | tf_op jit(solution)/shard_map/ppermute | solution.py:310
  35.8 2.1 %collective-permute-start.3 = (f32[16,2048]{1,0:T(8,128)S(1)}, f32[16,2048]{1,0:T(8,128)S(1)}, u32[]{:S(2)}, u32[]{:S(2)}) collective-permute-start(f32[16,2048]{1,0:T(8,128)S(1)} %get-tuple-element.19), channel_id=1, source_target_pairs={{2,4},{6,8},{10,12},{14,16},{18,20},{22,24},{26,28},{4,2},{8,6},{1... | collective-permute-start | bytes 393224 | tf_op jit(solution)/shard_map/ppermute | solution.py:310
  36.4 20.2 %collective-permute-start.14 = (f32[9,8,2048]{2,1,0:T(8,128)}, f32[9,8,2048]{2,1,0:T(8,128)S(1)}, u32[]{:S(2)}, u32[]{:S(2)}) collective-permute-start(f32[9,8,2048]{2,1,0:T(8,128)} %bitcast.9), channel_id=1, source_target_pairs={{0,1},{1,0},{2,3},{3,2},{4,5},{5,4},{6,7},{7,6},{8,9},{9,8},{10,11... | collective-permute-start | bytes 1769480 | tf_op jit(solution)/shard_map/ppermute | solution.py:307
  37.1 0.8 copy-start.15
  37.9 10.7 %copy-start.17 = (f32[16,2048]{1,0:T(8,128)}, f32[16,2048]{1,0:T(8,128)S(1)}, u32[]{:S(2)}) copy-start(f32[16,2048]{1,0:T(8,128)S(1)} %collective-permute-done.3.halo_2.own_p2) | copy-start | bytes 393220
  37.9 1.1 %copy-start.16 = (f32[8,8,2048]{2,1,0:T(8,128)S(1)}, f32[8,8,2048]{2,1,0:T(8,128)}, u32[]{:S(2)}) copy-start(f32[8,8,2048]{2,1,0:T(8,128)} %copy-done.15) | copy-start | bytes 1572868
  39.0 46.8 %copy-start.3 = (s32[8,8,4096]{2,1,0:T(8,128)S(1)}, s32[8,8,4096]{2,1,0:T(8,128)}, u32[]{:S(2)}) copy-start(s32[8,8,4096]{2,1,0:T(8,128)} %mask.5) | copy-start | bytes 3145732
  39.0 46.8 %copy-start.5 = (f32[8,8,4096]{2,1,0:T(8,128)S(1)}, f32[8,8,4096]{2,1,0:T(8,128)}, u32[]{:S(2)}) copy-start(f32[8,8,4096]{2,1,0:T(8,128)} %precision.5) | copy-start | bytes 3145732
  44.5 1.0 %copy-start.10 = (f32[16,8,2048]{2,1,0:T(8,128)}, f32[16,8,2048]{2,1,0:T(8,128)S(1)}, u32[]{:S(2)}) copy-start(f32[16,8,2048]{2,1,0:T(8,128)S(1)} %get-tuple-element.21.mapped) | copy-start | bytes 3145732
  45.4 1.0 %copy-start.13 = (f32[16,8,2048]{2,1,0:T(8,128)}, f32[16,8,2048]{2,1,0:T(8,128)S(1)}, u32[]{:S(2)}) copy-start(f32[16,8,2048]{2,1,0:T(8,128)S(1)} %get-tuple-element.25.data_weight) | copy-start | bytes 3145732
  46.4 0.8 copy-start.19
  47.2 0.6 copy-start.20
  47.9 0.7 copy-start.21
  48.5 6.6 %collective-permute-start.16 = (f32[16,2048]{1,0:T(8,128)}, f32[16,2048]{1,0:T(8,128)}, u32[]{:S(2)}, u32[]{:S(2)}) collective-permute-start(f32[16,2048]{1,0:T(8,128)} %bitcast.15), channel_id=1, source_target_pairs={{0,1},{1,0},{2,3},{3,2},{4,5},{5,4},{6,7},{7,6},{8,9},{9,8},{10,11... | collective-permute-start | bytes 393224 | tf_op jit(solution)/shard_map/ppermute | solution.py:307
  50.0 11.4 %collective-permute-start.8 = (f32[16,128]{1,0:T(8,128)S(1)}, f32[16,128]{1,0:T(8,128)S(1)}, u32[]{:S(2)}, u32[]{:S(2)}) collective-permute-start(f32[16,128]{1,0:T(8,128)S(1)} %get-tuple-element.24), channel_id=1, source_target_pairs={{0,1},{1,0},{2,3},{3,2},{4,5},{5,4},{6,7},{7,6},{8,9},{9,8},{10,11... | collective-permute-start | bytes 24584 | tf_op jit(solution)/shard_map/ppermute | solution.py:307
  50.6 11.5 %collective-permute-start.6 = (f32[16,2048]{1,0:T(8,128)}, f32[16,2048]{1,0:T(8,128)S(1)}, u32[]{:S(2)}, u32[]{:S(2)}) collective-permute-start(f32[16,2048]{1,0:T(8,128)} %copy-done.21), channel_id=1, source_target_pairs={{0,2},{2,0},{4,6},{6,4},{8,10},{10,8},{12,14},{14,12},{16,18},{18,... | collective-permute-start | bytes 393224 | tf_op jit(solution)/shard_map/ppermute | solution.py:310
  54.5 7.6 %collective-permute-start.7 = (f32[16,2048]{1,0:T(8,128)}, f32[16,2048]{1,0:T(8,128)S(1)}, u32[]{:S(2)}, u32[]{:S(2)}) collective-permute-start(f32[16,2048]{1,0:T(8,128)} %copy-done.20), channel_id=1, source_target_pairs={{2,4},{6,8},{10,12},{14,16},{18,20},{22,24},{26,28},{4,2},{8,6},{1... | collective-permute-start | bytes 393224 | tf_op jit(solution)/shard_map/ppermute | solution.py:310
  55.1 30.6 %collective-permute-start.15 = (f32[9,8,2048]{2,1,0:T(8,128)}, f32[9,8,2048]{2,1,0:T(8,128)S(1)}, u32[]{:S(2)}, u32[]{:S(2)}) collective-permute-start(f32[9,8,2048]{2,1,0:T(8,128)} %bitcast.32), channel_id=1, source_target_pairs={{0,1},{1,0},{2,3},{3,2},{4,5},{5,4},{6,7},{7,6},{8,9},{9,8},{10,11... | collective-permute-start | bytes 1769480 | tf_op jit(solution)/shard_map/ppermute | solution.py:307
  57.1 28.6 %collective-permute-start.17 = (f32[1,16,2048]{2,1,0:T(8,128)S(1)}, f32[1,16,2048]{2,1,0:T(8,128)S(1)}, u32[]{:S(2)}, u32[]{:S(2)}) collective-permute-start(f32[1,16,2048]{2,1,0:T(8,128)S(1)} %pad_maximum_fusion.1), channel_id=1, source_target_pairs={{0,2},{2,0},{4,6},{6,4},{8,10},{10,8},{12,14},{14,12},{16,18},{18,... | collective-permute-start | bytes 393224 | tf_op jit(solution)/shard_map/ppermute | solution.py:310
  61.4 24.4 %collective-permute-start.18 = (f32[1,16,2048]{2,1,0:T(8,128)S(1)}, f32[1,16,2048]{2,1,0:T(8,128)S(1)}, u32[]{:S(2)}, u32[]{:S(2)}) collective-permute-start(f32[1,16,2048]{2,1,0:T(8,128)S(1)} %pad_maximum_fusion.2), channel_id=1, source_target_pairs={{2,4},{6,8},{10,12},{14,16},{18,20},{22,24},{26,28},{4,2},{8,6},{1... | collective-permute-start | bytes 393224 | tf_op jit(solution)/shard_map/ppermute | solution.py:310
  62.1 1.2 %copy-start.11 = (f32[16,8,2048]{2,1,0:T(8,128)S(1)}, f32[16,8,2048]{2,1,0:T(8,128)}, u32[]{:S(2)}) copy-start(f32[16,8,2048]{2,1,0:T(8,128)} %copy-done.10) | copy-start | bytes 3145732
  63.3 1.2 %copy-start.14 = (f32[16,8,2048]{2,1,0:T(8,128)S(1)}, f32[16,8,2048]{2,1,0:T(8,128)}, u32[]{:S(2)}) copy-start(f32[16,8,2048]{2,1,0:T(8,128)} %copy-done.13) | copy-start | bytes 3145732
  66.4 3.9 %collective-permute-start.9 = (f32[8,128]{1,0:T(8,128)S(1)}, f32[8,128]{1,0:T(8,128)S(1)}, u32[]{:S(2)}, u32[]{:S(2)}) collective-permute-start(f32[8,128]{1,0:T(8,128)S(1)} %shard_map.79), channel_id=1, source_target_pairs={{0,2},{2,0},{4,6},{6,4},{8,10},{10,8},{12,14},{14,12},{16,18},{18,... | collective-permute-start | bytes 12296 | tf_op jit(solution)/shard_map/ppermute | solution.py:381
  70.2 3.8 %collective-permute-start.10 = (f32[8,128]{1,0:T(8,128)S(1)}, f32[8,128]{1,0:T(8,128)S(1)}, u32[]{:S(2)}, u32[]{:S(2)}) collective-permute-start(f32[8,128]{1,0:T(8,128)S(1)} %add.78), channel_id=1, source_target_pairs={{0,4},{2,6},{4,0},{6,2},{8,12},{10,14},{12,8},{14,10},{16,20},{18,... | collective-permute-start | bytes 12296 | tf_op jit(solution)/shard_map/ppermute | solution.py:381
  74.0 3.6 %collective-permute-start.11 = (f32[8,128]{1,0:T(8,128)S(1)}, f32[8,128]{1,0:T(8,128)S(1)}, u32[]{:S(2)}, u32[]{:S(2)}) collective-permute-start(f32[8,128]{1,0:T(8,128)S(1)} %add.79), channel_id=1, source_target_pairs={{0,8},{2,10},{4,12},{6,14},{8,0},{10,2},{12,4},{14,6},{16,24},{18,... | collective-permute-start | bytes 12296 | tf_op jit(solution)/shard_map/ppermute | solution.py:381
  77.6 4.5 %collective-permute-start.12 = (f32[8,128]{1,0:T(8,128)S(1)}, f32[8,128]{1,0:T(8,128)S(1)}, u32[]{:S(2)}, u32[]{:S(2)}) collective-permute-start(f32[8,128]{1,0:T(8,128)S(1)} %add.80), channel_id=1, source_target_pairs={{0,16},{2,18},{4,20},{6,22},{8,24},{10,26},{12,28},{14,30},{16,0},... | collective-permute-start | bytes 12296 | tf_op jit(solution)/shard_map/ppermute | solution.py:381
  82.1 3.6 %collective-permute-start.13 = (f32[8,128]{1,0:T(8,128)S(1)}, f32[8,128]{1,0:T(8,128)S(1)}, u32[]{:S(2)}, u32[]{:S(2)}) collective-permute-start(f32[8,128]{1,0:T(8,128)S(1)} %add.81), channel_id=1, source_target_pairs={{0,1},{1,0},{2,3},{3,2},{4,5},{5,4},{6,7},{7,6},{8,9},{9,8},{10,11... | collective-permute-start | bytes 12296 | tf_op jit(solution)/shard_map/ppermute | solution.py:385
  85.8 1.2 %copy-start.7 = (f32[8,8,4096]{2,1,0:T(8,128)S(1)}, f32[8,8,4096]{2,1,0:T(8,128)}, u32[]{:S(2)}) copy-start(f32[8,8,4096]{2,1,0:T(8,128)} %observed.3) | copy-start | bytes 3145732
  87.0 1.2 %copy-start.9 = (f32[16,8,2048]{2,1,0:T(8,128)S(1)}, f32[16,8,2048]{2,1,0:T(8,128)}, u32[]{:S(2)}) copy-start(f32[16,8,2048]{2,1,0:T(8,128)} %copy-done.8) | copy-start | bytes 3145732
  88.2 1.2 %copy-start.12 = (f32[16,8,2048]{2,1,0:T(8,128)S(1)}, f32[16,8,2048]{2,1,0:T(8,128)}, u32[]{:S(2)}) copy-start(f32[16,8,2048]{2,1,0:T(8,128)} %copy-done.10) | copy-start | bytes 3145732
  89.4 0.9 copy-start.18

commit v2 on v1

v2 whole, which is shorter than its diff:
```python
import functools

import jax
import jax.numpy as jnp
from jax import lax
from jax.experimental import pallas as pl
from jax.experimental.pallas import tpu as pltpu
from jax.sharding import PartitionSpec as P

MASS = 0.1
LANES = 128
VMEM = pl.BlockSpec(memory_space=pltpu.VMEM)
SMEM = pl.BlockSpec(memory_space=pltpu.SMEM)
HBM = pl.BlockSpec(memory_space=pltpu.HBM)
PARAMS = pltpu.CompilerParams(vmem_limit_bytes=8 * 1024 * 1024)

COST = pl.CostEstimate(flops=1, bytes_accessed=1, transcendentals=0)


def call(kernel, out_shapes, scratch, scalars, arrays, space=VMEM):
    def typed(entry):
        return entry if isinstance(entry[-1], (jnp.dtype, type)) else (entry, jnp.float32)

    if space is HBM:
        arrays = [pltpu.with_memory_space_constraint(array, pltpu.HBM) for array in arrays]
    return pl.pallas_call(
        kernel,
        out_shape=[jax.ShapeDtypeStruct(*typed(entry)) for entry in out_shapes],
        in_specs=[SMEM] * len(scalars) + [space] * len(arrays),
        out_specs=[VMEM] * len(out_shapes),
        scratch_shapes=[pltpu.VMEM(*typed(entry)) if isinstance(entry, tuple) else entry for entry in scratch],
        compiler_params=PARAMS,
        cost_estimate=COST,
    )(*scalars, *arrays)


def tile(index):
    return pl.ds(pl.multiple_of(index * LANES, LANES), LANES)


def columns(block, width):
    return pl.ds(pl.multiple_of(block * width, LANES), width)


def row_ids(width):
    return lax.broadcasted_iota(jnp.int32, (8, width), 0)


def lane_ids(width):
    return lax.broadcasted_iota(jnp.int32, (8, width), 1)


def window_start(block, dates_here, length, dates):
    return jnp.clip(block * dates_here - 1, 0, dates - length)


def edge_rows(value, parity):
    top, bottom = value[0:1], value[7:8]
    return jnp.where(parity == 0, bottom, top), jnp.where(parity == 0, top, bottom)


def halo_rows(first, second, parity):
    above = jnp.where(parity == 0, second, first)
    below = jnp.where(parity == 0, first, second)
    return above, below


def stencil(value, above, below, left, right, later, earlier, weights, diagonal, tau_up, tau_down):
    across, across_prev, downward, downward_prev = weights
    width = value.shape[1]
    rows, lanes = row_ids(width), lane_ids(width)
    next_column = jnp.where(lanes == width - 1, right, pltpu.roll(value, width - 1, 1))
    prev_column = jnp.where(lanes == 0, left, pltpu.roll(value, 1, 1))
    next_row = jnp.where(rows == 7, below, pltpu.roll(value, 7, 0))
    prev_row = jnp.where(rows == 0, above, pltpu.roll(value, 1, 0))
    away = across * next_column + across_prev * prev_column
    away = away + downward * next_row + downward_prev * prev_row
    return diagonal * value - (away + tau_up * later + tau_down * earlier)


def apply_inverse(inverse, source, store, first_total):
    dates = inverse.shape[0]

    def step(index, total):
        lanes = tile(index)
        values = [source[s, :, lanes] for s in range(dates)]
        for t in range(dates):
            mapped = inverse[t, 0, :, lanes].astype(jnp.float32) * values[0]
            for s in range(1, dates):
                mapped = mapped + inverse[t, s, :, lanes].astype(jnp.float32) * values[s]
            total = total + values[t] * mapped
            store(t, lanes, mapped)
        return total

    return lax.fori_loop(0, source.shape[2] // LANES, step, first_total)


def pack_edges(field, parity, first, second, ends):
    dates, _, width = field.shape
    lanes = lane_ids(LANES)
    begin = jnp.zeros((8, LANES), jnp.float32)
    end = begin
    for t in range(dates):
        value = field[t]
        send_1, send_2 = edge_rows(value, parity)
        first[t : t + 1, :] = send_1
        second[t : t + 1, :] = send_2
        begin = jnp.where(lanes == t, value[:, 0:1], begin)
        end = jnp.where(lanes == t, value[:, width - 1 : width], end)
    ends[0:8, :] = begin
    ends[8:16, :] = end


def gather_dates(target, own, received, date_block, blocks, dates_here):
    for j in range(dates_here):
        target[date_block * dates_here + j] = own(j)
    for k in range(1, blocks):
        source = lax.rem(date_block + blocks - k, blocks)
        base = source * dates_here
        for part in received:
            for j in range(part.shape[1]):
                target[base + j] = part[k - 1, j]
            base = base + part.shape[1]


def send_windows(field, parts, date_block, blocks, dates_here):
    length = sum(part.shape[1] for part in parts)
    for k in range(1, blocks):
        target = lax.rem(date_block + k, blocks)
        start = window_start(target, dates_here, length, field.shape[0])
        base = start
        for part in parts:
            for j in range(part.shape[1]):
                part[k - 1, j] = field[base + j]
            base = base + part.shape[1]


def send_kernel(blocks, spans, place, mask, precision, observed, *refs):
    outputs = refs[: len(spans)]
    masks, precisions, observations, arrived = refs[len(spans) :]
    width = masks.shape[3]
    first = min(start for _, start, _ in spans)
    last = max(stop for _, _, stop in spans)
    for k in range(1, blocks):
        there = columns(lax.rem(place[0] + k, blocks), width)

        def copies(j):
            sources = [(mask, masks), (precision, precisions)]
            if any(kind == "rhs" and start <= j < stop for kind, start, stop in spans):
                sources.append((observed, observations))
            return [
                pltpu.make_async_copy(source.at[j, :, there], target.at[k - 1, j], arrived.at[k - 1, j, index])
                for index, (source, target) in enumerate(sources)
            ]

        for j in range(first, last):
            for copy in copies(j):
                copy.start()
        for j in range(first, last):
            for copy in copies(j):
                copy.wait()
            value = masks[k - 1, j].astype(jnp.float32) * precisions[k - 1, j]
            for (kind, start, stop), output in zip(spans, outputs):
                if start <= j < stop:
                    output[k - 1, j - start] = value * observations[k - 1, j] if kind == "rhs" else value


def stage_kernel(
    mask, precision, observed, edge_class, inverse, staged, weight, rhs, weights, last_row, masks, precisions, observations, classes, arrived, loaded
):
    dates_here = mask.shape[0]
    dates = inverse.shape[0]
    loads = [pltpu.make_async_copy(edge_class, classes, loaded.at[dates])]
    loads += [pltpu.make_async_copy(inverse.at[t], staged.at[t], loaded.at[t]) for t in range(dates)]
    copies = [
        [
            pltpu.make_async_copy(source.at[j], target.at[j], arrived.at[j, index])
            for index, (source, target) in enumerate(((mask, masks), (precision, precisions), (observed, observations)))
        ]
        for j in range(dates_here)
    ]
    for group in copies:
        for copy in group:
            copy.start()
    for load in loads:
        load.start()
    for j, group in enumerate(copies):
        for copy in group:
            copy.wait()
        value = masks[j].astype(jnp.float32) * precisions[j]
        weight[j] = value
        rhs[j] = value * observations[j]
    loads[0].wait()
    width = weights.shape[2]
    lanes = lane_ids(width)
    across = jnp.where(lanes == width - 1, 0.0, 0.25 * (classes[0].astype(jnp.float32) + 1.0))
    weights[0] = across
    weights[1] = jnp.where(lanes == 0, 0.0, pltpu.roll(across, 1, 1))
    downward = 0.25 * (classes[1].astype(jnp.float32) + 1.0)
    weights[2] = downward
    last_row[...] = jnp.broadcast_to(downward[7:8], downward.shape)
    for load in loads[1:]:
        load.wait()


def forward_halos(halo_1, halo_2, forwarded, date_block, blocks):
    dates_here = forwarded.shape[1] // 2
    for k in range(1, blocks):
        target = lax.rem(date_block + k, blocks)
        for j in range(dates_here):
            date = pl.ds(target * dates_here + j, 1)
            forwarded[k - 1, j : j + 1, :] = halo_1[date, :]
            forwarded[k - 1, dates_here + j : dates_here + j + 1, :] = halo_2[date, :]


def first_kernel(blocks, place, rhs_here, early, late, inverse, precond, first, second, ends, early_windows, late_windows, dot, rhs):
    date_block, parity = place[0], place[1]
    dates_here = rhs_here.shape[0]
    here = columns(date_block, rhs.shape[2])
    gather_dates(rhs, lambda j: rhs_here[j, :, here], (early, late), date_block, blocks, dates_here)

    def store(t, lanes, value):
        precond[t, :, lanes] = value

    dot[...] = apply_inverse(inverse, rhs, store, jnp.zeros((8, LANES), jnp.float32))
    pack_edges(precond, parity, first, second, ends)
    send_windows(precond, (early_windows, late_windows), date_block, blocks, dates_here)


def edge_weights(place, weights_all, above, lanes):
    across, across_prev, downward = [weights_all[k, :, lanes] for k in range(3)]
    width = across.shape[1]
    rows = row_ids(width)
    downward = jnp.where((rows == 7) & (place[3] == 1), 0.0, downward)
    downward_prev = jnp.where(rows == 0, above[0:1, lanes], pltpu.roll(downward, 1, 0))
    weights = (across, across_prev, downward, downward_prev)
    return weights, MASS + across + across_prev + downward + downward_prev


def pixel_image(place, tau, weights_all, row_above, field, halo_1, halo_2, ends_left, ends_right, data_weight, use):
    date_block, parity = place[0], place[1]
    dates, _, width = field.shape
    here = columns(date_block, width)
    weights, weight_sum = edge_weights(place, weights_all, row_above, here)
    for t in range(dates):
        above, below = halo_rows(halo_1[t : t + 1, :], halo_2[t : t + 1, :], parity)
        tau_up, tau_down = tau[t + 1], tau[t]
        value = field[t]
        diagonal = weight_sum + data_weight[t] + (tau_up + tau_down)
        image = stencil(
            value,
            above,
            below,
            0.0 if ends_left is None else ends_left[:, t : t + 1],
            0.0 if ends_right is None else ends_right[:, t : t + 1],
            field[min(t + 1, dates - 1)],
            field[max(t - 1, 0)],
            weights,
            diagonal,
            tau_up,
            tau_down,
        )
        use(t, value, image)


def fold(value):
    total = value[:, :LANES]
    for index in range(1, value.shape[1] // LANES):
        total = total + value[:, index * LANES : (index + 1) * LANES]
    return total


def second_kernel(
    blocks, place, tau, weights, row_above, precond, halo_1, halo_2, ends_left, ends_right, weight_here, received, inverse,
    mapped, first, second, ends, windows, forwarded, data_weight, dot_image, dot_mapped, image_all, total,
):
    date_block, parity = place[0], place[1]
    dates_here = weight_here.shape[0]
    here = columns(date_block, precond.shape[2])
    gather_dates(data_weight, lambda j: weight_here[j, :, here], (received,), date_block, blocks, dates_here)
    total[...] = jnp.zeros_like(total)

    def use(t, value, image):
        image_all[t] = image
        total[...] = total[...] + fold(value * image)

    pixel_image(place, tau, weights, row_above, precond, halo_1, halo_2, ends_left, ends_right, data_weight, use)
    dot_image[...] = total[...]

    def store(t, lanes, value):
        mapped[t, :, lanes] = value

    dot_mapped[...] = apply_inverse(inverse, image_all, store, jnp.zeros((8, LANES), jnp.float32))
    pack_edges(mapped, parity, first, second, ends)
    send_windows(mapped, (windows,), date_block, blocks, dates_here)
    forward_halos(halo_1, halo_2, forwarded, date_block, blocks)


def third_kernel(
    blocks, place, tau, weights, row_above, mapped, halo_1, halo_2, data_weight, dot_1, dot_2, dot_3, *refs,
):
    *ends, sums, forwarded, total = refs
    left, right = ends or (None, None)
    total[...] = jnp.zeros_like(total)

    def use(t, value, image):
        total[...] = total[...] + fold(value * image)

    pixel_image(place, tau, weights, row_above, mapped, halo_1, halo_2, left, right, data_weight, use)
    rows = row_ids(LANES)
    result = jnp.zeros((8, LANES), jnp.float32)
    for index, dot in enumerate((dot_1, dot_2, dot_3, total)):
        result = jnp.where(rows == index, jnp.sum(dot[...]), result)
    sums[...] = result
    forward_halos(halo_1, halo_2, forwarded, place[0], blocks)


def join_kernel(place, weights, ends, sums, ends_other, sums_other, joined):
    width = weights.shape[2] // 2
    boundary = weights[0, :, width - LANES : width][:, LANES - 1 : LANES]
    dates = jnp.where(place[0] == 0, ends[8:16, :] * ends_other[0:8, :], ends[0:8, :] * ends_other[8:16, :])
    crossing = -2.0 * jnp.sum(boundary * dates)
    joined[...] = sums[...] + sums_other[...] + jnp.where(row_ids(LANES) == 3, crossing, 0.0)


def last_kernel(
    blocks, place, tau, weights_all, row_above, sums, precond, mapped, precond_early, precond_late, mapped_other, own_p1, own_p2, own_m1, own_m2,
    precond_halos, mapped_halos, weight_here, rhs, solution, residual, field, above_all, below_all,
):
    date_block, parity = place[0], place[1]
    dates, _, width = precond.shape
    dates_here, _, all_columns = rhs.shape
    length = field.shape[0]
    one = sums[0:1, :]
    two = sums[1:2, :]
    three = sums[2:3, :]
    four = sums[3:4, :]
    alpha = one / two
    rz = alpha * alpha * three - one
    ahead = 1.0 + rz / one
    curve = ahead * ahead * two - 2.0 * ahead * alpha * three + alpha * alpha * four
    alpha_last = rz / curve
    scale_p = jnp.tile(alpha + alpha_last * ahead, (1, width // LANES))
    scale_m = jnp.tile(-alpha_last * alpha, (1, width // LANES))

    def mix(p, m):
        return scale_p * p + scale_m * m

    start = window_start(date_block, dates_here, length, dates)
    offset = date_block * dates_here - start
    here = columns(date_block, width)
    for j in range(length):
        field[j, :, here] = mix(precond[start + j], mapped[start + j])
    for j in range(dates_here):
        date = pl.ds(date_block * dates_here + j, 1)
        above, below = halo_rows(mix(own_p1[date, :], own_m1[date, :]), mix(own_p2[date, :], own_m2[date, :]), parity)
        above_all[j : j + 1, here] = above
        below_all[j : j + 1, here] = below
    for k in range(1, blocks):
        there = columns(lax.rem(date_block + blocks - k, blocks), width)
        for j in range(length):
            count = precond_early.shape[1]
            other = precond_early[k - 1, j] if j < count else precond_late[k - 1, j - count]
            field[j, :, there] = mix(other, mapped_other[k - 1, j])
        for j in range(dates_here):
            one, two = slice(j, j + 1), slice(dates_here + j, dates_here + j + 1)
            above, below = halo_rows(
                mix(precond_halos[k - 1, one, :], mapped_halos[k - 1, one, :]),
                mix(precond_halos[k - 1, two, :], mapped_halos[k - 1, two, :]),
                parity,
            )
            above_all[j : j + 1, there] = above
            below_all[j : j + 1, there] = below
    weights, weight_sum = edge_weights(place, weights_all, row_above, slice(None))
    for j in range(dates_here):
        tau_up, tau_down = tau[date_block * dates_here + j + 1], tau[date_block * dates_here + j]
        data_weight = weight_here[j]
        place_j = offset + j
        value = field[place_j]
        image = stencil(
            value,
            above_all[j : j + 1, :],
            below_all[j : j + 1, :],
            0.0,
            0.0,
            field[jnp.minimum(place_j + 1, length - 1)],
            field[jnp.maximum(place_j - 1, 0)],
            weights,
            weight_sum + data_weight + (tau_up + tau_down),
            tau_up,
            tau_down,
        )
        solution[j] = value
        residual[j] = rhs[j] - image


def body(blocks, slabs, obs_mask, precision, observed, edge_class, temporal_weight, inverse):
    dates_here, lines, all_columns = observed.shape
    dates = inverse.shape[0]
    width = all_columns // blocks
    length = min(dates_here + (1 if blocks == 2 else 2), dates)
    line_block = lax.axis_index("rows")
    date_block = lax.axis_index("dates")
    parity = lax.rem(line_block, 2)
    at_end = (line_block == slabs - 1).astype(jnp.int32)
    place = jnp.stack([date_block, parity, line_block, at_end]).astype(jnp.int32)

    pairs = [(i, i ^ 1) for i in range(slabs)]
    across_pairs = [(i, i + 1) for i in range(1, slabs - 1, 2)]
    across_pairs = across_pairs + [(b, a) for a, b in across_pairs]

    def rotate(value, k):
        return lax.ppermute(value, "dates", [(i, (i + k) % blocks) for i in range(blocks)])

    def swap_rows(first, second):
        return lax.ppermute(first, "rows", pairs), lax.ppermute(second, "rows", across_pairs)

    def swap_ends(ends):
        if blocks == 2:
            other = rotate(ends, 1)
            return other[8:16], other[0:8]
        forward = [(i, i + 1) for i in range(blocks - 1)]
        backward = [(b, a) for a, b in forward]
        return lax.ppermute(ends[8:16], "dates", forward), lax.ppermute(ends[0:8], "dates", backward)

    def send(stack):
        return jnp.stack([rotate(stack[k - 1], k) for k in range(1, blocks)])

    pixel = (dates, lines, width)
    block = (dates_here, lines, all_columns)
    part = (blocks - 1, dates_here, lines, width)
    rows = (dates, width)
    ends_shape = (16, LANES)
    vector = (8, LANES)
    window_shape = (blocks - 1, length, lines, width)
    edges_shape = (blocks - 1, 2 * dates_here, width)

    half = max(dates_here // 2, 1)

    def send_parts(spans):
        return call(
            functools.partial(send_kernel, blocks, spans),
            [(blocks - 1, stop - start, lines, width) for _, start, stop in spans],
            [(part, jnp.int32), part, part, pltpu.SemaphoreType.DMA((blocks - 1, dates_here, 3))],
            [place],
            [obs_mask, precision, observed],
            HBM,
        )

    (rhs_part,) = send_parts([("rhs", 0, half)])
    rhs_late_part, weight_part = send_parts([("rhs", half, dates_here), ("weight", 0, dates_here)])
    rhs_other = send(rhs_part)
    rhs_late = send(rhs_late_part)
    weight_other = send(weight_part)


    staged, weight_here, rhs_here, weights, last_row = call(
        stage_kernel,
        [(inverse.shape, inverse.dtype), block, block, (3, lines, all_columns), (lines, all_columns)],
        [
            (block, jnp.int32), block, block, (edge_class.shape, jnp.int32),
            pltpu.SemaphoreType.DMA((dates_here, 3)), pltpu.SemaphoreType.DMA((dates + 1,)),
        ],
        [],
        [obs_mask, precision, observed, edge_class, inverse],
        HBM,
    )
    zero_one = jnp.zeros((1,), jnp.float32)
    tau = jnp.concatenate([zero_one, temporal_weight, zero_one])

    row_above = lax.ppermute(last_row, "rows", [(i, i + 1) for i in range(slabs - 1)])
    rhs_here, row_above = lax.optimization_barrier((rhs_here, row_above))
    early_shape = (blocks - 1, (length + 1) // 2, lines, width)
    late_shape = (blocks - 1, length // 2, lines, width)
    precond, p_first, p_second, p_ends, p_early, p_late, dot_1 = call(
        functools.partial(first_kernel, blocks),
        [pixel, rows, rows, ends_shape, early_shape, late_shape, vector],
        [pixel],
        [place],
        [rhs_here, rhs_other, rhs_late, staged],
    )
    p_halo_1, p_halo_2 = swap_rows(p_first, p_second)
    p_left, p_right = swap_ends(p_ends)
    p_early, p_late, p_left, p_halo_2 = lax.optimization_barrier((p_early, p_late, p_left, p_halo_2))
    precond_early = send(p_early)
    precond_late = send(p_late)
    mapped, m_first, m_second, m_ends, m_windows, p_forward, data_weight, dot_2, dot_3 = call(
        functools.partial(second_kernel, blocks),
        [pixel, rows, rows, ends_shape, window_shape, edges_shape, pixel, vector, vector],
        [pixel, vector],
        [place, tau],
        [weights, row_above, precond, p_halo_1, p_halo_2, p_left, p_right, weight_here, weight_other, staged],
    )
    m_halo_1, m_halo_2 = swap_rows(m_first, m_second)
    m_halo_1, precond_early, precond_late = lax.optimization_barrier((m_halo_1, precond_early, precond_late))
    m_ends_other = () if blocks == 2 else swap_ends(m_ends)
    sums, m_forward = call(
        functools.partial(third_kernel, blocks),
        [vector, edges_shape],
        [vector],
        [place, tau],
        [weights, row_above, mapped, m_halo_1, m_halo_2, data_weight, dot_1, dot_2, dot_3, *m_ends_other],
    )
    precond_halos = send(p_forward)
    sums, precond_halos = lax.optimization_barrier((sums, precond_halos))
    if blocks == 2:
        ends_other, sums_other = rotate(m_ends, 1), rotate(sums, 1)
        (sums,) = call(join_kernel, [vector], [], [place], [weights, m_ends, sums, ends_other, sums_other])
    else:
        steps = 1
        while steps < blocks:
            sums = sums + lax.ppermute(sums, "dates", [(i, i ^ steps) for i in range(blocks)])
            steps *= 2
    m_windows, m_forward, sums = lax.optimization_barrier((m_windows, m_forward, sums))
    mapped_halos = send(m_forward)
    mapped_other = send(m_windows)
    steps = 1
    while steps < slabs:
        sums = sums + lax.ppermute(sums, "rows", [(i, i ^ steps) for i in range(slabs)])
        steps *= 2
    return tuple(
        call(
            functools.partial(last_kernel, blocks),
            [block, block],
            [(length, lines, all_columns), (dates_here, all_columns), (dates_here, all_columns)],
            [place, tau],
            [
                weights, row_above, sums, precond, mapped, precond_early, precond_late, mapped_other, p_halo_1, p_halo_2, m_halo_1, m_halo_2,
                precond_halos, mapped_halos, weight_here, rhs_here,
            ],
        )
    )


def solution(mesh):
    return jax.shard_map(
        functools.partial(body, mesh.shape["dates"], mesh.shape["rows"]),
        mesh=mesh,
        in_specs=(
            P("dates", "rows", None),
            P("dates", "rows", None),
            P("dates", "rows", None),
            P(None, "rows", None),
            P(),
            P(None, None, "rows", "dates"),
        ),
        out_specs=(P("dates", "rows", None), P("dates", "rows", None)),
        check_vma=False,
    )
```

time: 94.9 us -> 74.1 us (0.78)
  the two profiles are of different devices: /device:TPU:0 before, /device:TPU:24 now
where the time goes in v2:
time: 74.1 us; the launch traced here: 73.8 us
  waiting for transfers between devices  27.7 us (37%)
  Pallas kernels  23.3 us (31%)
  starting transfers between devices  21.9 us (30%)
  between operations  0.75 us (1%)
    pallas_call x8, Pallas kernels, call(): pl.pallas_call(kernel, out_shape=[jax.ShapeDtypeStruct(*typed(entry)) for...  23.3 us
    ppermute x11, starting transfers between devices, rotate(): lax.ppermute(value, 'dates', [(i, (i + k) % blocks) for i in range(blocks)])  12.8 us
    ppermute x4, waiting for transfers between devices, body(): lax.ppermute(sums, 'rows', [(i, i ^ steps) for i in range(slabs)])  10.7 us
    ppermute x11, waiting for transfers between devices, rotate(): lax.ppermute(value, 'dates', [(i, (i + k) % blocks) for i in range(blocks)])  10.2 us
    ppermute x2, starting transfers between devices, swap_rows(): lax.ppermute(second, 'rows', across_pairs)  4.69 us
    ppermute x1, waiting for transfers between devices, body(): lax.ppermute(last_row, 'rows', [(i, i + 1) for i in range(slabs - 1)])  3.67 us
    ppermute x2, waiting for transfers between devices, swap_rows(): lax.ppermute(second, 'rows', across_pairs)  3.1 us
    ppermute x4, starting transfers between devices, body(): lax.ppermute(sums, 'rows', [(i, i ^ steps) for i in range(slabs)])  2.19 us
  transfers between devices with their start and end apart: 20, of which 11 were waited for; matrix products, arithmetic and copies ran while one was open for 0% of the time, Pallas kernels for 23%

profile of v2, /device:TPU:24, one launch (start us, length us, event | category | flops | bytes accessed | tf_op | source)
XLA Modules:
  0.0 73.8 jit_solution(12082061269999095202)
XLA Ops:
  0.6 0.1 pad_add_fusion.place
  0.7 1.9 %shard_map.78 = f32[1,4,8,2048]{3,2,1,0:T(8,128)S(1)} custom-call(s32[4]{0:T(128)S(1)} %pad_add_fusion.place, s32[8,8,4096]{2,1,0:T(8,128)} %mask.5, f32[8,8,4096]{2,1,0:T(8,128)} %precision.5, f32[8,8,4096]{2,1,0:T(8,128)} %observed.5), custom_call_target="tpu_custom_call" | custom-call | flops 1 | bytes 1 | tf_op jit(solution)/shard_map/pallas_call | solution.py:26
  2.6 1.6 %collective-permute-start.1 = (f32[4,8,2048]{2,1,0:T(8,128)S(1)}, f32[4,8,2048]{2,1,0:T(8,128)S(1)}, u32[]{:S(2)}, u32[]{:S(2)}) collective-permute-start(f32[4,8,2048]{2,1,0:T(8,128)S(1)} %bitcast.26), channel_id=1, source_target_pairs={{0,1},{1,0},{2,3},{3,2},{4,5},{5,4},{6,7},{7,6},{8,9},{9,8},{10,11... | collective-permute-start | bytes 786440 | tf_op jit(solution)/shard_map/ppermute | solution.py:413
  4.2 2.1 %shard_map.79 = (f32[1,4,8,2048]{3,2,1,0:T(8,128)S(1)}, f32[1,8,8,2048]{3,2,1,0:T(8,128)S(1)}) custom-call(s32[4]{0:T(128)S(1)} %pad_add_fusion.place, s32[8,8,4096]{2,1,0:T(8,128)} %mask.5, f32[8,8,4096]{2,1,0:T(8,128)} %precision.5, f32[8,8,4096]{2,1,0:T(8,128)} %observed.5), custom_call_target="tpu_custom_call" | custom-call | flops 1 | bytes 1 | tf_op jit(solution)/shard_map/pallas_call | solution.py:26
  6.3 0.0 copy-start
  6.3 0.6 collective-permute-start.2
  6.9 4.8 %shard_map.77 = (bf16[16,16,8,2048]{3,2,1,0:T(8,128)(2,1)S(1)}, f32[8,8,4096]{2,1,0:T(8,128)S(1)}, f32[8,8,4096]{2,1,0:T(8,128)S(1)}, f32[3,8,4096]{2,1,0:T(8,128)S(1)}, f32[8,4096]{1,0:T(8,128)S(1)}) custom-call(s32[8,8,4096]{2,1,0:T(8,128)} %mask.5, f32[8,8,4096]{2,1,0:T(8,128)} %precision.5, f32[8,8,4096]{2,1,0:T(8,128)} %observed.5, ...), custom_call_target="tpu_custom_call" | custom-call | flops 1 | bytes 1 | tf_op jit(solution)/shard_map/pallas_call | solution.py:26
  11.7 1.9 %collective-permute-start = (f32[8,4096]{1,0:T(8,128)S(1)}, f32[8,4096]{1,0:T(8,128)S(1)}, u32[]{:S(2)}, u32[]{:S(2)}) collective-permute-start(f32[8,4096]{1,0:T(8,128)S(1)} %get-tuple-element.43), channel_id=1, source_target_pairs={{0,2},{2,4},{4,6},{6,8},{8,10},{10,12},{12,14},{14,16},{16,18},{18... | collective-permute-start | bytes 393224 | tf_op jit(solution)/shard_map/ppermute | solution.py:471
  13.7 1.6 %collective-permute-start.6 = (f32[8,8,2048]{2,1,0:T(8,128)S(1)}, f32[8,8,2048]{2,1,0:T(8,128)S(1)}, u32[]{:S(2)}, u32[]{:S(2)}) collective-permute-start(f32[8,8,2048]{2,1,0:T(8,128)S(1)} %bitcast.30), channel_id=1, source_target_pairs={{0,1},{1,0},{2,3},{3,2},{4,5},{5,4},{6,7},{7,6},{8,9},{9,8},{10,11... | collective-permute-start | bytes 1572872 | tf_op jit(solution)/shard_map/ppermute | solution.py:413
  15.2 3.7 %collective-permute-done.row_above = f32[8,4096]{1,0:T(8,128)S(1)} collective-permute-done((f32[8,4096]{1,0:T(8,128)S(1)}, f32[8,4096]{1,0:T(8,128)S(1)}, u32[]{:S(2)}, u32[]{:S(2)}) %collective-permute-start) | collective-permute-done | bytes 131104 | tf_op jit(solution)/shard_map/ppermute | solution.py:471
  18.9 0.0 collective-permute-done.1
  18.9 0.0 collective-permute-done.2
  18.9 3.5 %shard_map.80 = (f32[16,8,2048]{2,1,0:T(8,128)S(1)}, f32[16,2048]{1,0:T(8,128)S(1)}, f32[16,2048]{1,0:T(8,128)S(1)}, f32[16,128]{1,0:T(8,128)S(1)}, f32[1,5,8,20...) custom-call(s32[4]{0:T(128)S(1)} %pad_add_fusion.place, ...), custom_call_target="tpu_custom_call" | custom-call | flops 1 | bytes 1 | tf_op jit(solution)/shard_map/pallas_call | solution.py:26
  22.4 1.6 %collective-permute-start.4 = (f32[16,128]{1,0:T(8,128)S(1)}, f32[16,128]{1,0:T(8,128)S(1)}, u32[]{:S(2)}, u32[]{:S(2)}) collective-permute-start(f32[16,128]{1,0:T(8,128)S(1)} %get-tuple-element.52), channel_id=1, source_target_pairs={{0,1},{1,0},{2,3},{3,2},{4,5},{5,4},{6,7},{7,6},{8,9},{9,8},{10,11... | collective-permute-start | bytes 24584 | tf_op jit(solution)/shard_map/ppermute | solution.py:413
  24.0 1.9 %collective-permute-start.5 = (f32[16,2048]{1,0:T(8,128)S(1)}, f32[16,2048]{1,0:T(8,128)S(1)}, u32[]{:S(2)}, u32[]{:S(2)}) collective-permute-start(f32[16,2048]{1,0:T(8,128)S(1)} %get-tuple-element.53), channel_id=1, source_target_pairs={{2,4},{6,8},{10,12},{14,16},{18,20},{22,24},{26,28},{4,2},{8,6},{1... | collective-permute-start | bytes 393224 | tf_op jit(solution)/shard_map/ppermute | solution.py:416
  25.9 2.2 %collective-permute-done.4 = f32[16,128]{1,0:T(8,128)S(1)} collective-permute-done((f32[16,128]{1,0:T(8,128)S(1)}, f32[16,128]{1,0:T(8,128)S(1)}, u32[]{:S(2)}, u32[]{:S(2)}) %collective-permute-start.4) | collective-permute-done | bytes 8224 | tf_op jit(solution)/shard_map/ppermute | solution.py:413
  28.1 3.0 %collective-permute-done.5.halo_2.own_p2 = f32[16,2048]{1,0:T(8,128)S(1)} collective-permute-done((f32[16,2048]{1,0:T(8,128)S(1)}, f32[16,2048]{1,0:T(8,128)S(1)}, u32[]{:S(2)}, u32[]{:S(2)}) %collective-permute-start.5) | collective-permute-done | bytes 131104 | tf_op jit(solution)/shard_map/ppermute | solution.py:416
  31.2 0.5 collective-permute-start.8
  31.7 1.5 %collective-permute-start.9 = (f32[4,8,2048]{2,1,0:T(8,128)S(1)}, f32[4,8,2048]{2,1,0:T(8,128)S(1)}, u32[]{:S(2)}, u32[]{:S(2)}) collective-permute-start(f32[4,8,2048]{2,1,0:T(8,128)S(1)} %bitcast.32), channel_id=1, source_target_pairs={{0,1},{1,0},{2,3},{3,2},{4,5},{5,4},{6,7},{7,6},{8,9},{9,8},{10,11... | collective-permute-start | bytes 786440 | tf_op jit(solution)/shard_map/ppermute | solution.py:413
  33.2 0.1 pad_maximum_fusion.tau
  33.3 0.0 collective-permute-done.3.halo_1.own_p1
  33.3 0.0 collective-permute-done.6
  33.3 4.8 %shard_map.81 = (f32[16,8,2048]{2,1,0:T(8,128)S(1)}, f32[16,2048]{1,0:T(8,128)S(1)}, f32[16,2048]{1,0:T(8,128)S(1)}, f32[16,128]{1,0:T(8,128)S(1)}, f32[1,9,8,20...) custom-call(s32[4]{0:T(128)S(1)} %pad_add_fusion.place, ...), custom_call_target="tpu_custom_call" | custom-call | flops 1 | bytes 1 | tf_op jit(solution)/shard_map/pallas_call | solution.py:26
  38.1 0.3 collective-permute-start.7
  38.4 2.8 %collective-permute-start.10 = (f32[16,2048]{1,0:T(8,128)S(1)}, f32[16,2048]{1,0:T(8,128)S(1)}, u32[]{:S(2)}, u32[]{:S(2)}) collective-permute-start(f32[16,2048]{1,0:T(8,128)S(1)} %get-tuple-element.64), channel_id=1, source_target_pairs={{2,4},{6,8},{10,12},{14,16},{18,20},{22,24},{26,28},{4,2},{8,6},{1... | collective-permute-start | bytes 393224 | tf_op jit(solution)/shard_map/ppermute | solution.py:416
  41.2 1.3 %collective-permute-start.11 = (f32[16,2048]{1,0:T(8,128)S(1)}, f32[16,2048]{1,0:T(8,128)S(1)}, u32[]{:S(2)}, u32[]{:S(2)}) collective-permute-start(f32[16,2048]{1,0:T(8,128)S(1)} %bitcast.35), channel_id=1, source_target_pairs={{0,1},{1,0},{2,3},{3,2},{4,5},{5,4},{6,7},{7,6},{8,9},{9,8},{10,11... | collective-permute-start | bytes 393224 | tf_op jit(solution)/shard_map/ppermute | solution.py:413
  42.5 0.0 collective-permute-done.7.halo_1.own_m1
  42.5 0.8 %collective-permute-start.12 = (f32[16,128]{1,0:T(8,128)S(1)}, f32[16,128]{1,0:T(8,128)S(1)}, u32[]{:S(2)}, u32[]{:S(2)}) collective-permute-start(f32[16,128]{1,0:T(8,128)S(1)} %get-tuple-element.70.ends), channel_id=1, source_target_pairs={{0,1},{1,0},{2,3},{3,2},{4,5},{5,4},{6,7},{7,6},{8,9},{9,8},{10,11... | collective-permute-start | bytes 24584 | tf_op jit(solution)/shard_map/ppermute | solution.py:413
  43.3 2.3 %collective-permute-done.9 = f32[4,8,2048]{2,1,0:T(8,128)S(1)} collective-permute-done((f32[4,8,2048]{2,1,0:T(8,128)S(1)}, f32[4,8,2048]{2,1,0:T(8,128)S(1)}, u32[]{:S(2)}, u32[]{:S(2)}) %collective-permute-start.9) | collective-permute-done | bytes 262176 | tf_op jit(solution)/shard_map/ppermute | solution.py:413
  45.6 0.0 collective-permute-done.8
  45.6 0.1 collective-permute-done.10.halo_2.own_m2
  45.7 1.7 %shard_map.82 = (f32[8,128]{1,0:T(8,128)S(1)}, f32[1,16,2048]{2,1,0:T(8,128)S(1)}) custom-call(s32[4]{0:T(128)S(1)} %pad_add_fusion.place, f32[17]{0:T(128)S(1)} %pad_maximum_fusion.tau, f32[3,8,4096]{2,1,0:T(8,128)S(1)} %get-tuple-element.41.weights.weights_all, f32[8,4096]{1,0:T(8,128)S(1)} %collective-permute-done.row_above, ...), custom_call_target="tpu_custom_call" | custom-call | flops 1 | bytes 1 | tf_op jit(solution)/shard_map/pallas_call | solution.py:26
  47.4 0.0 collective-permute-done.11
  47.4 1.2 %collective-permute-start.13 = (f32[8,128]{1,0:T(8,128)S(1)}, f32[8,128]{1,0:T(8,128)S(1)}, u32[]{:S(2)}, u32[]{:S(2)}) collective-permute-start(f32[8,128]{1,0:T(8,128)S(1)} %get-tuple-element.73.sums), channel_id=1, source_target_pairs={{0,1},{1,0},{2,3},{3,2},{4,5},{5,4},{6,7},{7,6},{8,9},{9,8},{10,11... | collective-permute-start | bytes 12296 | tf_op jit(solution)/shard_map/ppermute | solution.py:413
  48.7 2.4 %collective-permute-done.13.sums_other = f32[8,128]{1,0:T(8,128)S(1)} collective-permute-done((f32[8,128]{1,0:T(8,128)S(1)}, f32[8,128]{1,0:T(8,128)S(1)}, u32[]{:S(2)}, u32[]{:S(2)}) %collective-permute-start.13) | collective-permute-done | bytes 4128 | tf_op jit(solution)/shard_map/ppermute | solution.py:413
  51.1 0.7 shard_map.83
  51.9 1.2 %collective-permute-start.18 = (f32[9,8,2048]{2,1,0:T(8,128)S(1)}, f32[9,8,2048]{2,1,0:T(8,128)S(1)}, u32[]{:S(2)}, u32[]{:S(2)}) collective-permute-start(f32[9,8,2048]{2,1,0:T(8,128)S(1)} %bitcast.29), channel_id=1, source_target_pairs={{0,1},{1,0},{2,3},{3,2},{4,5},{5,4},{6,7},{7,6},{8,9},{9,8},{10,11... | collective-permute-start | bytes 1769480 | tf_op jit(solution)/shard_map/ppermute | solution.py:413
  53.1 0.9 %collective-permute-start.19 = (f32[16,2048]{1,0:T(8,128)S(1)}, f32[16,2048]{1,0:T(8,128)S(1)}, u32[]{:S(2)}, u32[]{:S(2)}) collective-permute-start(f32[16,2048]{1,0:T(8,128)S(1)} %bitcast.34), channel_id=1, source_target_pairs={{0,1},{1,0},{2,3},{3,2},{4,5},{5,4},{6,7},{7,6},{8,9},{9,8},{10,11... | collective-permute-start | bytes 393224 | tf_op jit(solution)/shard_map/ppermute | solution.py:413
  54.0 1.2 %collective-permute-done.14 = f32[8,128]{1,0:T(8,128)S(1)} collective-permute-done((f32[8,128]{1,0:T(8,128)S(1)}, f32[8,128]{1,0:T(8,128)S(1)}, u32[]{:S(2)}, u32[]{:S(2)}) %collective-permute-start.14) | collective-permute-done | bytes 4128 | tf_op jit(solution)/shard_map/ppermute | solution.py:519
  55.1 0.4 collective-permute-start.15
  55.5 3.2 %collective-permute-done.15 = f32[8,128]{1,0:T(8,128)S(1)} collective-permute-done((f32[8,128]{1,0:T(8,128)S(1)}, f32[8,128]{1,0:T(8,128)S(1)}, u32[]{:S(2)}, u32[]{:S(2)}) %collective-permute-start.15) | collective-permute-done | bytes 4128 | tf_op jit(solution)/shard_map/ppermute | solution.py:519
  58.7 1.0 %collective-permute-start.16 = (f32[8,128]{1,0:T(8,128)S(1)}, f32[8,128]{1,0:T(8,128)S(1)}, u32[]{:S(2)}, u32[]{:S(2)}) collective-permute-start(f32[8,128]{1,0:T(8,128)S(1)} %add.13), channel_id=1, source_target_pairs={{0,8},{2,10},{4,12},{6,14},{8,0},{10,2},{12,4},{14,6},{16,24},{18,... | collective-permute-start | bytes 12296 | tf_op jit(solution)/shard_map/ppermute | solution.py:519
  59.7 2.7 %collective-permute-done.16 = f32[8,128]{1,0:T(8,128)S(1)} collective-permute-done((f32[8,128]{1,0:T(8,128)S(1)}, f32[8,128]{1,0:T(8,128)S(1)}, u32[]{:S(2)}, u32[]{:S(2)}) %collective-permute-start.16) | collective-permute-done | bytes 4128 | tf_op jit(solution)/shard_map/ppermute | solution.py:519
  62.3 0.8 %collective-permute-start.17 = (f32[8,128]{1,0:T(8,128)S(1)}, f32[8,128]{1,0:T(8,128)S(1)}, u32[]{:S(2)}, u32[]{:S(2)}) collective-permute-start(f32[8,128]{1,0:T(8,128)S(1)} %add.14), channel_id=1, source_target_pairs={{0,16},{2,18},{4,20},{6,22},{8,24},{10,26},{12,28},{14,30},{16,0},... | collective-permute-start | bytes 12296 | tf_op jit(solution)/shard_map/ppermute | solution.py:519
  63.2 3.7 %collective-permute-done.17 = f32[8,128]{1,0:T(8,128)S(1)} collective-permute-done((f32[8,128]{1,0:T(8,128)S(1)}, f32[8,128]{1,0:T(8,128)S(1)}, u32[]{:S(2)}, u32[]{:S(2)}) %collective-permute-start.17) | collective-permute-done | bytes 4128 | tf_op jit(solution)/shard_map/ppermute | solution.py:519
  66.9 3.2 %collective-permute-done.19 = f32[16,2048]{1,0:T(8,128)S(1)} collective-permute-done((f32[16,2048]{1,0:T(8,128)S(1)}, f32[16,2048]{1,0:T(8,128)S(1)}, u32[]{:S(2)}, u32[]{:S(2)}) %collective-permute-start.19) | collective-permute-done | bytes 131104 | tf_op jit(solution)/shard_map/ppermute | solution.py:413
  70.1 0.0 collective-permute-done.18
  70.1 3.7 %shard_map.84 = (f32[8,8,4096]{2,1,0:T(8,128)}, f32[8,8,4096]{2,1,0:T(8,128)}) custom-call(s32[4]{0:T(128)S(1)} %pad_add_fusion.place, f32[17]{0:T(128)S(1)} %pad_maximum_fusion.tau, f32[3,8,4096]{2,1,0:T(8,128)S(1)} %get-tuple-element.41.weights.weights_all, f32[8,4096]{1,0:T(8,128)S(1)} %collective-permute-done.row_above, f32[8,128]{1,0:T(8,128)S(1)} %add.15.sums, ...), custom_call_target="tpu_custom_call" | custom-call | flops 1 | bytes 1 | tf_op jit(solution)/shard_map/pallas_call | solution.py:26
  (9 shorter events, 0.0 us)
Async XLA Ops:
  2.6 16.3 %collective-permute-start.1 = (f32[4,8,2048]{2,1,0:T(8,128)S(1)}, f32[4,8,2048]{2,1,0:T(8,128)S(1)}, u32[]{:S(2)}, u32[]{:S(2)}) collective-permute-start(f32[4,8,2048]{2,1,0:T(8,128)S(1)} %bitcast.26), channel_id=1, source_target_pairs={{0,1},{1,0},{2,3},{3,2},{4,5},{5,4},{6,7},{7,6},{8,9},{9,8},{10,11... | collective-permute-start | bytes 786440 | tf_op jit(solution)/shard_map/ppermute | solution.py:413
  6.3 26.9 %copy-start = (f32[15]{0:T(128)S(1)}, f32[15]{0:T(128)}, u32[]{:S(2)}) copy-start(f32[15]{0:T(128)} %param.10) | copy-start | bytes 184
  6.3 12.6 %collective-permute-start.2 = (f32[4,8,2048]{2,1,0:T(8,128)S(1)}, f32[4,8,2048]{2,1,0:T(8,128)S(1)}, u32[]{:S(2)}, u32[]{:S(2)}) collective-permute-start(f32[4,8,2048]{2,1,0:T(8,128)S(1)} %bitcast.33), channel_id=1, source_target_pairs={{0,1},{1,0},{2,3},{3,2},{4,5},{5,4},{6,7},{7,6},{8,9},{9,8},{10,11... | collective-permute-start | bytes 786440 | tf_op jit(solution)/shard_map/ppermute | solution.py:413
  11.7 7.2 %collective-permute-start = (f32[8,4096]{1,0:T(8,128)S(1)}, f32[8,4096]{1,0:T(8,128)S(1)}, u32[]{:S(2)}, u32[]{:S(2)}) collective-permute-start(f32[8,4096]{1,0:T(8,128)S(1)} %get-tuple-element.43), channel_id=1, source_target_pairs={{0,2},{2,4},{4,6},{6,8},{8,10},{10,12},{12,14},{14,16},{16,18},{18... | collective-permute-start | bytes 393224 | tf_op jit(solution)/shard_map/ppermute | solution.py:471
  13.7 19.6 %collective-permute-start.6 = (f32[8,8,2048]{2,1,0:T(8,128)S(1)}, f32[8,8,2048]{2,1,0:T(8,128)S(1)}, u32[]{:S(2)}, u32[]{:S(2)}) collective-permute-start(f32[8,8,2048]{2,1,0:T(8,128)S(1)} %bitcast.30), channel_id=1, source_target_pairs={{0,1},{1,0},{2,3},{3,2},{4,5},{5,4},{6,7},{7,6},{8,9},{9,8},{10,11... | collective-permute-start | bytes 1572872 | tf_op jit(solution)/shard_map/ppermute | solution.py:413
  22.4 5.7 %collective-permute-start.4 = (f32[16,128]{1,0:T(8,128)S(1)}, f32[16,128]{1,0:T(8,128)S(1)}, u32[]{:S(2)}, u32[]{:S(2)}) collective-permute-start(f32[16,128]{1,0:T(8,128)S(1)} %get-tuple-element.52), channel_id=1, source_target_pairs={{0,1},{1,0},{2,3},{3,2},{4,5},{5,4},{6,7},{7,6},{8,9},{9,8},{10,11... | collective-permute-start | bytes 24584 | tf_op jit(solution)/shard_map/ppermute | solution.py:413
  24.0 7.2 %collective-permute-start.5 = (f32[16,2048]{1,0:T(8,128)S(1)}, f32[16,2048]{1,0:T(8,128)S(1)}, u32[]{:S(2)}, u32[]{:S(2)}) collective-permute-start(f32[16,2048]{1,0:T(8,128)S(1)} %get-tuple-element.53), channel_id=1, source_target_pairs={{2,4},{6,8},{10,12},{14,16},{18,20},{22,24},{26,28},{4,2},{8,6},{1... | collective-permute-start | bytes 393224 | tf_op jit(solution)/shard_map/ppermute | solution.py:416
  31.2 14.4 %collective-permute-start.8 = (f32[5,8,2048]{2,1,0:T(8,128)S(1)}, f32[5,8,2048]{2,1,0:T(8,128)S(1)}, u32[]{:S(2)}, u32[]{:S(2)}) collective-permute-start(f32[5,8,2048]{2,1,0:T(8,128)S(1)} %bitcast.31), channel_id=1, source_target_pairs={{0,1},{1,0},{2,3},{3,2},{4,5},{5,4},{6,7},{7,6},{8,9},{9,8},{10,11... | collective-permute-start | bytes 983048 | tf_op jit(solution)/shard_map/ppermute | solution.py:413
  31.7 1.6 %collective-permute-start.3 = (f32[16,2048]{1,0:T(8,128)S(1)}, f32[16,2048]{1,0:T(8,128)S(1)}, u32[]{:S(2)}, u32[]{:S(2)}) collective-permute-start(f32[16,2048]{1,0:T(8,128)S(1)} %get-tuple-element.49), channel_id=1, source_target_pairs={{0,2},{2,0},{4,6},{6,4},{8,10},{10,8},{12,14},{14,12},{16,18},{18,... | collective-permute-start | bytes 393224 | tf_op jit(solution)/shard_map/ppermute | solution.py:416
  31.7 13.9 %collective-permute-start.9 = (f32[4,8,2048]{2,1,0:T(8,128)S(1)}, f32[4,8,2048]{2,1,0:T(8,128)S(1)}, u32[]{:S(2)}, u32[]{:S(2)}) collective-permute-start(f32[4,8,2048]{2,1,0:T(8,128)S(1)} %bitcast.32), channel_id=1, source_target_pairs={{0,1},{1,0},{2,3},{3,2},{4,5},{5,4},{6,7},{7,6},{8,9},{9,8},{10,11... | collective-permute-start | bytes 786440 | tf_op jit(solution)/shard_map/ppermute | solution.py:413
  38.1 4.4 %collective-permute-start.7 = (f32[16,2048]{1,0:T(8,128)S(1)}, f32[16,2048]{1,0:T(8,128)S(1)}, u32[]{:S(2)}, u32[]{:S(2)}) collective-permute-start(f32[16,2048]{1,0:T(8,128)S(1)} %get-tuple-element.60), channel_id=1, source_target_pairs={{0,2},{2,0},{4,6},{6,4},{8,10},{10,8},{12,14},{14,12},{16,18},{18,... | collective-permute-start | bytes 393224 | tf_op jit(solution)/shard_map/ppermute | solution.py:416
  38.4 7.3 %collective-permute-start.10 = (f32[16,2048]{1,0:T(8,128)S(1)}, f32[16,2048]{1,0:T(8,128)S(1)}, u32[]{:S(2)}, u32[]{:S(2)}) collective-permute-start(f32[16,2048]{1,0:T(8,128)S(1)} %get-tuple-element.64), channel_id=1, source_target_pairs={{2,4},{6,8},{10,12},{14,16},{18,20},{22,24},{26,28},{4,2},{8,6},{1... | collective-permute-start | bytes 393224 | tf_op jit(solution)/shard_map/ppermute | solution.py:416
  41.2 6.2 %collective-permute-start.11 = (f32[16,2048]{1,0:T(8,128)S(1)}, f32[16,2048]{1,0:T(8,128)S(1)}, u32[]{:S(2)}, u32[]{:S(2)}) collective-permute-start(f32[16,2048]{1,0:T(8,128)S(1)} %bitcast.35), channel_id=1, source_target_pairs={{0,1},{1,0},{2,3},{3,2},{4,5},{5,4},{6,7},{7,6},{8,9},{9,8},{10,11... | collective-permute-start | bytes 393224 | tf_op jit(solution)/shard_map/ppermute | solution.py:413
  42.5 6.2 %collective-permute-start.12 = (f32[16,128]{1,0:T(8,128)S(1)}, f32[16,128]{1,0:T(8,128)S(1)}, u32[]{:S(2)}, u32[]{:S(2)}) collective-permute-start(f32[16,128]{1,0:T(8,128)S(1)} %get-tuple-element.70.ends), channel_id=1, source_target_pairs={{0,1},{1,0},{2,3},{3,2},{4,5},{5,4},{6,7},{7,6},{8,9},{9,8},{10,11... | collective-permute-start | bytes 24584 | tf_op jit(solution)/shard_map/ppermute | solution.py:413
  47.4 3.7 %collective-permute-start.13 = (f32[8,128]{1,0:T(8,128)S(1)}, f32[8,128]{1,0:T(8,128)S(1)}, u32[]{:S(2)}, u32[]{:S(2)}) collective-permute-start(f32[8,128]{1,0:T(8,128)S(1)} %get-tuple-element.73.sums), channel_id=1, source_target_pairs={{0,1},{1,0},{2,3},{3,2},{4,5},{5,4},{6,7},{7,6},{8,9},{9,8},{10,11... | collective-permute-start | bytes 12296 | tf_op jit(solution)/shard_map/ppermute | solution.py:413
  51.9 18.2 %collective-permute-start.18 = (f32[9,8,2048]{2,1,0:T(8,128)S(1)}, f32[9,8,2048]{2,1,0:T(8,128)S(1)}, u32[]{:S(2)}, u32[]{:S(2)}) collective-permute-start(f32[9,8,2048]{2,1,0:T(8,128)S(1)} %bitcast.29), channel_id=1, source_target_pairs={{0,1},{1,0},{2,3},{3,2},{4,5},{5,4},{6,7},{7,6},{8,9},{9,8},{10,11... | collective-permute-start | bytes 1769480 | tf_op jit(solution)/shard_map/ppermute | solution.py:413
  53.1 17.0 %collective-permute-start.19 = (f32[16,2048]{1,0:T(8,128)S(1)}, f32[16,2048]{1,0:T(8,128)S(1)}, u32[]{:S(2)}, u32[]{:S(2)}) collective-permute-start(f32[16,2048]{1,0:T(8,128)S(1)} %bitcast.34), channel_id=1, source_target_pairs={{0,1},{1,0},{2,3},{3,2},{4,5},{5,4},{6,7},{7,6},{8,9},{9,8},{10,11... | collective-permute-start | bytes 393224 | tf_op jit(solution)/shard_map/ppermute | solution.py:413
  54.0 1.2 %collective-permute-start.14 = (f32[8,128]{1,0:T(8,128)S(1)}, f32[8,128]{1,0:T(8,128)S(1)}, u32[]{:S(2)}, u32[]{:S(2)}) collective-permute-start(f32[8,128]{1,0:T(8,128)S(1)} %shard_map.83), channel_id=1, source_target_pairs={{0,2},{2,0},{4,6},{6,4},{8,10},{10,8},{12,14},{14,12},{16,18},{18,... | collective-permute-start | bytes 12296 | tf_op jit(solution)/shard_map/ppermute | solution.py:519
  55.1 3.6 %collective-permute-start.15 = (f32[8,128]{1,0:T(8,128)S(1)}, f32[8,128]{1,0:T(8,128)S(1)}, u32[]{:S(2)}, u32[]{:S(2)}) collective-permute-start(f32[8,128]{1,0:T(8,128)S(1)} %add.12), channel_id=1, source_target_pairs={{0,4},{2,6},{4,0},{6,2},{8,12},{10,14},{12,8},{14,10},{16,20},{18,... | collective-permute-start | bytes 12296 | tf_op jit(solution)/shard_map/ppermute | solution.py:519
  58.7 3.6 %collective-permute-start.16 = (f32[8,128]{1,0:T(8,128)S(1)}, f32[8,128]{1,0:T(8,128)S(1)}, u32[]{:S(2)}, u32[]{:S(2)}) collective-permute-start(f32[8,128]{1,0:T(8,128)S(1)} %add.13), channel_id=1, source_target_pairs={{0,8},{2,10},{4,12},{6,14},{8,0},{10,2},{12,4},{14,6},{16,24},{18,... | collective-permute-start | bytes 12296 | tf_op jit(solution)/shard_map/ppermute | solution.py:519
  62.3 4.5 %collective-permute-start.17 = (f32[8,128]{1,0:T(8,128)S(1)}, f32[8,128]{1,0:T(8,128)S(1)}, u32[]{:S(2)}, u32[]{:S(2)}) collective-permute-start(f32[8,128]{1,0:T(8,128)S(1)} %add.14), channel_id=1, source_target_pairs={{0,16},{2,18},{4,20},{6,22},{8,24},{10,26},{12,28},{14,30},{16,0},... | collective-permute-start | bytes 12296 | tf_op jit(solution)/shard_map/ppermute | solution.py:519

commit v3 on v2

--- a/solution.py
+++ b/solution.py
@@ -17,7 +17,7 @@
 COST = pl.CostEstimate(flops=1, bytes_accessed=1, transcendentals=0)
 
 
-def call(kernel, out_shapes, scratch, scalars, arrays, space=VMEM):
+def call(kernel, out_shapes, scratch, scalars, arrays, space=VMEM, out_space=VMEM):
     def typed(entry):
         return entry if isinstance(entry[-1], (jnp.dtype, type)) else (entry, jnp.float32)
 
@@ -27,15 +27,15 @@
         kernel,
         out_shape=[jax.ShapeDtypeStruct(*typed(entry)) for entry in out_shapes],
         in_specs=[SMEM] * len(scalars) + [space] * len(arrays),
-        out_specs=[VMEM] * len(out_shapes),
+        out_specs=[out_space] * len(out_shapes),
         scratch_shapes=[pltpu.VMEM(*typed(entry)) if isinstance(entry, tuple) else entry for entry in scratch],
         compiler_params=PARAMS,
         cost_estimate=COST,
     )(*scalars, *arrays)
 
 
-def tile(index):
-    return pl.ds(pl.multiple_of(index * LANES, LANES), LANES)
+def tile(index, width=LANES):
+    return pl.ds(pl.multiple_of(index * width, LANES), width)
 
 
 def columns(block, width):
@@ -78,11 +78,13 @@
     return diagonal * value - (away + tau_up * later + tau_down * earlier)
 
 
-def apply_inverse(inverse, source, store, first_total):
+def apply_inverse(inverse, source, store):
     dates = inverse.shape[0]
+    width = source.shape[2]
+    step_width = 2 * LANES if width % (2 * LANES) == 0 else LANES
 
     def step(index, total):
-        lanes = tile(index)
+        lanes = tile(index, step_width)
         values = [source[s, :, lanes] for s in range(dates)]
         for t in range(dates):
             mapped = inverse[t, 0, :, lanes].astype(jnp.float32) * values[0]
@@ -92,7 +94,7 @@
             store(t, lanes, mapped)
         return total
 
-    return lax.fori_loop(0, source.shape[2] // LANES, step, first_total)
+    return fold(lax.fori_loop(0, width // step_width, step, jnp.zeros((8, step_width), jnp.float32)))
 
 
 def pack_edges(field, parity, first, second, ends):
@@ -222,7 +224,7 @@
     def store(t, lanes, value):
         precond[t, :, lanes] = value
 
-    dot[...] = apply_inverse(inverse, rhs, store, jnp.zeros((8, LANES), jnp.float32))
+    dot[...] = apply_inverse(inverse, rhs, store)
     pack_edges(precond, parity, first, second, ends)
     send_windows(precond, (early_windows, late_windows), date_block, blocks, dates_here)
 
@@ -232,7 +234,8 @@
     width = across.shape[1]
     rows = row_ids(width)
     downward = jnp.where((rows == 7) & (place[3] == 1), 0.0, downward)
-    downward_prev = jnp.where(rows == 0, above[0:1, lanes], pltpu.roll(downward, 1, 0))
+    row_above = jnp.where(place[2] == 0, 0.0, above[0:1, lanes])
+    downward_prev = jnp.where(rows == 0, row_above, pltpu.roll(downward, 1, 0))
     weights = (across, across_prev, downward, downward_prev)
     return weights, MASS + across + across_prev + downward + downward_prev
 
@@ -290,7 +293,7 @@
     def store(t, lanes, value):
         mapped[t, :, lanes] = value
 
-    dot_mapped[...] = apply_inverse(inverse, image_all, store, jnp.zeros((8, LANES), jnp.float32))
+    dot_mapped[...] = apply_inverse(inverse, image_all, store)
     pack_edges(mapped, parity, first, second, ends)
     send_windows(mapped, (windows,), date_block, blocks, dates_here)
     forward_halos(halo_1, halo_2, forwarded, date_block, blocks)
@@ -325,7 +328,7 @@
 
 def last_kernel(
     blocks, place, tau, weights_all, row_above, sums, precond, mapped, precond_early, precond_late, mapped_other, own_p1, own_p2, own_m1, own_m2,
-    precond_halos, mapped_halos, weight_here, rhs, solution, residual, field, above_all, below_all,
+    precond_halos, mapped_halos, weight_here, rhs, solution, residual, field, above_all, below_all, remainder, sent,
 ):
     date_block, parity = place[0], place[1]
     dates, _, width = precond.shape
@@ -371,6 +374,9 @@
             )
             above_all[j : j + 1, there] = above
             below_all[j : j + 1, there] = below
+    copies = [pltpu.make_async_copy(field.at[offset + j], solution.at[j], sent.at[0, j]) for j in range(dates_here)]
+    for copy in copies:
+        copy.start()
     weights, weight_sum = edge_weights(place, weights_all, row_above, slice(None))
     for j in range(dates_here):
         tau_up, tau_down = tau[date_block * dates_here + j + 1], tau[date_block * dates_here + j]
@@ -390,8 +396,12 @@
             tau_up,
             tau_down,
         )
-        solution[j] = value
-        residual[j] = rhs[j] - image
+        remainder[j] = rhs[j] - image
+        copy = pltpu.make_async_copy(remainder.at[j], residual.at[j], sent.at[1, j])
+        copy.start()
+        copies.append(copy)
+    for copy in copies:
+        copy.wait()
 
 
 def body(blocks, slabs, obs_mask, precision, observed, edge_class, temporal_weight, inverse):
@@ -406,7 +416,7 @@
     place = jnp.stack([date_block, parity, line_block, at_end]).astype(jnp.int32)
 
     pairs = [(i, i ^ 1) for i in range(slabs)]
-    across_pairs = [(i, i + 1) for i in range(1, slabs - 1, 2)]
+    across_pairs = [(i, (i + 1) % slabs) for i in range(1, slabs, 2)]
     across_pairs = across_pairs + [(b, a) for a, b in across_pairs]
 
     def rotate(value, k):
@@ -468,7 +478,7 @@
     zero_one = jnp.zeros((1,), jnp.float32)
     tau = jnp.concatenate([zero_one, temporal_weight, zero_one])
 
-    row_above = lax.ppermute(last_row, "rows", [(i, i + 1) for i in range(slabs - 1)])
+    row_above = lax.ppermute(last_row, "rows", [(i, (i + 1) % slabs) for i in range(slabs)])
     rhs_here, row_above = lax.optimization_barrier((rhs_here, row_above))
     early_shape = (blocks - 1, (length + 1) // 2, lines, width)
     late_shape = (blocks - 1, length // 2, lines, width)
@@ -492,7 +502,6 @@
         [weights, row_above, precond, p_halo_1, p_halo_2, p_left, p_right, weight_here, weight_other, staged],
     )
     m_halo_1, m_halo_2 = swap_rows(m_first, m_second)
-    m_halo_1, precond_early, precond_late = lax.optimization_barrier((m_halo_1, precond_early, precond_late))
     m_ends_other = () if blocks == 2 else swap_ends(m_ends)
     sums, m_forward = call(
         functools.partial(third_kernel, blocks),
@@ -502,7 +511,7 @@
         [weights, row_above, mapped, m_halo_1, m_halo_2, data_weight, dot_1, dot_2, dot_3, *m_ends_other],
     )
     precond_halos = send(p_forward)
-    sums, precond_halos = lax.optimization_barrier((sums, precond_halos))
+    sums, precond_early, precond_late = lax.optimization_barrier((sums, precond_early, precond_late))
     if blocks == 2:
         ends_other, sums_other = rotate(m_ends, 1), rotate(sums, 1)
         (sums,) = call(join_kernel, [vector], [], [place], [weights, m_ends, sums, ends_other, sums_other])
@@ -511,7 +520,7 @@
         while steps < blocks:
             sums = sums + lax.ppermute(sums, "dates", [(i, i ^ steps) for i in range(blocks)])
             steps *= 2
-    m_windows, m_forward, sums = lax.optimization_barrier((m_windows, m_forward, sums))
+    m_windows, m_forward, precond_halos, sums = lax.optimization_barrier((m_windows, m_forward, precond_halos, sums))
     mapped_halos = send(m_forward)
     mapped_other = send(m_windows)
     steps = 1
@@ -522,12 +531,16 @@
         call(
             functools.partial(last_kernel, blocks),
             [block, block],
-            [(length, lines, all_columns), (dates_here, all_columns), (dates_here, all_columns)],
+            [
+                (length, lines, all_columns), (dates_here, all_columns), (dates_here, all_columns), block,
+                pltpu.SemaphoreType.DMA((2, dates_here)),
+            ],
             [place, tau],
             [
                 weights, row_above, sums, precond, mapped, precond_early, precond_late, mapped_other, p_halo_1, p_halo_2, m_halo_1, m_halo_2,
                 precond_halos, mapped_halos, weight_here, rhs_here,
             ],
+            out_space=HBM,
         )
     )
 

time: 74.1 us -> 70.1 us (0.946)
  the two profiles are of different devices: /device:TPU:24 before, /device:TPU:0 now
where the time goes in v3:
time: 70.1 us; the launch traced here: 69.9 us
  waiting for transfers between devices  28.7 us (41%)
  Pallas kernels  21.5 us (31%)
  starting transfers between devices  18.8 us (27%)
  between operations  0.75 us (1%)
    pallas_call x8, Pallas kernels, call(): pl.pallas_call(kernel, out_shape=[jax.ShapeDtypeStruct(*typed(entry)) for...  21.5 us
    ppermute x11, starting transfers between devices, rotate(): lax.ppermute(value, 'dates', [(i, (i + k) % blocks) for i in range(blocks)])  14.6 us
    ppermute x4, waiting for transfers between devices, body(): lax.ppermute(sums, 'rows', [(i, i ^ steps) for i in range(slabs)])  12.1 us
    ppermute x11, waiting for transfers between devices, rotate(): lax.ppermute(value, 'dates', [(i, (i + k) % blocks) for i in range(blocks)])  6.45 us
    ppermute x2, waiting for transfers between devices, swap_rows(): lax.ppermute(second, 'rows', across_pairs)  5.17 us
    ppermute x1, waiting for transfers between devices, body(): lax.ppermute(last_row, 'rows', [(i, (i + 1) % slabs) for i in range(slabs)])  5.01 us
    ppermute x2, starting transfers between devices, swap_rows(): lax.ppermute(second, 'rows', across_pairs)  2.97 us
  transfers between devices with their start and end apart: 20, of which 9 were waited for; matrix products, arithmetic and copies ran while one was open for 0% of the time, Pallas kernels for 23%

profile of v3, /device:TPU:0, one launch (start us, length us, event | category | flops | bytes accessed | tf_op | source)
XLA Modules:
  0.0 69.9 jit_solution(224812837200056102)
XLA Ops:
  0.6 0.1 pad_add_fusion.place
  0.7 1.9 %shard_map.78 = f32[1,4,8,2048]{3,2,1,0:T(8,128)S(1)} custom-call(s32[4]{0:T(128)S(1)} %pad_add_fusion.place, s32[8,8,4096]{2,1,0:T(8,128)} %mask.5, f32[8,8,4096]{2,1,0:T(8,128)} %precision.5, f32[8,8,4096]{2,1,0:T(8,128)} %observed.5), custom_call_target="tpu_custom_call" | custom-call | flops 1 | bytes 1 | tf_op jit(solution)/shard_map/pallas_call | solution.py:26
  2.6 3.0 %collective-permute-start.1 = (f32[4,8,2048]{2,1,0:T(8,128)S(1)}, f32[4,8,2048]{2,1,0:T(8,128)S(1)}, u32[]{:S(2)}, u32[]{:S(2)}) collective-permute-start(f32[4,8,2048]{2,1,0:T(8,128)S(1)} %bitcast.26), channel_id=1, source_target_pairs={{0,1},{1,0},{2,3},{3,2},{4,5},{5,4},{6,7},{7,6},{8,9},{9,8},{10,11... | collective-permute-start | bytes 786440 | tf_op jit(solution)/shard_map/ppermute | solution.py:423
  5.7 2.1 %shard_map.79 = (f32[1,4,8,2048]{3,2,1,0:T(8,128)S(1)}, f32[1,8,8,2048]{3,2,1,0:T(8,128)S(1)}) custom-call(s32[4]{0:T(128)S(1)} %pad_add_fusion.place, s32[8,8,4096]{2,1,0:T(8,128)} %mask.5, f32[8,8,4096]{2,1,0:T(8,128)} %precision.5, f32[8,8,4096]{2,1,0:T(8,128)} %observed.5), custom_call_target="tpu_custom_call" | custom-call | flops 1 | bytes 1 | tf_op jit(solution)/shard_map/pallas_call | solution.py:26
  7.8 0.0 copy-start
  7.8 0.1 collective-permute-start.2
  7.9 4.8 %shard_map.77 = (bf16[16,16,8,2048]{3,2,1,0:T(8,128)(2,1)S(1)}, f32[8,8,4096]{2,1,0:T(8,128)S(1)}, f32[8,8,4096]{2,1,0:T(8,128)S(1)}, f32[3,8,4096]{2,1,0:T(8,128)S(1)}, f32[8,4096]{1,0:T(8,128)S(1)}) custom-call(s32[8,8,4096]{2,1,0:T(8,128)} %mask.5, f32[8,8,4096]{2,1,0:T(8,128)} %precision.5, f32[8,8,4096]{2,1,0:T(8,128)} %observed.5, ...), custom_call_target="tpu_custom_call" | custom-call | flops 1 | bytes 1 | tf_op jit(solution)/shard_map/pallas_call | solution.py:26
  12.7 0.1 collective-permute-start
  12.8 2.1 %collective-permute-start.6 = (f32[8,8,2048]{2,1,0:T(8,128)S(1)}, f32[8,8,2048]{2,1,0:T(8,128)S(1)}, u32[]{:S(2)}, u32[]{:S(2)}) collective-permute-start(f32[8,8,2048]{2,1,0:T(8,128)S(1)} %bitcast.30), channel_id=1, source_target_pairs={{0,1},{1,0},{2,3},{3,2},{4,5},{5,4},{6,7},{7,6},{8,9},{9,8},{10,11... | collective-permute-start | bytes 1572872 | tf_op jit(solution)/shard_map/ppermute | solution.py:423
  14.8 5.0 %collective-permute-done.row_above = f32[8,4096]{1,0:T(8,128)S(1)} collective-permute-done((f32[8,4096]{1,0:T(8,128)S(1)}, f32[8,4096]{1,0:T(8,128)S(1)}, u32[]{:S(2)}, u32[]{:S(2)}) %collective-permute-start) | collective-permute-done | bytes 131104 | tf_op jit(solution)/shard_map/ppermute | solution.py:481
  19.8 0.0 collective-permute-done.1
  19.8 0.0 collective-permute-done.2
  19.8 2.8 %shard_map.80 = (f32[16,8,2048]{2,1,0:T(8,128)S(1)}, f32[16,2048]{1,0:T(8,128)S(1)}, f32[16,2048]{1,0:T(8,128)S(1)}, f32[16,128]{1,0:T(8,128)S(1)}, f32[1,5,8,20...) custom-call(s32[4]{0:T(128)S(1)} %pad_add_fusion.place, ...), custom_call_target="tpu_custom_call" | custom-call | flops 1 | bytes 1 | tf_op jit(solution)/shard_map/pallas_call | solution.py:26
  22.6 2.1 %collective-permute-start.4 = (f32[16,128]{1,0:T(8,128)S(1)}, f32[16,128]{1,0:T(8,128)S(1)}, u32[]{:S(2)}, u32[]{:S(2)}) collective-permute-start(f32[16,128]{1,0:T(8,128)S(1)} %get-tuple-element.51), channel_id=1, source_target_pairs={{0,1},{1,0},{2,3},{3,2},{4,5},{5,4},{6,7},{7,6},{8,9},{9,8},{10,11... | collective-permute-start | bytes 24584 | tf_op jit(solution)/shard_map/ppermute | solution.py:423
  24.7 0.3 collective-permute-start.5
  25.0 4.0 %collective-permute-done.4 = f32[16,128]{1,0:T(8,128)S(1)} collective-permute-done((f32[16,128]{1,0:T(8,128)S(1)}, f32[16,128]{1,0:T(8,128)S(1)}, u32[]{:S(2)}, u32[]{:S(2)}) %collective-permute-start.4) | collective-permute-done | bytes 8224 | tf_op jit(solution)/shard_map/ppermute | solution.py:423
  29.0 2.8 %collective-permute-done.5.halo_2.own_p2 = f32[16,2048]{1,0:T(8,128)S(1)} collective-permute-done((f32[16,2048]{1,0:T(8,128)S(1)}, f32[16,2048]{1,0:T(8,128)S(1)}, u32[]{:S(2)}, u32[]{:S(2)}) %collective-permute-start.5) | collective-permute-done | bytes 131104 | tf_op jit(solution)/shard_map/ppermute | solution.py:426
  31.8 0.1 collective-permute-start.10
  31.9 0.0 collective-permute-start.3
  31.9 1.9 %collective-permute-start.11 = (f32[4,8,2048]{2,1,0:T(8,128)S(1)}, f32[4,8,2048]{2,1,0:T(8,128)S(1)}, u32[]{:S(2)}, u32[]{:S(2)}) collective-permute-start(f32[4,8,2048]{2,1,0:T(8,128)S(1)} %bitcast.32), channel_id=1, source_target_pairs={{0,1},{1,0},{2,3},{3,2},{4,5},{5,4},{6,7},{7,6},{8,9},{9,8},{10,11... | collective-permute-start | bytes 786440 | tf_op jit(solution)/shard_map/ppermute | solution.py:423
  33.8 0.1 pad_maximum_fusion.tau
  33.9 0.0 collective-permute-done.3.halo_1.own_p1
  33.9 0.0 collective-permute-done.6
  33.9 4.1 %shard_map.81 = (f32[16,8,2048]{2,1,0:T(8,128)S(1)}, f32[16,2048]{1,0:T(8,128)S(1)}, f32[16,2048]{1,0:T(8,128)S(1)}, f32[16,128]{1,0:T(8,128)S(1)}, f32[1,9,8,20...) custom-call(s32[4]{0:T(128)S(1)} %pad_add_fusion.place, ...), custom_call_target="tpu_custom_call" | custom-call | flops 1 | bytes 1 | tf_op jit(solution)/shard_map/pallas_call | solution.py:26
  38.0 0.3 collective-permute-start.7
  38.3 2.6 %collective-permute-start.8 = (f32[16,2048]{1,0:T(8,128)S(1)}, f32[16,2048]{1,0:T(8,128)S(1)}, u32[]{:S(2)}, u32[]{:S(2)}) collective-permute-start(f32[16,2048]{1,0:T(8,128)S(1)} %get-tuple-element.60), channel_id=1, source_target_pairs={{2,4},{6,8},{10,12},{14,16},{18,20},{22,24},{26,28},{30,0},{4,2},{... | collective-permute-start | bytes 393224 | tf_op jit(solution)/shard_map/ppermute | solution.py:426
  40.9 0.8 %collective-permute-start.9 = (f32[16,2048]{1,0:T(8,128)S(1)}, f32[16,2048]{1,0:T(8,128)S(1)}, u32[]{:S(2)}, u32[]{:S(2)}) collective-permute-start(f32[16,2048]{1,0:T(8,128)S(1)} %bitcast.35), channel_id=1, source_target_pairs={{0,1},{1,0},{2,3},{3,2},{4,5},{5,4},{6,7},{7,6},{8,9},{9,8},{10,11... | collective-permute-start | bytes 393224 | tf_op jit(solution)/shard_map/ppermute | solution.py:423
  41.7 0.0 collective-permute-done.7.halo_1.own_m1
  41.7 1.3 %collective-permute-start.12 = (f32[16,128]{1,0:T(8,128)S(1)}, f32[16,128]{1,0:T(8,128)S(1)}, u32[]{:S(2)}, u32[]{:S(2)}) collective-permute-start(f32[16,128]{1,0:T(8,128)S(1)} %get-tuple-element.67.ends), channel_id=1, source_target_pairs={{0,1},{1,0},{2,3},{3,2},{4,5},{5,4},{6,7},{7,6},{8,9},{9,8},{10,11... | collective-permute-start | bytes 24584 | tf_op jit(solution)/shard_map/ppermute | solution.py:423
  43.0 2.4 %collective-permute-done.8.halo_2.own_m2 = f32[16,2048]{1,0:T(8,128)S(1)} collective-permute-done((f32[16,2048]{1,0:T(8,128)S(1)}, f32[16,2048]{1,0:T(8,128)S(1)}, u32[]{:S(2)}, u32[]{:S(2)}) %collective-permute-start.8) | collective-permute-done | bytes 131104 | tf_op jit(solution)/shard_map/ppermute | solution.py:426
  45.4 1.8 %shard_map.82 = (f32[8,128]{1,0:T(8,128)S(1)}, f32[1,16,2048]{2,1,0:T(8,128)S(1)}) custom-call(s32[4]{0:T(128)S(1)} %pad_add_fusion.place, f32[17]{0:T(128)S(1)} %pad_maximum_fusion.tau, f32[3,8,4096]{2,1,0:T(8,128)S(1)} %get-tuple-element.40.weights.weights_all, f32[8,4096]{1,0:T(8,128)S(1)} %collective-permute-done.row_above, ...), custom_call_target="tpu_custom_call" | custom-call | flops 1 | bytes 1 | tf_op jit(solution)/shard_map/pallas_call | solution.py:26
  47.2 0.0 collective-permute-done.11
  47.2 0.0 collective-permute-done.10
  47.2 1.2 %collective-permute-start.13 = (f32[8,128]{1,0:T(8,128)S(1)}, f32[8,128]{1,0:T(8,128)S(1)}, u32[]{:S(2)}, u32[]{:S(2)}) collective-permute-start(f32[8,128]{1,0:T(8,128)S(1)} %get-tuple-element.71.sums), channel_id=1, source_target_pairs={{0,1},{1,0},{2,3},{3,2},{4,5},{5,4},{6,7},{7,6},{8,9},{9,8},{10,11... | collective-permute-start | bytes 12296 | tf_op jit(solution)/shard_map/ppermute | solution.py:423
  48.4 0.0 collective-permute-done.12.ends_other
  48.4 2.4 %collective-permute-done.13.sums_other = f32[8,128]{1,0:T(8,128)S(1)} collective-permute-done((f32[8,128]{1,0:T(8,128)S(1)}, f32[8,128]{1,0:T(8,128)S(1)}, u32[]{:S(2)}, u32[]{:S(2)}) %collective-permute-start.13) | collective-permute-done | bytes 4128 | tf_op jit(solution)/shard_map/ppermute | solution.py:423
  50.9 0.7 %shard_map.83 = f32[8,128]{1,0:T(8,128)S(1)} custom-call(s32[4]{0:T(128)S(1)} %pad_add_fusion.place, f32[3,8,4096]{2,1,0:T(8,128)S(1)} %get-tuple-element.40.weights.weights_all, f32[16,128]{1,0:T(8,128)S(1)} %get-tuple-element.67.ends, f32[8,128]{1,0:T(8,128)S(1)} %get-tuple-element.71.sums, f32[16,128]{1,0:T(8,128)S(1)} %collective-permute-done.12.ends_other, ...), custom_call_target="tpu_custom_call" | custom-call | flops 1 | bytes 1 | tf_op jit(solution)/shard_map/pallas_call | solution.py:26
  51.6 1.2 %collective-permute-start.18 = (f32[9,8,2048]{2,1,0:T(8,128)S(1)}, f32[9,8,2048]{2,1,0:T(8,128)S(1)}, u32[]{:S(2)}, u32[]{:S(2)}) collective-permute-start(f32[9,8,2048]{2,1,0:T(8,128)S(1)} %bitcast.29), channel_id=1, source_target_pairs={{0,1},{1,0},{2,3},{3,2},{4,5},{5,4},{6,7},{7,6},{8,9},{9,8},{10,11... | collective-permute-start | bytes 1769480 | tf_op jit(solution)/shard_map/ppermute | solution.py:423
  52.8 0.8 %collective-permute-start.19 = (f32[16,2048]{1,0:T(8,128)S(1)}, f32[16,2048]{1,0:T(8,128)S(1)}, u32[]{:S(2)}, u32[]{:S(2)}) collective-permute-start(f32[16,2048]{1,0:T(8,128)S(1)} %bitcast.34), channel_id=1, source_target_pairs={{0,1},{1,0},{2,3},{3,2},{4,5},{5,4},{6,7},{7,6},{8,9},{9,8},{10,11... | collective-permute-start | bytes 393224 | tf_op jit(solution)/shard_map/ppermute | solution.py:423
  53.7 0.0 collective-permute-start.14
  53.7 1.2 %collective-permute-done.14 = f32[8,128]{1,0:T(8,128)S(1)} collective-permute-done((f32[8,128]{1,0:T(8,128)S(1)}, f32[8,128]{1,0:T(8,128)S(1)}, u32[]{:S(2)}, u32[]{:S(2)}) %collective-permute-start.14) | collective-permute-done | bytes 4128 | tf_op jit(solution)/shard_map/ppermute | solution.py:528
  54.9 0.0 collective-permute-start.15
  54.9 3.6 %collective-permute-done.15 = f32[8,128]{1,0:T(8,128)S(1)} collective-permute-done((f32[8,128]{1,0:T(8,128)S(1)}, f32[8,128]{1,0:T(8,128)S(1)}, u32[]{:S(2)}, u32[]{:S(2)}) %collective-permute-start.15) | collective-permute-done | bytes 4128 | tf_op jit(solution)/shard_map/ppermute | solution.py:528
  58.5 0.0 collective-permute-start.16
  58.5 3.6 %collective-permute-done.16 = f32[8,128]{1,0:T(8,128)S(1)} collective-permute-done((f32[8,128]{1,0:T(8,128)S(1)}, f32[8,128]{1,0:T(8,128)S(1)}, u32[]{:S(2)}, u32[]{:S(2)}) %collective-permute-start.16) | collective-permute-done | bytes 4128 | tf_op jit(solution)/shard_map/ppermute | solution.py:528
  62.1 0.8 %collective-permute-start.17 = (f32[8,128]{1,0:T(8,128)S(1)}, f32[8,128]{1,0:T(8,128)S(1)}, u32[]{:S(2)}, u32[]{:S(2)}) collective-permute-start(f32[8,128]{1,0:T(8,128)S(1)} %add.14), channel_id=1, source_target_pairs={{0,16},{2,18},{4,20},{6,22},{8,24},{10,26},{12,28},{14,30},{16,0},... | collective-permute-start | bytes 12296 | tf_op jit(solution)/shard_map/ppermute | solution.py:528
  62.9 3.7 %collective-permute-done.17 = f32[8,128]{1,0:T(8,128)S(1)} collective-permute-done((f32[8,128]{1,0:T(8,128)S(1)}, f32[8,128]{1,0:T(8,128)S(1)}, u32[]{:S(2)}, u32[]{:S(2)}) %collective-permute-start.17) | collective-permute-done | bytes 4128 | tf_op jit(solution)/shard_map/ppermute | solution.py:528
  66.6 3.3 %shard_map.84 = (f32[8,8,4096]{2,1,0:T(8,128)}, f32[8,8,4096]{2,1,0:T(8,128)}) custom-call(s32[4]{0:T(128)S(1)} %pad_add_fusion.place, f32[17]{0:T(128)S(1)} %pad_maximum_fusion.tau, f32[3,8,4096]{2,1,0:T(8,128)S(1)} %get-tuple-element.40.weights.weights_all, f32[8,4096]{1,0:T(8,128)S(1)} %collective-permute-done.row_above, f32[8,128]{1,0:T(8,128)S(1)} %add.15.sums, ...), custom_call_target="tpu_custom_call" | custom-call | flops 1 | bytes 1 | tf_op jit(solution)/shard_map/pallas_call | solution.py:26
  (9 shorter events, 0.0 us)
Async XLA Ops:
  2.6 17.2 %collective-permute-start.1 = (f32[4,8,2048]{2,1,0:T(8,128)S(1)}, f32[4,8,2048]{2,1,0:T(8,128)S(1)}, u32[]{:S(2)}, u32[]{:S(2)}) collective-permute-start(f32[4,8,2048]{2,1,0:T(8,128)S(1)} %bitcast.26), channel_id=1, source_target_pairs={{0,1},{1,0},{2,3},{3,2},{4,5},{5,4},{6,7},{7,6},{8,9},{9,8},{10,11... | collective-permute-start | bytes 786440 | tf_op jit(solution)/shard_map/ppermute | solution.py:423
  7.8 26.0 %copy-start = (f32[15]{0:T(128)S(1)}, f32[15]{0:T(128)}, u32[]{:S(2)}) copy-start(f32[15]{0:T(128)} %param.10) | copy-start | bytes 184
  7.8 12.1 %collective-permute-start.2 = (f32[4,8,2048]{2,1,0:T(8,128)S(1)}, f32[4,8,2048]{2,1,0:T(8,128)S(1)}, u32[]{:S(2)}, u32[]{:S(2)}) collective-permute-start(f32[4,8,2048]{2,1,0:T(8,128)S(1)} %bitcast.33), channel_id=1, source_target_pairs={{0,1},{1,0},{2,3},{3,2},{4,5},{5,4},{6,7},{7,6},{8,9},{9,8},{10,11... | collective-permute-start | bytes 786440 | tf_op jit(solution)/shard_map/ppermute | solution.py:423
  12.7 7.1 %collective-permute-start = (f32[8,4096]{1,0:T(8,128)S(1)}, f32[8,4096]{1,0:T(8,128)S(1)}, u32[]{:S(2)}, u32[]{:S(2)}) collective-permute-start(f32[8,4096]{1,0:T(8,128)S(1)} %get-tuple-element.42), channel_id=1, source_target_pairs={{0,2},{2,4},{4,6},{6,8},{8,10},{10,12},{12,14},{14,16},{16,18},{18... | collective-permute-start | bytes 393224 | tf_op jit(solution)/shard_map/ppermute | solution.py:481
  12.8 21.1 %collective-permute-start.6 = (f32[8,8,2048]{2,1,0:T(8,128)S(1)}, f32[8,8,2048]{2,1,0:T(8,128)S(1)}, u32[]{:S(2)}, u32[]{:S(2)}) collective-permute-start(f32[8,8,2048]{2,1,0:T(8,128)S(1)} %bitcast.30), channel_id=1, source_target_pairs={{0,1},{1,0},{2,3},{3,2},{4,5},{5,4},{6,7},{7,6},{8,9},{9,8},{10,11... | collective-permute-start | bytes 1572872 | tf_op jit(solution)/shard_map/ppermute | solution.py:423
  22.6 6.4 %collective-permute-start.4 = (f32[16,128]{1,0:T(8,128)S(1)}, f32[16,128]{1,0:T(8,128)S(1)}, u32[]{:S(2)}, u32[]{:S(2)}) collective-permute-start(f32[16,128]{1,0:T(8,128)S(1)} %get-tuple-element.51), channel_id=1, source_target_pairs={{0,1},{1,0},{2,3},{3,2},{4,5},{5,4},{6,7},{7,6},{8,9},{9,8},{10,11... | collective-permute-start | bytes 24584 | tf_op jit(solution)/shard_map/ppermute | solution.py:423
  24.7 7.1 %collective-permute-start.5 = (f32[16,2048]{1,0:T(8,128)S(1)}, f32[16,2048]{1,0:T(8,128)S(1)}, u32[]{:S(2)}, u32[]{:S(2)}) collective-permute-start(f32[16,2048]{1,0:T(8,128)S(1)} %get-tuple-element.52), channel_id=1, source_target_pairs={{2,4},{6,8},{10,12},{14,16},{18,20},{22,24},{26,28},{30,0},{4,2},{... | collective-permute-start | bytes 393224 | tf_op jit(solution)/shard_map/ppermute | solution.py:426
  31.8 15.4 %collective-permute-start.10 = (f32[5,8,2048]{2,1,0:T(8,128)S(1)}, f32[5,8,2048]{2,1,0:T(8,128)S(1)}, u32[]{:S(2)}, u32[]{:S(2)}) collective-permute-start(f32[5,8,2048]{2,1,0:T(8,128)S(1)} %bitcast.31), channel_id=1, source_target_pairs={{0,1},{1,0},{2,3},{3,2},{4,5},{5,4},{6,7},{7,6},{8,9},{9,8},{10,11... | collective-permute-start | bytes 983048 | tf_op jit(solution)/shard_map/ppermute | solution.py:423
  31.9 2.0 %collective-permute-start.3 = (f32[16,2048]{1,0:T(8,128)S(1)}, f32[16,2048]{1,0:T(8,128)S(1)}, u32[]{:S(2)}, u32[]{:S(2)}) collective-permute-start(f32[16,2048]{1,0:T(8,128)S(1)} %get-tuple-element.48), channel_id=1, source_target_pairs={{0,2},{2,0},{4,6},{6,4},{8,10},{10,8},{12,14},{14,12},{16,18},{18,... | collective-permute-start | bytes 393224 | tf_op jit(solution)/shard_map/ppermute | solution.py:426
  31.9 15.3 %collective-permute-start.11 = (f32[4,8,2048]{2,1,0:T(8,128)S(1)}, f32[4,8,2048]{2,1,0:T(8,128)S(1)}, u32[]{:S(2)}, u32[]{:S(2)}) collective-permute-start(f32[4,8,2048]{2,1,0:T(8,128)S(1)} %bitcast.32), channel_id=1, source_target_pairs={{0,1},{1,0},{2,3},{3,2},{4,5},{5,4},{6,7},{7,6},{8,9},{9,8},{10,11... | collective-permute-start | bytes 786440 | tf_op jit(solution)/shard_map/ppermute | solution.py:423
  38.0 3.7 %collective-permute-start.7 = (f32[16,2048]{1,0:T(8,128)S(1)}, f32[16,2048]{1,0:T(8,128)S(1)}, u32[]{:S(2)}, u32[]{:S(2)}) collective-permute-start(f32[16,2048]{1,0:T(8,128)S(1)} %get-tuple-element.59), channel_id=1, source_target_pairs={{0,2},{2,0},{4,6},{6,4},{8,10},{10,8},{12,14},{14,12},{16,18},{18,... | collective-permute-start | bytes 393224 | tf_op jit(solution)/shard_map/ppermute | solution.py:426
  38.3 7.1 %collective-permute-start.8 = (f32[16,2048]{1,0:T(8,128)S(1)}, f32[16,2048]{1,0:T(8,128)S(1)}, u32[]{:S(2)}, u32[]{:S(2)}) collective-permute-start(f32[16,2048]{1,0:T(8,128)S(1)} %get-tuple-element.60), channel_id=1, source_target_pairs={{2,4},{6,8},{10,12},{14,16},{18,20},{22,24},{26,28},{30,0},{4,2},{... | collective-permute-start | bytes 393224 | tf_op jit(solution)/shard_map/ppermute | solution.py:426
  40.9 10.6 %collective-permute-start.9 = (f32[16,2048]{1,0:T(8,128)S(1)}, f32[16,2048]{1,0:T(8,128)S(1)}, u32[]{:S(2)}, u32[]{:S(2)}) collective-permute-start(f32[16,2048]{1,0:T(8,128)S(1)} %bitcast.35), channel_id=1, source_target_pairs={{0,1},{1,0},{2,3},{3,2},{4,5},{5,4},{6,7},{7,6},{8,9},{9,8},{10,11... | collective-permute-start | bytes 393224 | tf_op jit(solution)/shard_map/ppermute | solution.py:423
  41.7 6.7 %collective-permute-start.12 = (f32[16,128]{1,0:T(8,128)S(1)}, f32[16,128]{1,0:T(8,128)S(1)}, u32[]{:S(2)}, u32[]{:S(2)}) collective-permute-start(f32[16,128]{1,0:T(8,128)S(1)} %get-tuple-element.67.ends), channel_id=1, source_target_pairs={{0,1},{1,0},{2,3},{3,2},{4,5},{5,4},{6,7},{7,6},{8,9},{9,8},{10,11... | collective-permute-start | bytes 24584 | tf_op jit(solution)/shard_map/ppermute | solution.py:423
  47.2 3.7 %collective-permute-start.13 = (f32[8,128]{1,0:T(8,128)S(1)}, f32[8,128]{1,0:T(8,128)S(1)}, u32[]{:S(2)}, u32[]{:S(2)}) collective-permute-start(f32[8,128]{1,0:T(8,128)S(1)} %get-tuple-element.71.sums), channel_id=1, source_target_pairs={{0,1},{1,0},{2,3},{3,2},{4,5},{5,4},{6,7},{7,6},{8,9},{9,8},{10,11... | collective-permute-start | bytes 12296 | tf_op jit(solution)/shard_map/ppermute | solution.py:423
  51.6 15.0 %collective-permute-start.18 = (f32[9,8,2048]{2,1,0:T(8,128)S(1)}, f32[9,8,2048]{2,1,0:T(8,128)S(1)}, u32[]{:S(2)}, u32[]{:S(2)}) collective-permute-start(f32[9,8,2048]{2,1,0:T(8,128)S(1)} %bitcast.29), channel_id=1, source_target_pairs={{0,1},{1,0},{2,3},{3,2},{4,5},{5,4},{6,7},{7,6},{8,9},{9,8},{10,11... | collective-permute-start | bytes 1769480 | tf_op jit(solution)/shard_map/ppermute | solution.py:423
  52.8 13.8 %collective-permute-start.19 = (f32[16,2048]{1,0:T(8,128)S(1)}, f32[16,2048]{1,0:T(8,128)S(1)}, u32[]{:S(2)}, u32[]{:S(2)}) collective-permute-start(f32[16,2048]{1,0:T(8,128)S(1)} %bitcast.34), channel_id=1, source_target_pairs={{0,1},{1,0},{2,3},{3,2},{4,5},{5,4},{6,7},{7,6},{8,9},{9,8},{10,11... | collective-permute-start | bytes 393224 | tf_op jit(solution)/shard_map/ppermute | solution.py:423
  53.7 1.2 %collective-permute-start.14 = (f32[8,128]{1,0:T(8,128)S(1)}, f32[8,128]{1,0:T(8,128)S(1)}, u32[]{:S(2)}, u32[]{:S(2)}) collective-permute-start(f32[8,128]{1,0:T(8,128)S(1)} %shard_map.83), channel_id=1, source_target_pairs={{0,2},{2,0},{4,6},{6,4},{8,10},{10,8},{12,14},{14,12},{16,18},{18,... | collective-permute-start | bytes 12296 | tf_op jit(solution)/shard_map/ppermute | solution.py:528
  54.9 3.6 %collective-permute-start.15 = (f32[8,128]{1,0:T(8,128)S(1)}, f32[8,128]{1,0:T(8,128)S(1)}, u32[]{:S(2)}, u32[]{:S(2)}) collective-permute-start(f32[8,128]{1,0:T(8,128)S(1)} %add.12), channel_id=1, source_target_pairs={{0,4},{2,6},{4,0},{6,2},{8,12},{10,14},{12,8},{14,10},{16,20},{18,... | collective-permute-start | bytes 12296 | tf_op jit(solution)/shard_map/ppermute | solution.py:528
  58.5 3.6 %collective-permute-start.16 = (f32[8,128]{1,0:T(8,128)S(1)}, f32[8,128]{1,0:T(8,128)S(1)}, u32[]{:S(2)}, u32[]{:S(2)}) collective-permute-start(f32[8,128]{1,0:T(8,128)S(1)} %add.13), channel_id=1, source_target_pairs={{0,8},{2,10},{4,12},{6,14},{8,0},{10,2},{12,4},{14,6},{16,24},{18,... | collective-permute-start | bytes 12296 | tf_op jit(solution)/shard_map/ppermute | solution.py:528
  62.1 4.5 %collective-permute-start.17 = (f32[8,128]{1,0:T(8,128)S(1)}, f32[8,128]{1,0:T(8,128)S(1)}, u32[]{:S(2)}, u32[]{:S(2)}) collective-permute-start(f32[8,128]{1,0:T(8,128)S(1)} %add.14), channel_id=1, source_target_pairs={{0,16},{2,18},{4,20},{6,22},{8,24},{10,26},{12,28},{14,30},{16,0},... | collective-permute-start | bytes 12296 | tf_op jit(solution)/shard_map/ppermute | solution.py:528

commit v4 on v3

--- a/solution.py
+++ b/solution.py
@@ -137,14 +137,14 @@
             base = base + part.shape[1]
 
 
-def send_kernel(blocks, spans, place, mask, precision, observed, *refs):
+def send_kernel(blocks, spans, mask, precision, observed, *refs):
     outputs = refs[: len(spans)]
     masks, precisions, observations, arrived = refs[len(spans) :]
     width = masks.shape[3]
     first = min(start for _, start, _ in spans)
     last = max(stop for _, _, stop in spans)
     for k in range(1, blocks):
-        there = columns(lax.rem(place[0] + k, blocks), width)
+        there = columns(lax.rem(lax.axis_index("dates") + k, blocks), width)
 
         def copies(j):
             sources = [(mask, masks), (precision, precisions)]
@@ -215,8 +215,8 @@
             forwarded[k - 1, dates_here + j : dates_here + j + 1, :] = halo_2[date, :]
 
 
-def first_kernel(blocks, place, rhs_here, early, late, inverse, precond, first, second, ends, early_windows, late_windows, dot, rhs):
-    date_block, parity = place[0], place[1]
+def first_kernel(blocks, rhs_here, early, late, inverse, precond, first, second, ends, early_windows, late_windows, dot, rhs):
+    date_block, parity = lax.axis_index("dates"), lax.rem(lax.axis_index("rows"), 2)
     dates_here = rhs_here.shape[0]
     here = columns(date_block, rhs.shape[2])
     gather_dates(rhs, lambda j: rhs_here[j, :, here], (early, late), date_block, blocks, dates_here)
@@ -229,25 +229,25 @@
     send_windows(precond, (early_windows, late_windows), date_block, blocks, dates_here)
 
 
-def edge_weights(place, weights_all, above, lanes):
+def edge_weights(weights_all, above, lanes):
     across, across_prev, downward = [weights_all[k, :, lanes] for k in range(3)]
     width = across.shape[1]
     rows = row_ids(width)
-    downward = jnp.where((rows == 7) & (place[3] == 1), 0.0, downward)
-    row_above = jnp.where(place[2] == 0, 0.0, above[0:1, lanes])
+    downward = jnp.where((rows == 7) & (lax.axis_index("rows") == lax.axis_size("rows") - 1), 0.0, downward)
+    row_above = jnp.where(lax.axis_index("rows") == 0, 0.0, above[0:1, lanes])
     downward_prev = jnp.where(rows == 0, row_above, pltpu.roll(downward, 1, 0))
     weights = (across, across_prev, downward, downward_prev)
     return weights, MASS + across + across_prev + downward + downward_prev
 
 
-def pixel_image(place, tau, weights_all, row_above, field, halo_1, halo_2, ends_left, ends_right, data_weight, use):
-    date_block, parity = place[0], place[1]
+def pixel_image(tau, weights_all, row_above, field, halo_1, halo_2, ends_left, ends_right, data_weight, use):
+    date_block, parity = lax.axis_index("dates"), lax.rem(lax.axis_index("rows"), 2)
     dates, _, width = field.shape
     here = columns(date_block, width)
-    weights, weight_sum = edge_weights(place, weights_all, row_above, here)
+    weights, weight_sum = edge_weights(weights_all, row_above, here)
     for t in range(dates):
         above, below = halo_rows(halo_1[t : t + 1, :], halo_2[t : t + 1, :], parity)
-        tau_up, tau_down = tau[t + 1], tau[t]
+        tau_up, tau_down = spread(tau, t + 1, width), spread(tau, t, width)
         value = field[t]
         diagonal = weight_sum + data_weight[t] + (tau_up + tau_down)
         image = stencil(
@@ -266,6 +266,10 @@
         use(t, value, image)
 
 
+def spread(tau, index, width):
+    return jnp.tile(jnp.broadcast_to(tau[pl.ds(index, 1), :], (8, LANES)), (1, width // LANES))
+
+
 def fold(value):
     total = value[:, :LANES]
     for index in range(1, value.shape[1] // LANES):
@@ -274,10 +278,10 @@
 
 
 def second_kernel(
-    blocks, place, tau, weights, row_above, precond, halo_1, halo_2, ends_left, ends_right, weight_here, received, inverse,
+    blocks, tau, weights, row_above, precond, halo_1, halo_2, ends_left, ends_right, weight_here, received, inverse,
     mapped, first, second, ends, windows, forwarded, data_weight, dot_image, dot_mapped, image_all, total,
 ):
-    date_block, parity = place[0], place[1]
+    date_block, parity = lax.axis_index("dates"), lax.rem(lax.axis_index("rows"), 2)
     dates_here = weight_here.shape[0]
     here = columns(date_block, precond.shape[2])
     gather_dates(data_weight, lambda j: weight_here[j, :, here], (received,), date_block, blocks, dates_here)
@@ -287,7 +291,7 @@
         image_all[t] = image
         total[...] = total[...] + fold(value * image)
 
-    pixel_image(place, tau, weights, row_above, precond, halo_1, halo_2, ends_left, ends_right, data_weight, use)
+    pixel_image(tau, weights, row_above, precond, halo_1, halo_2, ends_left, ends_right, data_weight, use)
     dot_image[...] = total[...]
 
     def store(t, lanes, value):
@@ -300,7 +304,7 @@
 
 
 def third_kernel(
-    blocks, place, tau, weights, row_above, mapped, halo_1, halo_2, data_weight, dot_1, dot_2, dot_3, *refs,
+    blocks, tau, weights, row_above, mapped, halo_1, halo_2, data_weight, dot_1, dot_2, dot_3, *refs,
 ):
     *ends, sums, forwarded, total = refs
     left, right = ends or (None, None)
@@ -309,28 +313,28 @@
     def use(t, value, image):
         total[...] = total[...] + fold(value * image)
 
-    pixel_image(place, tau, weights, row_above, mapped, halo_1, halo_2, left, right, data_weight, use)
+    pixel_image(tau, weights, row_above, mapped, halo_1, halo_2, left, right, data_weight, use)
     rows = row_ids(LANES)
     result = jnp.zeros((8, LANES), jnp.float32)
     for index, dot in enumerate((dot_1, dot_2, dot_3, total)):
         result = jnp.where(rows == index, jnp.sum(dot[...]), result)
     sums[...] = result
-    forward_halos(halo_1, halo_2, forwarded, place[0], blocks)
-
-
-def join_kernel(place, weights, ends, sums, ends_other, sums_other, joined):
+    forward_halos(halo_1, halo_2, forwarded, lax.axis_index("dates"), blocks)
+
+
+def join_kernel(weights, ends, sums, ends_other, sums_other, joined):
     width = weights.shape[2] // 2
     boundary = weights[0, :, width - LANES : width][:, LANES - 1 : LANES]
-    dates = jnp.where(place[0] == 0, ends[8:16, :] * ends_other[0:8, :], ends[0:8, :] * ends_other[8:16, :])
+    dates = jnp.where(lax.axis_index("dates") == 0, ends[8:16, :] * ends_other[0:8, :], ends[0:8, :] * ends_other[8:16, :])
     crossing = -2.0 * jnp.sum(boundary * dates)
     joined[...] = sums[...] + sums_other[...] + jnp.where(row_ids(LANES) == 3, crossing, 0.0)
 
 
 def last_kernel(
-    blocks, place, tau, weights_all, row_above, sums, precond, mapped, precond_early, precond_late, mapped_other, own_p1, own_p2, own_m1, own_m2,
+    blocks, tau, weights_all, row_above, sums, precond, mapped, precond_early, precond_late, mapped_other, own_p1, own_p2, own_m1, own_m2,
     precond_halos, mapped_halos, weight_here, rhs, solution, residual, field, above_all, below_all, remainder, sent,
 ):
-    date_block, parity = place[0], place[1]
+    date_block, parity = lax.axis_index("dates"), lax.rem(lax.axis_index("rows"), 2)
     dates, _, width = precond.shape
     dates_here, _, all_columns = rhs.shape
     length = field.shape[0]
@@ -354,32 +358,36 @@
     here = columns(date_block, width)
     for j in range(length):
         field[j, :, here] = mix(precond[start + j], mapped[start + j])
-    for j in range(dates_here):
-        date = pl.ds(date_block * dates_here + j, 1)
-        above, below = halo_rows(mix(own_p1[date, :], own_m1[date, :]), mix(own_p2[date, :], own_m2[date, :]), parity)
-        above_all[j : j + 1, here] = above
-        below_all[j : j + 1, here] = below
+    first_date = date_block * dates_here
+
+    def own(rows):
+        if dates_here % 8 == 0:
+            return rows[pl.ds(pl.multiple_of(first_date, 8), dates_here), :]
+        return jnp.concatenate([rows[pl.ds(first_date + j, 1), :] for j in range(dates_here)], axis=0)
+
+    above, below = halo_rows(mix(own(own_p1), own(own_m1)), mix(own(own_p2), own(own_m2)), parity)
+    above_all[:, here] = above
+    below_all[:, here] = below
     for k in range(1, blocks):
         there = columns(lax.rem(date_block + blocks - k, blocks), width)
         for j in range(length):
             count = precond_early.shape[1]
             other = precond_early[k - 1, j] if j < count else precond_late[k - 1, j - count]
             field[j, :, there] = mix(other, mapped_other[k - 1, j])
-        for j in range(dates_here):
-            one, two = slice(j, j + 1), slice(dates_here + j, dates_here + j + 1)
-            above, below = halo_rows(
-                mix(precond_halos[k - 1, one, :], mapped_halos[k - 1, one, :]),
-                mix(precond_halos[k - 1, two, :], mapped_halos[k - 1, two, :]),
-                parity,
-            )
-            above_all[j : j + 1, there] = above
-            below_all[j : j + 1, there] = below
+        above, below = halo_rows(
+            mix(precond_halos[k - 1, :dates_here, :], mapped_halos[k - 1, :dates_here, :]),
+            mix(precond_halos[k - 1, dates_here:, :], mapped_halos[k - 1, dates_here:, :]),
+            parity,
+        )
+        above_all[:, there] = above
+        below_all[:, there] = below
     copies = [pltpu.make_async_copy(field.at[offset + j], solution.at[j], sent.at[0, j]) for j in range(dates_here)]
     for copy in copies:
         copy.start()
-    weights, weight_sum = edge_weights(place, weights_all, row_above, slice(None))
+    weights, weight_sum = edge_weights(weights_all, row_above, slice(None))
     for j in range(dates_here):
-        tau_up, tau_down = tau[date_block * dates_here + j + 1], tau[date_block * dates_here + j]
+        date = date_block * dates_here + j
+        tau_up, tau_down = spread(tau, date + 1, all_columns), spread(tau, date, all_columns)
         data_weight = weight_here[j]
         place_j = offset + j
         value = field[place_j]
@@ -409,11 +417,6 @@
     dates = inverse.shape[0]
     width = all_columns // blocks
     length = min(dates_here + (1 if blocks == 2 else 2), dates)
-    line_block = lax.axis_index("rows")
-    date_block = lax.axis_index("dates")
-    parity = lax.rem(line_block, 2)
-    at_end = (line_block == slabs - 1).astype(jnp.int32)
-    place = jnp.stack([date_block, parity, line_block, at_end]).astype(jnp.int32)
 
     pairs = [(i, i ^ 1) for i in range(slabs)]
     across_pairs = [(i, (i + 1) % slabs) for i in range(1, slabs, 2)]
@@ -452,7 +455,7 @@
             functools.partial(send_kernel, blocks, spans),
             [(blocks - 1, stop - start, lines, width) for _, start, stop in spans],
             [(part, jnp.int32), part, part, pltpu.SemaphoreType.DMA((blocks - 1, dates_here, 3))],
-            [place],
+            [],
             [obs_mask, precision, observed],
             HBM,
         )
@@ -477,18 +480,19 @@
     )
     zero_one = jnp.zeros((1,), jnp.float32)
     tau = jnp.concatenate([zero_one, temporal_weight, zero_one])
+    tau = jnp.broadcast_to(tau[:, None], (dates + 1, LANES))
 
     row_above = lax.ppermute(last_row, "rows", [(i, (i + 1) % slabs) for i in range(slabs)])
-    rhs_here, row_above = lax.optimization_barrier((rhs_here, row_above))
     early_shape = (blocks - 1, (length + 1) // 2, lines, width)
     late_shape = (blocks - 1, length // 2, lines, width)
     precond, p_first, p_second, p_ends, p_early, p_late, dot_1 = call(
         functools.partial(first_kernel, blocks),
         [pixel, rows, rows, ends_shape, early_shape, late_shape, vector],
         [pixel],
-        [place],
+        [],
         [rhs_here, rhs_other, rhs_late, staged],
     )
+    p_second, row_above = lax.optimization_barrier((p_second, row_above))
     p_halo_1, p_halo_2 = swap_rows(p_first, p_second)
     p_left, p_right = swap_ends(p_ends)
     p_early, p_late, p_left, p_halo_2 = lax.optimization_barrier((p_early, p_late, p_left, p_halo_2))
@@ -498,8 +502,8 @@
         functools.partial(second_kernel, blocks),
         [pixel, rows, rows, ends_shape, window_shape, edges_shape, pixel, vector, vector],
         [pixel, vector],
-        [place, tau],
-        [weights, row_above, precond, p_halo_1, p_halo_2, p_left, p_right, weight_here, weight_other, staged],
+        [],
+        [tau, weights, row_above, precond, p_halo_1, p_halo_2, p_left, p_right, weight_here, weight_other, staged],
     )
     m_halo_1, m_halo_2 = swap_rows(m_first, m_second)
     m_ends_other = () if blocks == 2 else swap_ends(m_ends)
@@ -507,14 +511,14 @@
         functools.partial(third_kernel, blocks),
         [vector, edges_shape],
         [vector],
-        [place, tau],
-        [weights, row_above, mapped, m_halo_1, m_halo_2, data_weight, dot_1, dot_2, dot_3, *m_ends_other],
+        [],
+        [tau, weights, row_above, mapped, m_halo_1, m_halo_2, data_weight, dot_1, dot_2, dot_3, *m_ends_other],
     )
     precond_halos = send(p_forward)
     sums, precond_early, precond_late = lax.optimization_barrier((sums, precond_early, precond_late))
     if blocks == 2:
         ends_other, sums_other = rotate(m_ends, 1), rotate(sums, 1)
-        (sums,) = call(join_kernel, [vector], [], [place], [weights, m_ends, sums, ends_other, sums_other])
+        (sums,) = call(join_kernel, [vector], [], [], [weights, m_ends, sums, ends_other, sums_other])
     else:
         steps = 1
         while steps < blocks:
@@ -535,9 +539,9 @@
                 (length, lines, all_columns), (dates_here, all_columns), (dates_here, all_columns), block,
                 pltpu.SemaphoreType.DMA((2, dates_here)),
             ],
-            [place, tau],
+            [],
             [
-                weights, row_above, sums, precond, mapped, precond_early, precond_late, mapped_other, p_halo_1, p_halo_2, m_halo_1, m_halo_2,
+                tau, weights, row_above, sums, precond, mapped, precond_early, precond_late, mapped_other, p_halo_1, p_halo_2, m_halo_1, m_halo_2,
                 precond_halos, mapped_halos, weight_here, rhs_here,
             ],
             out_space=HBM,

time: 70.1 us -> 65.9 us (0.940)
  starting transfers between devices: 18.8 us -> 27.2 us
  waiting for transfers between devices: 28.7 us -> 20.5 us
  Pallas kernels: 21.5 us -> 17.1 us
    ppermute x11, waiting for transfers between devices: 6.45 us -> 11.6 us  [rotate(): lax.ppermute(value, 'dates', [(i, (i + k) % blocks) for i in range(blocks)])]
    ppermute x1, waiting for transfers between devices: 5.01 us -> 0.01 us  [body(): lax.ppermute(last_row, 'rows', [(i, (i + 1) % slabs) for i in range(slabs)])]
    ppermute x4, waiting for transfers between devices: 12.1 us -> 7.29 us  [body(): lax.ppermute(sums, 'rows', [(i, i ^ steps) for i in range(slabs)])]
    ppermute x4, starting transfers between devices: 0.83 us -> 5.6 us  [body(): lax.ppermute(sums, 'rows', [(i, i ^ steps) for i in range(slabs)])]
    pallas_call x8, Pallas kernels: 21.5 us -> 17.1 us  [call(): pl.pallas_call(kernel, out_shape=[jax.ShapeDtypeStruct(*typed(entry)) for...]
    ppermute x2, waiting for transfers between devices: 5.17 us -> 1.23 us  [swap_rows(): lax.ppermute(second, 'rows', across_pairs)]
    ppermute x2, starting transfers between devices: 2.97 us -> 6.43 us  [swap_rows(): lax.ppermute(second, 'rows', across_pairs)]
  transfers between devices with their start and end apart: 20 -> 20, of which waited for: 9 -> 11; matrix products, arithmetic and copies ran while one was open for 0% -> 0% of each run, Pallas kernels for 23% -> 21%
where the time goes in v4:
time: 65.9 us; the launch traced here: 65.6 us
  starting transfers between devices  27.2 us (41%)
  waiting for transfers between devices  20.5 us (31%)
  Pallas kernels  17.1 us (26%)
  between operations  0.73 us (1%)
    pallas_call x8, Pallas kernels, call(): pl.pallas_call(kernel, out_shape=[jax.ShapeDtypeStruct(*typed(entry)) for...  17.1 us
    ppermute x11, starting transfers between devices, rotate(): lax.ppermute(value, 'dates', [(i, (i + k) % blocks) for i in range(blocks)])  14.9 us
    ppermute x11, waiting for transfers between devices, rotate(): lax.ppermute(value, 'dates', [(i, (i + k) % blocks) for i in range(blocks)])  11.6 us
    ppermute x4, waiting for transfers between devices, body(): lax.ppermute(sums, 'rows', [(i, i ^ steps) for i in range(slabs)])  7.29 us
    ppermute x2, starting transfers between devices, swap_rows(): lax.ppermute(second, 'rows', across_pairs)  6.43 us
    ppermute x4, starting transfers between devices, body(): lax.ppermute(sums, 'rows', [(i, i ^ steps) for i in range(slabs)])  5.6 us
  transfers between devices with their start and end apart: 20, of which 11 were waited for; matrix products, arithmetic and copies ran while one was open for 0% of the time, Pallas kernels for 21%

profile of v4, /device:TPU:0, one launch (start us, length us, event | category | flops | bytes accessed | tf_op | source)
XLA Modules:
  0.0 65.6 jit_solution(9992437702690443818)
XLA Ops:
  0.6 1.4 %shard_map.78 = f32[1,4,8,2048]{3,2,1,0:T(8,128)S(1)} custom-call(s32[8,8,4096]{2,1,0:T(8,128)} %mask.5, f32[8,8,4096]{2,1,0:T(8,128)} %precision.5, f32[8,8,4096]{2,1,0:T(8,128)} %observed.5), custom_call_target="tpu_custom_call" | custom-call | flops 1 | bytes 1 | tf_op jit(solution)/shard_map/pallas_call | solution.py:26
  2.0 3.0 %collective-permute-start = (f32[4,8,2048]{2,1,0:T(8,128)S(1)}, f32[4,8,2048]{2,1,0:T(8,128)S(1)}, u32[]{:S(2)}, u32[]{:S(2)}) collective-permute-start(f32[4,8,2048]{2,1,0:T(8,128)S(1)} %bitcast.22), channel_id=1, source_target_pairs={{0,1},{1,0},{2,3},{3,2},{4,5},{5,4},{6,7},{7,6},{8,9},{9,8},{10,11... | collective-permute-start | bytes 786440 | tf_op jit(solution)/shard_map/ppermute | solution.py:426
  5.1 1.5 %shard_map.79 = (f32[1,4,8,2048]{3,2,1,0:T(8,128)S(1)}, f32[1,8,8,2048]{3,2,1,0:T(8,128)S(1)}) custom-call(s32[8,8,4096]{2,1,0:T(8,128)} %mask.5, f32[8,8,4096]{2,1,0:T(8,128)} %precision.5, f32[8,8,4096]{2,1,0:T(8,128)} %observed.5), custom_call_target="tpu_custom_call" | custom-call | flops 1 | bytes 1 | tf_op jit(solution)/shard_map/pallas_call | solution.py:26
  6.6 0.0 copy-start
  6.6 0.1 collective-permute-start.1
  6.7 4.8 %shard_map.77 = (bf16[16,16,8,2048]{3,2,1,0:T(8,128)(2,1)S(1)}, f32[8,8,4096]{2,1,0:T(8,128)S(1)}, f32[8,8,4096]{2,1,0:T(8,128)S(1)}, f32[3,8,4096]{2,1,0:T(8,128)S(1)}, f32[8,4096]{1,0:T(8,128)S(1)}) custom-call(s32[8,8,4096]{2,1,0:T(8,128)} %mask.5, f32[8,8,4096]{2,1,0:T(8,128)} %precision.5, f32[8,8,4096]{2,1,0:T(8,128)} %observed.5, ...), custom_call_target="tpu_custom_call" | custom-call | flops 1 | bytes 1 | tf_op jit(solution)/shard_map/pallas_call | solution.py:26
  11.5 0.1 collective-permute-start.2
  11.6 2.1 %collective-permute-start.6 = (f32[8,8,2048]{2,1,0:T(8,128)S(1)}, f32[8,8,2048]{2,1,0:T(8,128)S(1)}, u32[]{:S(2)}, u32[]{:S(2)}) collective-permute-start(f32[8,8,2048]{2,1,0:T(8,128)S(1)} %bitcast.26), channel_id=1, source_target_pairs={{0,1},{1,0},{2,3},{3,2},{4,5},{5,4},{6,7},{7,6},{8,9},{9,8},{10,11... | collective-permute-start | bytes 1572872 | tf_op jit(solution)/shard_map/ppermute | solution.py:426
  13.6 0.0 collective-permute-done
  13.7 4.0 %collective-permute-done.1 = f32[4,8,2048]{2,1,0:T(8,128)S(1)} collective-permute-done((f32[4,8,2048]{2,1,0:T(8,128)S(1)}, f32[4,8,2048]{2,1,0:T(8,128)S(1)}, u32[]{:S(2)}, u32[]{:S(2)}) %collective-permute-start.1) | collective-permute-done | bytes 262176 | tf_op jit(solution)/shard_map/ppermute | solution.py:426
  17.6 2.2 %shard_map.80 = (f32[16,8,2048]{2,1,0:T(8,128)S(1)}, f32[16,2048]{1,0:T(8,128)S(1)}, f32[16,2048]{1,0:T(8,128)S(1)}, f32[16,128]{1,0:T(8,128)S(1)}, f32[1,5,8,20...) custom-call(f32[8,8,4096]{2,1,0:T(8,128)S(1)} %get-tuple-element.41.rhs_here.rhs, ...), custom_call_target="tpu_custom_call" | custom-call | flops 1 | bytes 1 | tf_op jit(solution)/shard_map/pallas_call | solution.py:26
  19.9 2.0 %collective-permute-start.4 = (f32[16,128]{1,0:T(8,128)S(1)}, f32[16,128]{1,0:T(8,128)S(1)}, u32[]{:S(2)}, u32[]{:S(2)}) collective-permute-start(f32[16,128]{1,0:T(8,128)S(1)} %get-tuple-element.51), channel_id=1, source_target_pairs={{0,1},{1,0},{2,3},{3,2},{4,5},{5,4},{6,7},{7,6},{8,9},{9,8},{10,11... | collective-permute-start | bytes 24584 | tf_op jit(solution)/shard_map/ppermute | solution.py:426
  21.9 0.0 collective-permute-done.2.row_above
  21.9 1.9 %collective-permute-start.5 = (f32[16,2048]{1,0:T(8,128)S(1)}, f32[16,2048]{1,0:T(8,128)S(1)}, u32[]{:S(2)}, u32[]{:S(2)}) collective-permute-start(f32[16,2048]{1,0:T(8,128)S(1)} %get-tuple-element.52), channel_id=1, source_target_pairs={{2,4},{6,8},{10,12},{14,16},{18,20},{22,24},{26,28},{30,0},{4,2},{... | collective-permute-start | bytes 393224 | tf_op jit(solution)/shard_map/ppermute | solution.py:429
  23.9 4.5 %collective-permute-done.4 = f32[16,128]{1,0:T(8,128)S(1)} collective-permute-done((f32[16,128]{1,0:T(8,128)S(1)}, f32[16,128]{1,0:T(8,128)S(1)}, u32[]{:S(2)}, u32[]{:S(2)}) %collective-permute-start.4) | collective-permute-done | bytes 8224 | tf_op jit(solution)/shard_map/ppermute | solution.py:426
  28.4 0.6 collective-permute-done.5.halo_2.own_p2
  29.0 1.1 %collective-permute-start.10 = (f32[5,8,2048]{2,1,0:T(8,128)S(1)}, f32[5,8,2048]{2,1,0:T(8,128)S(1)}, u32[]{:S(2)}, u32[]{:S(2)}) collective-permute-start(f32[5,8,2048]{2,1,0:T(8,128)S(1)} %bitcast.27), channel_id=1, source_target_pairs={{0,1},{1,0},{2,3},{3,2},{4,5},{5,4},{6,7},{7,6},{8,9},{9,8},{10,11... | collective-permute-start | bytes 983048 | tf_op jit(solution)/shard_map/ppermute | solution.py:426
  30.1 0.0 collective-permute-start.3
  30.1 0.9 %collective-permute-start.11 = (f32[4,8,2048]{2,1,0:T(8,128)S(1)}, f32[4,8,2048]{2,1,0:T(8,128)S(1)}, u32[]{:S(2)}, u32[]{:S(2)}) collective-permute-start(f32[4,8,2048]{2,1,0:T(8,128)S(1)} %bitcast.28), channel_id=1, source_target_pairs={{0,1},{1,0},{2,3},{3,2},{4,5},{5,4},{6,7},{7,6},{8,9},{9,8},{10,11... | collective-permute-start | bytes 786440 | tf_op jit(solution)/shard_map/ppermute | solution.py:426
  31.0 0.1 pad_maximum_fusion
  31.1 0.4 collective-permute-done.3.halo_1.own_p1
  31.5 0.0 collective-permute-done.6
  31.5 0.1 broadcast_in_dim.2.tau
  31.6 3.4 %shard_map.81 = (f32[16,8,2048]{2,1,0:T(8,128)S(1)}, f32[16,2048]{1,0:T(8,128)S(1)}, f32[16,2048]{1,0:T(8,128)S(1)}, f32[16,128]{1,0:T(8,128)S(1)}, f32[1,9,8,20...) custom-call(f32[17,128]{1,0:T(8,128)S(1)} %broadcast_in_dim.2.tau, ...), custom_call_target="tpu_custom_call" | custom-call | flops 1 | bytes 1 | tf_op jit(solution)/shard_map/pallas_call | solution.py:26
  35.0 0.2 collective-permute-start.7
  35.2 4.5 %collective-permute-start.8 = (f32[16,2048]{1,0:T(8,128)S(1)}, f32[16,2048]{1,0:T(8,128)S(1)}, u32[]{:S(2)}, u32[]{:S(2)}) collective-permute-start(f32[16,2048]{1,0:T(8,128)S(1)} %get-tuple-element.60), channel_id=1, source_target_pairs={{2,4},{6,8},{10,12},{14,16},{18,20},{22,24},{26,28},{30,0},{4,2},{... | collective-permute-start | bytes 393224 | tf_op jit(solution)/shard_map/ppermute | solution.py:429
  39.7 0.8 %collective-permute-start.9 = (f32[16,2048]{1,0:T(8,128)S(1)}, f32[16,2048]{1,0:T(8,128)S(1)}, u32[]{:S(2)}, u32[]{:S(2)}) collective-permute-start(f32[16,2048]{1,0:T(8,128)S(1)} %bitcast.31), channel_id=1, source_target_pairs={{0,1},{1,0},{2,3},{3,2},{4,5},{5,4},{6,7},{7,6},{8,9},{9,8},{10,11... | collective-permute-start | bytes 393224 | tf_op jit(solution)/shard_map/ppermute | solution.py:426
  40.4 0.0 collective-permute-done.7.halo_1.own_m1
  40.5 1.3 %collective-permute-start.12 = (f32[16,128]{1,0:T(8,128)S(1)}, f32[16,128]{1,0:T(8,128)S(1)}, u32[]{:S(2)}, u32[]{:S(2)}) collective-permute-start(f32[16,128]{1,0:T(8,128)S(1)} %get-tuple-element.67.ends), channel_id=1, source_target_pairs={{0,1},{1,0},{2,3},{3,2},{4,5},{5,4},{6,7},{7,6},{8,9},{9,8},{10,11... | collective-permute-start | bytes 24584 | tf_op jit(solution)/shard_map/ppermute | solution.py:426
  41.7 0.6 collective-permute-done.8.halo_2.own_m2
  42.3 1.4 %shard_map.82 = (f32[8,128]{1,0:T(8,128)S(1)}, f32[1,16,2048]{2,1,0:T(8,128)S(1)}) custom-call(f32[17,128]{1,0:T(8,128)S(1)} %broadcast_in_dim.2.tau, f32[3,8,4096]{2,1,0:T(8,128)S(1)} %get-tuple-element.40.weights.weights_all, f32[8,4096]{1,0:T(8,128)S(1)} %collective-permute-done.2.row_above, f32[16,8,2048]{2,1,0:T(8,128)S(1)} %get-tuple-element.58.mapped, ...), custom_call_target="tpu_custom_call" | custom-call | flops 1 | bytes 1 | tf_op jit(solution)/shard_map/pallas_call | solution.py:26
  43.7 0.9 %collective-permute-done.11 = f32[4,8,2048]{2,1,0:T(8,128)S(1)} collective-permute-done((f32[4,8,2048]{2,1,0:T(8,128)S(1)}, f32[4,8,2048]{2,1,0:T(8,128)S(1)}, u32[]{:S(2)}, u32[]{:S(2)}) %collective-permute-start.11) | collective-permute-done | bytes 262176 | tf_op jit(solution)/shard_map/ppermute | solution.py:426
  44.6 0.0 collective-permute-done.10
  44.6 1.5 %collective-permute-start.13 = (f32[8,128]{1,0:T(8,128)S(1)}, f32[8,128]{1,0:T(8,128)S(1)}, u32[]{:S(2)}, u32[]{:S(2)}) collective-permute-start(f32[8,128]{1,0:T(8,128)S(1)} %get-tuple-element.71.sums), channel_id=1, source_target_pairs={{0,1},{1,0},{2,3},{3,2},{4,5},{5,4},{6,7},{7,6},{8,9},{9,8},{10,11... | collective-permute-start | bytes 12296 | tf_op jit(solution)/shard_map/ppermute | solution.py:426
  46.1 0.0 collective-permute-done.12.ends_other
  46.1 2.1 %collective-permute-done.13.sums_other = f32[8,128]{1,0:T(8,128)S(1)} collective-permute-done((f32[8,128]{1,0:T(8,128)S(1)}, f32[8,128]{1,0:T(8,128)S(1)}, u32[]{:S(2)}, u32[]{:S(2)}) %collective-permute-start.13) | collective-permute-done | bytes 4128 | tf_op jit(solution)/shard_map/ppermute | solution.py:426
  48.2 0.2 shard_map.83
  48.4 1.6 %collective-permute-start.18 = (f32[9,8,2048]{2,1,0:T(8,128)S(1)}, f32[9,8,2048]{2,1,0:T(8,128)S(1)}, u32[]{:S(2)}, u32[]{:S(2)}) collective-permute-start(f32[9,8,2048]{2,1,0:T(8,128)S(1)} %bitcast.25), channel_id=1, source_target_pairs={{0,1},{1,0},{2,3},{3,2},{4,5},{5,4},{6,7},{7,6},{8,9},{9,8},{10,11... | collective-permute-start | bytes 1769480 | tf_op jit(solution)/shard_map/ppermute | solution.py:426
  50.0 0.5 collective-permute-start.19
  50.5 0.0 collective-permute-start.14
  50.5 1.2 %collective-permute-done.14 = f32[8,128]{1,0:T(8,128)S(1)} collective-permute-done((f32[8,128]{1,0:T(8,128)S(1)}, f32[8,128]{1,0:T(8,128)S(1)}, u32[]{:S(2)}, u32[]{:S(2)}) %collective-permute-start.14) | collective-permute-done | bytes 4128 | tf_op jit(solution)/shard_map/ppermute | solution.py:532
  51.7 1.5 %collective-permute-start.15 = (f32[8,128]{1,0:T(8,128)S(1)}, f32[8,128]{1,0:T(8,128)S(1)}, u32[]{:S(2)}, u32[]{:S(2)}) collective-permute-start(f32[8,128]{1,0:T(8,128)S(1)} %add.12), channel_id=1, source_target_pairs={{0,4},{2,6},{4,0},{6,2},{8,12},{10,14},{12,8},{14,10},{16,20},{18,... | collective-permute-start | bytes 12296 | tf_op jit(solution)/shard_map/ppermute | solution.py:532
  53.2 2.1 %collective-permute-done.15 = f32[8,128]{1,0:T(8,128)S(1)} collective-permute-done((f32[8,128]{1,0:T(8,128)S(1)}, f32[8,128]{1,0:T(8,128)S(1)}, u32[]{:S(2)}, u32[]{:S(2)}) %collective-permute-start.15) | collective-permute-done | bytes 4128 | tf_op jit(solution)/shard_map/ppermute | solution.py:532
  55.3 1.5 %collective-permute-start.16 = (f32[8,128]{1,0:T(8,128)S(1)}, f32[8,128]{1,0:T(8,128)S(1)}, u32[]{:S(2)}, u32[]{:S(2)}) collective-permute-start(f32[8,128]{1,0:T(8,128)S(1)} %add.13), channel_id=1, source_target_pairs={{0,8},{2,10},{4,12},{6,14},{8,0},{10,2},{12,4},{14,6},{16,24},{18,... | collective-permute-start | bytes 12296 | tf_op jit(solution)/shard_map/ppermute | solution.py:532
  56.8 2.1 %collective-permute-done.16 = f32[8,128]{1,0:T(8,128)S(1)} collective-permute-done((f32[8,128]{1,0:T(8,128)S(1)}, f32[8,128]{1,0:T(8,128)S(1)}, u32[]{:S(2)}, u32[]{:S(2)}) %collective-permute-start.16) | collective-permute-done | bytes 4128 | tf_op jit(solution)/shard_map/ppermute | solution.py:532
  58.9 2.5 %collective-permute-start.17 = (f32[8,128]{1,0:T(8,128)S(1)}, f32[8,128]{1,0:T(8,128)S(1)}, u32[]{:S(2)}, u32[]{:S(2)}) collective-permute-start(f32[8,128]{1,0:T(8,128)S(1)} %add.14), channel_id=1, source_target_pairs={{0,16},{2,18},{4,20},{6,22},{8,24},{10,26},{12,28},{14,30},{16,0},... | collective-permute-start | bytes 12296 | tf_op jit(solution)/shard_map/ppermute | solution.py:532
  61.5 2.0 %collective-permute-done.17 = f32[8,128]{1,0:T(8,128)S(1)} collective-permute-done((f32[8,128]{1,0:T(8,128)S(1)}, f32[8,128]{1,0:T(8,128)S(1)}, u32[]{:S(2)}, u32[]{:S(2)}) %collective-permute-start.17) | collective-permute-done | bytes 4128 | tf_op jit(solution)/shard_map/ppermute | solution.py:532
  63.4 2.2 %shard_map.84 = (f32[8,8,4096]{2,1,0:T(8,128)}, f32[8,8,4096]{2,1,0:T(8,128)}) custom-call(f32[17,128]{1,0:T(8,128)S(1)} %broadcast_in_dim.2.tau, f32[3,8,4096]{2,1,0:T(8,128)S(1)} %get-tuple-element.40.weights.weights_all, f32[8,4096]{1,0:T(8,128)S(1)} %collective-permute-done.2.row_above, f32[8,128]{1,0:T(8,128)S(1)} %add.15.sums, ...), custom_call_target="tpu_custom_call" | custom-call | flops 1 | bytes 1 | tf_op jit(solution)/shard_map/pallas_call | solution.py:26
  (9 shorter events, 0.0 us)
Async XLA Ops:
  2.0 11.6 %collective-permute-start = (f32[4,8,2048]{2,1,0:T(8,128)S(1)}, f32[4,8,2048]{2,1,0:T(8,128)S(1)}, u32[]{:S(2)}, u32[]{:S(2)}) collective-permute-start(f32[4,8,2048]{2,1,0:T(8,128)S(1)} %bitcast.22), channel_id=1, source_target_pairs={{0,1},{1,0},{2,3},{3,2},{4,5},{5,4},{6,7},{7,6},{8,9},{9,8},{10,11... | collective-permute-start | bytes 786440 | tf_op jit(solution)/shard_map/ppermute | solution.py:426
  6.6 24.4 %copy-start = (f32[15]{0:T(128)S(1)}, f32[15]{0:T(128)}, u32[]{:S(2)}) copy-start(f32[15]{0:T(128)} %param.10) | copy-start | bytes 184
  6.6 11.0 %collective-permute-start.1 = (f32[4,8,2048]{2,1,0:T(8,128)S(1)}, f32[4,8,2048]{2,1,0:T(8,128)S(1)}, u32[]{:S(2)}, u32[]{:S(2)}) collective-permute-start(f32[4,8,2048]{2,1,0:T(8,128)S(1)} %bitcast.29), channel_id=1, source_target_pairs={{0,1},{1,0},{2,3},{3,2},{4,5},{5,4},{6,7},{7,6},{8,9},{9,8},{10,11... | collective-permute-start | bytes 786440 | tf_op jit(solution)/shard_map/ppermute | solution.py:426
  11.5 10.4 %collective-permute-start.2 = (f32[8,4096]{1,0:T(8,128)S(1)}, f32[8,4096]{1,0:T(8,128)S(1)}, u32[]{:S(2)}, u32[]{:S(2)}) collective-permute-start(f32[8,4096]{1,0:T(8,128)S(1)} %get-tuple-element.45), channel_id=1, source_target_pairs={{0,2},{2,4},{4,6},{6,8},{8,10},{10,12},{12,14},{14,16},{16,18},{18... | collective-permute-start | bytes 393224 | tf_op jit(solution)/shard_map/ppermute | solution.py:485
  11.6 19.9 %collective-permute-start.6 = (f32[8,8,2048]{2,1,0:T(8,128)S(1)}, f32[8,8,2048]{2,1,0:T(8,128)S(1)}, u32[]{:S(2)}, u32[]{:S(2)}) collective-permute-start(f32[8,8,2048]{2,1,0:T(8,128)S(1)} %bitcast.26), channel_id=1, source_target_pairs={{0,1},{1,0},{2,3},{3,2},{4,5},{5,4},{6,7},{7,6},{8,9},{9,8},{10,11... | collective-permute-start | bytes 1572872 | tf_op jit(solution)/shard_map/ppermute | solution.py:426
  19.9 8.5 %collective-permute-start.4 = (f32[16,128]{1,0:T(8,128)S(1)}, f32[16,128]{1,0:T(8,128)S(1)}, u32[]{:S(2)}, u32[]{:S(2)}) collective-permute-start(f32[16,128]{1,0:T(8,128)S(1)} %get-tuple-element.51), channel_id=1, source_target_pairs={{0,1},{1,0},{2,3},{3,2},{4,5},{5,4},{6,7},{7,6},{8,9},{9,8},{10,11... | collective-permute-start | bytes 24584 | tf_op jit(solution)/shard_map/ppermute | solution.py:426
  21.9 7.1 %collective-permute-start.5 = (f32[16,2048]{1,0:T(8,128)S(1)}, f32[16,2048]{1,0:T(8,128)S(1)}, u32[]{:S(2)}, u32[]{:S(2)}) collective-permute-start(f32[16,2048]{1,0:T(8,128)S(1)} %get-tuple-element.52), channel_id=1, source_target_pairs={{2,4},{6,8},{10,12},{14,16},{18,20},{22,24},{26,28},{30,0},{4,2},{... | collective-permute-start | bytes 393224 | tf_op jit(solution)/shard_map/ppermute | solution.py:429
  29.0 15.6 %collective-permute-start.10 = (f32[5,8,2048]{2,1,0:T(8,128)S(1)}, f32[5,8,2048]{2,1,0:T(8,128)S(1)}, u32[]{:S(2)}, u32[]{:S(2)}) collective-permute-start(f32[5,8,2048]{2,1,0:T(8,128)S(1)} %bitcast.27), channel_id=1, source_target_pairs={{0,1},{1,0},{2,3},{3,2},{4,5},{5,4},{6,7},{7,6},{8,9},{9,8},{10,11... | collective-permute-start | bytes 983048 | tf_op jit(solution)/shard_map/ppermute | solution.py:426
  30.1 1.3 %collective-permute-start.3 = (f32[16,2048]{1,0:T(8,128)S(1)}, f32[16,2048]{1,0:T(8,128)S(1)}, u32[]{:S(2)}, u32[]{:S(2)}) collective-permute-start(f32[16,2048]{1,0:T(8,128)S(1)} %get-tuple-element.48), channel_id=1, source_target_pairs={{0,2},{2,0},{4,6},{6,4},{8,10},{10,8},{12,14},{14,12},{16,18},{18,... | collective-permute-start | bytes 393224 | tf_op jit(solution)/shard_map/ppermute | solution.py:429
  30.1 14.5 %collective-permute-start.11 = (f32[4,8,2048]{2,1,0:T(8,128)S(1)}, f32[4,8,2048]{2,1,0:T(8,128)S(1)}, u32[]{:S(2)}, u32[]{:S(2)}) collective-permute-start(f32[4,8,2048]{2,1,0:T(8,128)S(1)} %bitcast.28), channel_id=1, source_target_pairs={{0,1},{1,0},{2,3},{3,2},{4,5},{5,4},{6,7},{7,6},{8,9},{9,8},{10,11... | collective-permute-start | bytes 786440 | tf_op jit(solution)/shard_map/ppermute | solution.py:426
  35.0 5.5 %collective-permute-start.7 = (f32[16,2048]{1,0:T(8,128)S(1)}, f32[16,2048]{1,0:T(8,128)S(1)}, u32[]{:S(2)}, u32[]{:S(2)}) collective-permute-start(f32[16,2048]{1,0:T(8,128)S(1)} %get-tuple-element.59), channel_id=1, source_target_pairs={{0,2},{2,0},{4,6},{6,4},{8,10},{10,8},{12,14},{14,12},{16,18},{18,... | collective-permute-start | bytes 393224 | tf_op jit(solution)/shard_map/ppermute | solution.py:429
  35.2 7.1 %collective-permute-start.8 = (f32[16,2048]{1,0:T(8,128)S(1)}, f32[16,2048]{1,0:T(8,128)S(1)}, u32[]{:S(2)}, u32[]{:S(2)}) collective-permute-start(f32[16,2048]{1,0:T(8,128)S(1)} %get-tuple-element.60), channel_id=1, source_target_pairs={{2,4},{6,8},{10,12},{14,16},{18,20},{22,24},{26,28},{30,0},{4,2},{... | collective-permute-start | bytes 393224 | tf_op jit(solution)/shard_map/ppermute | solution.py:429
  39.7 8.7 %collective-permute-start.9 = (f32[16,2048]{1,0:T(8,128)S(1)}, f32[16,2048]{1,0:T(8,128)S(1)}, u32[]{:S(2)}, u32[]{:S(2)}) collective-permute-start(f32[16,2048]{1,0:T(8,128)S(1)} %bitcast.31), channel_id=1, source_target_pairs={{0,1},{1,0},{2,3},{3,2},{4,5},{5,4},{6,7},{7,6},{8,9},{9,8},{10,11... | collective-permute-start | bytes 393224 | tf_op jit(solution)/shard_map/ppermute | solution.py:426
  40.5 5.7 %collective-permute-start.12 = (f32[16,128]{1,0:T(8,128)S(1)}, f32[16,128]{1,0:T(8,128)S(1)}, u32[]{:S(2)}, u32[]{:S(2)}) collective-permute-start(f32[16,128]{1,0:T(8,128)S(1)} %get-tuple-element.67.ends), channel_id=1, source_target_pairs={{0,1},{1,0},{2,3},{3,2},{4,5},{5,4},{6,7},{7,6},{8,9},{9,8},{10,11... | collective-permute-start | bytes 24584 | tf_op jit(solution)/shard_map/ppermute | solution.py:426
  44.6 3.6 %collective-permute-start.13 = (f32[8,128]{1,0:T(8,128)S(1)}, f32[8,128]{1,0:T(8,128)S(1)}, u32[]{:S(2)}, u32[]{:S(2)}) collective-permute-start(f32[8,128]{1,0:T(8,128)S(1)} %get-tuple-element.71.sums), channel_id=1, source_target_pairs={{0,1},{1,0},{2,3},{3,2},{4,5},{5,4},{6,7},{7,6},{8,9},{9,8},{10,11... | collective-permute-start | bytes 12296 | tf_op jit(solution)/shard_map/ppermute | solution.py:426
  48.4 15.0 %collective-permute-start.18 = (f32[9,8,2048]{2,1,0:T(8,128)S(1)}, f32[9,8,2048]{2,1,0:T(8,128)S(1)}, u32[]{:S(2)}, u32[]{:S(2)}) collective-permute-start(f32[9,8,2048]{2,1,0:T(8,128)S(1)} %bitcast.25), channel_id=1, source_target_pairs={{0,1},{1,0},{2,3},{3,2},{4,5},{5,4},{6,7},{7,6},{8,9},{9,8},{10,11... | collective-permute-start | bytes 1769480 | tf_op jit(solution)/shard_map/ppermute | solution.py:426
  50.0 13.4 %collective-permute-start.19 = (f32[16,2048]{1,0:T(8,128)S(1)}, f32[16,2048]{1,0:T(8,128)S(1)}, u32[]{:S(2)}, u32[]{:S(2)}) collective-permute-start(f32[16,2048]{1,0:T(8,128)S(1)} %bitcast.30), channel_id=1, source_target_pairs={{0,1},{1,0},{2,3},{3,2},{4,5},{5,4},{6,7},{7,6},{8,9},{9,8},{10,11... | collective-permute-start | bytes 393224 | tf_op jit(solution)/shard_map/ppermute | solution.py:426
  50.5 1.2 %collective-permute-start.14 = (f32[8,128]{1,0:T(8,128)S(1)}, f32[8,128]{1,0:T(8,128)S(1)}, u32[]{:S(2)}, u32[]{:S(2)}) collective-permute-start(f32[8,128]{1,0:T(8,128)S(1)} %shard_map.83), channel_id=1, source_target_pairs={{0,2},{2,0},{4,6},{6,4},{8,10},{10,8},{12,14},{14,12},{16,18},{18,... | collective-permute-start | bytes 12296 | tf_op jit(solution)/shard_map/ppermute | solution.py:532
  51.7 3.6 %collective-permute-start.15 = (f32[8,128]{1,0:T(8,128)S(1)}, f32[8,128]{1,0:T(8,128)S(1)}, u32[]{:S(2)}, u32[]{:S(2)}) collective-permute-start(f32[8,128]{1,0:T(8,128)S(1)} %add.12), channel_id=1, source_target_pairs={{0,4},{2,6},{4,0},{6,2},{8,12},{10,14},{12,8},{14,10},{16,20},{18,... | collective-permute-start | bytes 12296 | tf_op jit(solution)/shard_map/ppermute | solution.py:532
  55.3 3.6 %collective-permute-start.16 = (f32[8,128]{1,0:T(8,128)S(1)}, f32[8,128]{1,0:T(8,128)S(1)}, u32[]{:S(2)}, u32[]{:S(2)}) collective-permute-start(f32[8,128]{1,0:T(8,128)S(1)} %add.13), channel_id=1, source_target_pairs={{0,8},{2,10},{4,12},{6,14},{8,0},{10,2},{12,4},{14,6},{16,24},{18,... | collective-permute-start | bytes 12296 | tf_op jit(solution)/shard_map/ppermute | solution.py:532
  58.9 4.5 %collective-permute-start.17 = (f32[8,128]{1,0:T(8,128)S(1)}, f32[8,128]{1,0:T(8,128)S(1)}, u32[]{:S(2)}, u32[]{:S(2)}) collective-permute-start(f32[8,128]{1,0:T(8,128)S(1)} %add.14), channel_id=1, source_target_pairs={{0,16},{2,18},{4,20},{6,22},{8,24},{10,26},{12,28},{14,30},{16,0},... | collective-permute-start | bytes 12296 | tf_op jit(solution)/shard_map/ppermute | solution.py:532

commit v5 on v4

--- a/solution.py
+++ b/solution.py
@@ -307,7 +307,7 @@
     blocks, tau, weights, row_above, mapped, halo_1, halo_2, data_weight, dot_1, dot_2, dot_3, *refs,
 ):
     *ends, sums, forwarded, total = refs
-    left, right = ends or (None, None)
+    left, right = ends if blocks != 2 else (None, None)
     total[...] = jnp.zeros_like(total)
 
     def use(t, value, image):
@@ -318,16 +318,20 @@
     result = jnp.zeros((8, LANES), jnp.float32)
     for index, dot in enumerate((dot_1, dot_2, dot_3, total)):
         result = jnp.where(rows == index, jnp.sum(dot[...]), result)
-    sums[...] = result
+    if blocks == 2:
+        sums[0:16, :] = ends[0][...]
+        sums[16:24, :] = result
+    else:
+        sums[...] = result
     forward_halos(halo_1, halo_2, forwarded, lax.axis_index("dates"), blocks)
 
 
-def join_kernel(weights, ends, sums, ends_other, sums_other, joined):
+def join_kernel(weights, here, other, joined):
     width = weights.shape[2] // 2
     boundary = weights[0, :, width - LANES : width][:, LANES - 1 : LANES]
-    dates = jnp.where(lax.axis_index("dates") == 0, ends[8:16, :] * ends_other[0:8, :], ends[0:8, :] * ends_other[8:16, :])
+    dates = jnp.where(lax.axis_index("dates") == 0, here[8:16, :] * other[0:8, :], here[0:8, :] * other[8:16, :])
     crossing = -2.0 * jnp.sum(boundary * dates)
-    joined[...] = sums[...] + sums_other[...] + jnp.where(row_ids(LANES) == 3, crossing, 0.0)
+    joined[...] = here[16:24, :] + other[16:24, :] + jnp.where(row_ids(LANES) == 3, crossing, 0.0)
 
 
 def last_kernel(
@@ -506,10 +510,10 @@
         [tau, weights, row_above, precond, p_halo_1, p_halo_2, p_left, p_right, weight_here, weight_other, staged],
     )
     m_halo_1, m_halo_2 = swap_rows(m_first, m_second)
-    m_ends_other = () if blocks == 2 else swap_ends(m_ends)
+    m_ends_other = (m_ends,) if blocks == 2 else swap_ends(m_ends)
     sums, m_forward = call(
         functools.partial(third_kernel, blocks),
-        [vector, edges_shape],
+        [(24, LANES) if blocks == 2 else vector, edges_shape],
         [vector],
         [],
         [tau, weights, row_above, mapped, m_halo_1, m_halo_2, data_weight, dot_1, dot_2, dot_3, *m_ends_other],
@@ -517,8 +521,7 @@
     precond_halos = send(p_forward)
     sums, precond_early, precond_late = lax.optimization_barrier((sums, precond_early, precond_late))
     if blocks == 2:
-        ends_other, sums_other = rotate(m_ends, 1), rotate(sums, 1)
-        (sums,) = call(join_kernel, [vector], [], [], [weights, m_ends, sums, ends_other, sums_other])
+        (sums,) = call(join_kernel, [vector], [], [], [weights, sums, rotate(sums, 1)])
     else:
         steps = 1
         while steps < blocks:

time: 65.9 us -> 66 us (level)
  waiting for transfers between devices: 20.5 us -> 22.4 us
  starting transfers between devices: 27.2 us -> 25.4 us
    ppermute x2, waiting for transfers between devices: 1.23 us -> 2.5 us  [swap_rows(): lax.ppermute(second, 'rows', across_pairs)]
    ppermute x11 -> x10, starting transfers between devices: 14.9 us -> 13.6 us  [rotate(): lax.ppermute(value, 'dates', [(i, (i + k) % blocks) for i in range(blocks)])]
    ppermute x11 -> x10, waiting for transfers between devices: 11.6 us -> 11.7 us  [rotate(): lax.ppermute(value, 'dates', [(i, (i + k) % blocks) for i in range(blocks)])]
  transfers between devices with their start and end apart: 20 -> 19, of which waited for: 11 -> 11; matrix products, arithmetic and copies ran while one was open for 0% -> 0% of each run, Pallas kernels for 21% -> 21%
where the time goes in v5:
time: 66 us; the launch traced here: 65.8 us
  starting transfers between devices  25.4 us (38%)
  waiting for transfers between devices  22.4 us (34%)
  Pallas kernels  17.1 us (26%)
  between operations  0.73 us (1%)
    pallas_call x8, Pallas kernels, call(): pl.pallas_call(kernel, out_shape=[jax.ShapeDtypeStruct(*typed(entry)) for...  17.1 us
    ppermute x10, starting transfers between devices, rotate(): lax.ppermute(value, 'dates', [(i, (i + k) % blocks) for i in range(blocks)])  13.6 us
    ppermute x10, waiting for transfers between devices, rotate(): lax.ppermute(value, 'dates', [(i, (i + k) % blocks) for i in range(blocks)])  11.7 us
    ppermute x4, waiting for transfers between devices, body(): lax.ppermute(sums, 'rows', [(i, i ^ steps) for i in range(slabs)])  7.78 us
    ppermute x2, starting transfers between devices, swap_rows(): lax.ppermute(second, 'rows', across_pairs)  6.44 us
    ppermute x4, starting transfers between devices, body(): lax.ppermute(sums, 'rows', [(i, i ^ steps) for i in range(slabs)])  5.1 us
    ppermute x2, waiting for transfers between devices, swap_rows(): lax.ppermute(second, 'rows', across_pairs)  2.5 us
  transfers between devices with their start and end apart: 19, of which 11 were waited for; matrix products, arithmetic and copies ran while one was open for 0% of the time, Pallas kernels for 21%

profile of v5, /device:TPU:0, one launch (start us, length us, event | category | flops | bytes accessed | tf_op | source)
XLA Modules:
  0.0 65.8 jit_solution(6582884514006161867)
XLA Ops:
  0.6 1.4 %shard_map.78 = f32[1,4,8,2048]{3,2,1,0:T(8,128)S(1)} custom-call(s32[8,8,4096]{2,1,0:T(8,128)} %mask.5, f32[8,8,4096]{2,1,0:T(8,128)} %precision.5, f32[8,8,4096]{2,1,0:T(8,128)} %observed.5), custom_call_target="tpu_custom_call" | custom-call | flops 1 | bytes 1 | tf_op jit(solution)/shard_map/pallas_call | solution.py:26
  2.0 3.0 %collective-permute-start = (f32[4,8,2048]{2,1,0:T(8,128)S(1)}, f32[4,8,2048]{2,1,0:T(8,128)S(1)}, u32[]{:S(2)}, u32[]{:S(2)}) collective-permute-start(f32[4,8,2048]{2,1,0:T(8,128)S(1)} %bitcast.22), channel_id=1, source_target_pairs={{0,1},{1,0},{2,3},{3,2},{4,5},{5,4},{6,7},{7,6},{8,9},{9,8},{10,11... | collective-permute-start | bytes 786440 | tf_op jit(solution)/shard_map/ppermute | solution.py:430
  5.1 1.5 %shard_map.79 = (f32[1,4,8,2048]{3,2,1,0:T(8,128)S(1)}, f32[1,8,8,2048]{3,2,1,0:T(8,128)S(1)}) custom-call(s32[8,8,4096]{2,1,0:T(8,128)} %mask.5, f32[8,8,4096]{2,1,0:T(8,128)} %precision.5, f32[8,8,4096]{2,1,0:T(8,128)} %observed.5), custom_call_target="tpu_custom_call" | custom-call | flops 1 | bytes 1 | tf_op jit(solution)/shard_map/pallas_call | solution.py:26
  6.6 0.0 copy-start
  6.6 0.1 collective-permute-start.1
  6.7 4.8 %shard_map.77 = (bf16[16,16,8,2048]{3,2,1,0:T(8,128)(2,1)S(1)}, f32[8,8,4096]{2,1,0:T(8,128)S(1)}, f32[8,8,4096]{2,1,0:T(8,128)S(1)}, f32[3,8,4096]{2,1,0:T(8,128)S(1)}, f32[8,4096]{1,0:T(8,128)S(1)}) custom-call(s32[8,8,4096]{2,1,0:T(8,128)} %mask.5, f32[8,8,4096]{2,1,0:T(8,128)} %precision.5, f32[8,8,4096]{2,1,0:T(8,128)} %observed.5, ...), custom_call_target="tpu_custom_call" | custom-call | flops 1 | bytes 1 | tf_op jit(solution)/shard_map/pallas_call | solution.py:26
  11.5 0.1 collective-permute-start.2
  11.6 2.1 %collective-permute-start.6 = (f32[8,8,2048]{2,1,0:T(8,128)S(1)}, f32[8,8,2048]{2,1,0:T(8,128)S(1)}, u32[]{:S(2)}, u32[]{:S(2)}) collective-permute-start(f32[8,8,2048]{2,1,0:T(8,128)S(1)} %bitcast.26), channel_id=1, source_target_pairs={{0,1},{1,0},{2,3},{3,2},{4,5},{5,4},{6,7},{7,6},{8,9},{9,8},{10,11... | collective-permute-start | bytes 1572872 | tf_op jit(solution)/shard_map/ppermute | solution.py:430
  13.6 0.0 collective-permute-done
  13.7 4.0 %collective-permute-done.1 = f32[4,8,2048]{2,1,0:T(8,128)S(1)} collective-permute-done((f32[4,8,2048]{2,1,0:T(8,128)S(1)}, f32[4,8,2048]{2,1,0:T(8,128)S(1)}, u32[]{:S(2)}, u32[]{:S(2)}) %collective-permute-start.1) | collective-permute-done | bytes 262176 | tf_op jit(solution)/shard_map/ppermute | solution.py:430
  17.6 2.2 %shard_map.80 = (f32[16,8,2048]{2,1,0:T(8,128)S(1)}, f32[16,2048]{1,0:T(8,128)S(1)}, f32[16,2048]{1,0:T(8,128)S(1)}, f32[16,128]{1,0:T(8,128)S(1)}, f32[1,5,8,20...) custom-call(f32[8,8,4096]{2,1,0:T(8,128)S(1)} %get-tuple-element.41.rhs_here.rhs, ...), custom_call_target="tpu_custom_call" | custom-call | flops 1 | bytes 1 | tf_op jit(solution)/shard_map/pallas_call | solution.py:26
  19.9 2.0 %collective-permute-start.4 = (f32[16,128]{1,0:T(8,128)S(1)}, f32[16,128]{1,0:T(8,128)S(1)}, u32[]{:S(2)}, u32[]{:S(2)}) collective-permute-start(f32[16,128]{1,0:T(8,128)S(1)} %get-tuple-element.51), channel_id=1, source_target_pairs={{0,1},{1,0},{2,3},{3,2},{4,5},{5,4},{6,7},{7,6},{8,9},{9,8},{10,11... | collective-permute-start | bytes 24584 | tf_op jit(solution)/shard_map/ppermute | solution.py:430
  21.9 0.0 collective-permute-done.2.row_above
  21.9 1.9 %collective-permute-start.5 = (f32[16,2048]{1,0:T(8,128)S(1)}, f32[16,2048]{1,0:T(8,128)S(1)}, u32[]{:S(2)}, u32[]{:S(2)}) collective-permute-start(f32[16,2048]{1,0:T(8,128)S(1)} %get-tuple-element.52), channel_id=1, source_target_pairs={{2,4},{6,8},{10,12},{14,16},{18,20},{22,24},{26,28},{30,0},{4,2},{... | collective-permute-start | bytes 393224 | tf_op jit(solution)/shard_map/ppermute | solution.py:433
  23.9 4.5 %collective-permute-done.4 = f32[16,128]{1,0:T(8,128)S(1)} collective-permute-done((f32[16,128]{1,0:T(8,128)S(1)}, f32[16,128]{1,0:T(8,128)S(1)}, u32[]{:S(2)}, u32[]{:S(2)}) %collective-permute-start.4) | collective-permute-done | bytes 8224 | tf_op jit(solution)/shard_map/ppermute | solution.py:430
  28.4 0.6 collective-permute-done.5.halo_2.own_p2
  29.0 1.1 %collective-permute-start.10 = (f32[5,8,2048]{2,1,0:T(8,128)S(1)}, f32[5,8,2048]{2,1,0:T(8,128)S(1)}, u32[]{:S(2)}, u32[]{:S(2)}) collective-permute-start(f32[5,8,2048]{2,1,0:T(8,128)S(1)} %bitcast.27), channel_id=1, source_target_pairs={{0,1},{1,0},{2,3},{3,2},{4,5},{5,4},{6,7},{7,6},{8,9},{9,8},{10,11... | collective-permute-start | bytes 983048 | tf_op jit(solution)/shard_map/ppermute | solution.py:430
  30.1 0.0 collective-permute-start.3
  30.1 0.9 %collective-permute-start.11 = (f32[4,8,2048]{2,1,0:T(8,128)S(1)}, f32[4,8,2048]{2,1,0:T(8,128)S(1)}, u32[]{:S(2)}, u32[]{:S(2)}) collective-permute-start(f32[4,8,2048]{2,1,0:T(8,128)S(1)} %bitcast.28), channel_id=1, source_target_pairs={{0,1},{1,0},{2,3},{3,2},{4,5},{5,4},{6,7},{7,6},{8,9},{9,8},{10,11... | collective-permute-start | bytes 786440 | tf_op jit(solution)/shard_map/ppermute | solution.py:430
  31.0 0.1 pad_maximum_fusion
  31.1 0.4 collective-permute-done.3.halo_1.own_p1
  31.5 0.0 collective-permute-done.6
  31.5 0.1 broadcast_in_dim.2.tau
  31.6 3.4 %shard_map.81 = (f32[16,8,2048]{2,1,0:T(8,128)S(1)}, f32[16,2048]{1,0:T(8,128)S(1)}, f32[16,2048]{1,0:T(8,128)S(1)}, f32[16,128]{1,0:T(8,128)S(1)}, f32[1,9,8,20...) custom-call(f32[17,128]{1,0:T(8,128)S(1)} %broadcast_in_dim.2.tau, ...), custom_call_target="tpu_custom_call" | custom-call | flops 1 | bytes 1 | tf_op jit(solution)/shard_map/pallas_call | solution.py:26
  35.0 0.2 collective-permute-start.7
  35.2 4.5 %collective-permute-start.8 = (f32[16,2048]{1,0:T(8,128)S(1)}, f32[16,2048]{1,0:T(8,128)S(1)}, u32[]{:S(2)}, u32[]{:S(2)}) collective-permute-start(f32[16,2048]{1,0:T(8,128)S(1)} %get-tuple-element.60), channel_id=1, source_target_pairs={{2,4},{6,8},{10,12},{14,16},{18,20},{22,24},{26,28},{30,0},{4,2},{... | collective-permute-start | bytes 393224 | tf_op jit(solution)/shard_map/ppermute | solution.py:433
  39.7 0.8 %collective-permute-start.9 = (f32[16,2048]{1,0:T(8,128)S(1)}, f32[16,2048]{1,0:T(8,128)S(1)}, u32[]{:S(2)}, u32[]{:S(2)}) collective-permute-start(f32[16,2048]{1,0:T(8,128)S(1)} %bitcast.31), channel_id=1, source_target_pairs={{0,1},{1,0},{2,3},{3,2},{4,5},{5,4},{6,7},{7,6},{8,9},{9,8},{10,11... | collective-permute-start | bytes 393224 | tf_op jit(solution)/shard_map/ppermute | solution.py:430
  40.5 0.0 collective-permute-done.7.halo_1.own_m1
  40.5 1.9 %collective-permute-done.8.halo_2.own_m2 = f32[16,2048]{1,0:T(8,128)S(1)} collective-permute-done((f32[16,2048]{1,0:T(8,128)S(1)}, f32[16,2048]{1,0:T(8,128)S(1)}, u32[]{:S(2)}, u32[]{:S(2)}) %collective-permute-start.8) | collective-permute-done | bytes 131104 | tf_op jit(solution)/shard_map/ppermute | solution.py:433
  42.3 1.4 %shard_map.82 = (f32[24,128]{1,0:T(8,128)S(1)}, f32[1,16,2048]{2,1,0:T(8,128)S(1)}) custom-call(f32[17,128]{1,0:T(8,128)S(1)} %broadcast_in_dim.2.tau, f32[3,8,4096]{2,1,0:T(8,128)S(1)} %get-tuple-element.40.weights.weights_all, f32[8,4096]{1,0:T(8,128)S(1)} %collective-permute-done.2.row_above, f32[16,8,2048]{2,1,0:T(8,128)S(1)} %get-tuple-element.58.mapped, ...), custom_call_target="tpu_custom_call" | custom-call | flops 1 | bytes 1 | tf_op jit(solution)/shard_map/pallas_call | solution.py:26
  43.7 0.9 %collective-permute-done.11 = f32[4,8,2048]{2,1,0:T(8,128)S(1)} collective-permute-done((f32[4,8,2048]{2,1,0:T(8,128)S(1)}, f32[4,8,2048]{2,1,0:T(8,128)S(1)}, u32[]{:S(2)}, u32[]{:S(2)}) %collective-permute-start.11) | collective-permute-done | bytes 262176 | tf_op jit(solution)/shard_map/ppermute | solution.py:430
  44.6 0.0 collective-permute-done.10
  44.6 1.5 %collective-permute-start.12 = (f32[24,128]{1,0:T(8,128)S(1)}, f32[24,128]{1,0:T(8,128)S(1)}, u32[]{:S(2)}, u32[]{:S(2)}) collective-permute-start(f32[24,128]{1,0:T(8,128)S(1)} %get-tuple-element.71.here), channel_id=1, source_target_pairs={{0,1},{1,0},{2,3},{3,2},{4,5},{5,4},{6,7},{7,6},{8,9},{9,8},{10,11... | collective-permute-start | bytes 36872 | tf_op jit(solution)/shard_map/ppermute | solution.py:430
  46.1 2.3 %collective-permute-done.12.other = f32[24,128]{1,0:T(8,128)S(1)} collective-permute-done((f32[24,128]{1,0:T(8,128)S(1)}, f32[24,128]{1,0:T(8,128)S(1)}, u32[]{:S(2)}, u32[]{:S(2)}) %collective-permute-start.12) | collective-permute-done | bytes 12320 | tf_op jit(solution)/shard_map/ppermute | solution.py:430
  48.4 0.2 shard_map.83
  48.6 0.0 collective-permute-done.9
  48.6 1.6 %collective-permute-start.17 = (f32[9,8,2048]{2,1,0:T(8,128)S(1)}, f32[9,8,2048]{2,1,0:T(8,128)S(1)}, u32[]{:S(2)}, u32[]{:S(2)}) collective-permute-start(f32[9,8,2048]{2,1,0:T(8,128)S(1)} %bitcast.25), channel_id=1, source_target_pairs={{0,1},{1,0},{2,3},{3,2},{4,5},{5,4},{6,7},{7,6},{8,9},{9,8},{10,11... | collective-permute-start | bytes 1769480 | tf_op jit(solution)/shard_map/ppermute | solution.py:430
  50.2 0.5 collective-permute-start.18
  50.7 0.0 collective-permute-start.13
  50.7 1.2 %collective-permute-done.13 = f32[8,128]{1,0:T(8,128)S(1)} collective-permute-done((f32[8,128]{1,0:T(8,128)S(1)}, f32[8,128]{1,0:T(8,128)S(1)}, u32[]{:S(2)}, u32[]{:S(2)}) %collective-permute-start.13) | collective-permute-done | bytes 4128 | tf_op jit(solution)/shard_map/ppermute | solution.py:535
  51.9 1.4 %collective-permute-start.14 = (f32[8,128]{1,0:T(8,128)S(1)}, f32[8,128]{1,0:T(8,128)S(1)}, u32[]{:S(2)}, u32[]{:S(2)}) collective-permute-start(f32[8,128]{1,0:T(8,128)S(1)} %add.12), channel_id=1, source_target_pairs={{0,4},{2,6},{4,0},{6,2},{8,12},{10,14},{12,8},{14,10},{16,20},{18,... | collective-permute-start | bytes 12296 | tf_op jit(solution)/shard_map/ppermute | solution.py:535
  53.2 2.2 %collective-permute-done.14 = f32[8,128]{1,0:T(8,128)S(1)} collective-permute-done((f32[8,128]{1,0:T(8,128)S(1)}, f32[8,128]{1,0:T(8,128)S(1)}, u32[]{:S(2)}, u32[]{:S(2)}) %collective-permute-start.14) | collective-permute-done | bytes 4128 | tf_op jit(solution)/shard_map/ppermute | solution.py:535
  55.5 1.4 %collective-permute-start.15 = (f32[8,128]{1,0:T(8,128)S(1)}, f32[8,128]{1,0:T(8,128)S(1)}, u32[]{:S(2)}, u32[]{:S(2)}) collective-permute-start(f32[8,128]{1,0:T(8,128)S(1)} %add.13), channel_id=1, source_target_pairs={{0,8},{2,10},{4,12},{6,14},{8,0},{10,2},{12,4},{14,6},{16,24},{18,... | collective-permute-start | bytes 12296 | tf_op jit(solution)/shard_map/ppermute | solution.py:535
  56.8 2.2 %collective-permute-done.15 = f32[8,128]{1,0:T(8,128)S(1)} collective-permute-done((f32[8,128]{1,0:T(8,128)S(1)}, f32[8,128]{1,0:T(8,128)S(1)}, u32[]{:S(2)}, u32[]{:S(2)}) %collective-permute-start.15) | collective-permute-done | bytes 4128 | tf_op jit(solution)/shard_map/ppermute | solution.py:535
  59.1 2.4 %collective-permute-start.16 = (f32[8,128]{1,0:T(8,128)S(1)}, f32[8,128]{1,0:T(8,128)S(1)}, u32[]{:S(2)}, u32[]{:S(2)}) collective-permute-start(f32[8,128]{1,0:T(8,128)S(1)} %add.14), channel_id=1, source_target_pairs={{0,16},{2,18},{4,20},{6,22},{8,24},{10,26},{12,28},{14,30},{16,0},... | collective-permute-start | bytes 12296 | tf_op jit(solution)/shard_map/ppermute | solution.py:535
  61.5 2.1 %collective-permute-done.16 = f32[8,128]{1,0:T(8,128)S(1)} collective-permute-done((f32[8,128]{1,0:T(8,128)S(1)}, f32[8,128]{1,0:T(8,128)S(1)}, u32[]{:S(2)}, u32[]{:S(2)}) %collective-permute-start.16) | collective-permute-done | bytes 4128 | tf_op jit(solution)/shard_map/ppermute | solution.py:535
  63.6 0.0 collective-permute-done.17
  63.6 2.2 %shard_map.84 = (f32[8,8,4096]{2,1,0:T(8,128)}, f32[8,8,4096]{2,1,0:T(8,128)}) custom-call(f32[17,128]{1,0:T(8,128)S(1)} %broadcast_in_dim.2.tau, f32[3,8,4096]{2,1,0:T(8,128)S(1)} %get-tuple-element.40.weights.weights_all, f32[8,4096]{1,0:T(8,128)S(1)} %collective-permute-done.2.row_above, f32[8,128]{1,0:T(8,128)S(1)} %add.15.sums, ...), custom_call_target="tpu_custom_call" | custom-call | flops 1 | bytes 1 | tf_op jit(solution)/shard_map/pallas_call | solution.py:26
  (7 shorter events, 0.0 us)
Async XLA Ops:
  2.0 11.6 %collective-permute-start = (f32[4,8,2048]{2,1,0:T(8,128)S(1)}, f32[4,8,2048]{2,1,0:T(8,128)S(1)}, u32[]{:S(2)}, u32[]{:S(2)}) collective-permute-start(f32[4,8,2048]{2,1,0:T(8,128)S(1)} %bitcast.22), channel_id=1, source_target_pairs={{0,1},{1,0},{2,3},{3,2},{4,5},{5,4},{6,7},{7,6},{8,9},{9,8},{10,11... | collective-permute-start | bytes 786440 | tf_op jit(solution)/shard_map/ppermute | solution.py:430
  6.6 24.4 %copy-start = (f32[15]{0:T(128)S(1)}, f32[15]{0:T(128)}, u32[]{:S(2)}) copy-start(f32[15]{0:T(128)} %param.10) | copy-start | bytes 184
  6.6 11.0 %collective-permute-start.1 = (f32[4,8,2048]{2,1,0:T(8,128)S(1)}, f32[4,8,2048]{2,1,0:T(8,128)S(1)}, u32[]{:S(2)}, u32[]{:S(2)}) collective-permute-start(f32[4,8,2048]{2,1,0:T(8,128)S(1)} %bitcast.29), channel_id=1, source_target_pairs={{0,1},{1,0},{2,3},{3,2},{4,5},{5,4},{6,7},{7,6},{8,9},{9,8},{10,11... | collective-permute-start | bytes 786440 | tf_op jit(solution)/shard_map/ppermute | solution.py:430
  11.5 10.4 %collective-permute-start.2 = (f32[8,4096]{1,0:T(8,128)S(1)}, f32[8,4096]{1,0:T(8,128)S(1)}, u32[]{:S(2)}, u32[]{:S(2)}) collective-permute-start(f32[8,4096]{1,0:T(8,128)S(1)} %get-tuple-element.45), channel_id=1, source_target_pairs={{0,2},{2,4},{4,6},{6,8},{8,10},{10,12},{12,14},{14,16},{16,18},{18... | collective-permute-start | bytes 393224 | tf_op jit(solution)/shard_map/ppermute | solution.py:489
  11.6 19.9 %collective-permute-start.6 = (f32[8,8,2048]{2,1,0:T(8,128)S(1)}, f32[8,8,2048]{2,1,0:T(8,128)S(1)}, u32[]{:S(2)}, u32[]{:S(2)}) collective-permute-start(f32[8,8,2048]{2,1,0:T(8,128)S(1)} %bitcast.26), channel_id=1, source_target_pairs={{0,1},{1,0},{2,3},{3,2},{4,5},{5,4},{6,7},{7,6},{8,9},{9,8},{10,11... | collective-permute-start | bytes 1572872 | tf_op jit(solution)/shard_map/ppermute | solution.py:430
  19.9 8.5 %collective-permute-start.4 = (f32[16,128]{1,0:T(8,128)S(1)}, f32[16,128]{1,0:T(8,128)S(1)}, u32[]{:S(2)}, u32[]{:S(2)}) collective-permute-start(f32[16,128]{1,0:T(8,128)S(1)} %get-tuple-element.51), channel_id=1, source_target_pairs={{0,1},{1,0},{2,3},{3,2},{4,5},{5,4},{6,7},{7,6},{8,9},{9,8},{10,11... | collective-permute-start | bytes 24584 | tf_op jit(solution)/shard_map/ppermute | solution.py:430
  21.9 7.1 %collective-permute-start.5 = (f32[16,2048]{1,0:T(8,128)S(1)}, f32[16,2048]{1,0:T(8,128)S(1)}, u32[]{:S(2)}, u32[]{:S(2)}) collective-permute-start(f32[16,2048]{1,0:T(8,128)S(1)} %get-tuple-element.52), channel_id=1, source_target_pairs={{2,4},{6,8},{10,12},{14,16},{18,20},{22,24},{26,28},{30,0},{4,2},{... | collective-permute-start | bytes 393224 | tf_op jit(solution)/shard_map/ppermute | solution.py:433
  29.0 15.6 %collective-permute-start.10 = (f32[5,8,2048]{2,1,0:T(8,128)S(1)}, f32[5,8,2048]{2,1,0:T(8,128)S(1)}, u32[]{:S(2)}, u32[]{:S(2)}) collective-permute-start(f32[5,8,2048]{2,1,0:T(8,128)S(1)} %bitcast.27), channel_id=1, source_target_pairs={{0,1},{1,0},{2,3},{3,2},{4,5},{5,4},{6,7},{7,6},{8,9},{9,8},{10,11... | collective-permute-start | bytes 983048 | tf_op jit(solution)/shard_map/ppermute | solution.py:430
  30.1 1.3 %collective-permute-start.3 = (f32[16,2048]{1,0:T(8,128)S(1)}, f32[16,2048]{1,0:T(8,128)S(1)}, u32[]{:S(2)}, u32[]{:S(2)}) collective-permute-start(f32[16,2048]{1,0:T(8,128)S(1)} %get-tuple-element.48), channel_id=1, source_target_pairs={{0,2},{2,0},{4,6},{6,4},{8,10},{10,8},{12,14},{14,12},{16,18},{18,... | collective-permute-start | bytes 393224 | tf_op jit(solution)/shard_map/ppermute | solution.py:433
  30.1 14.5 %collective-permute-start.11 = (f32[4,8,2048]{2,1,0:T(8,128)S(1)}, f32[4,8,2048]{2,1,0:T(8,128)S(1)}, u32[]{:S(2)}, u32[]{:S(2)}) collective-permute-start(f32[4,8,2048]{2,1,0:T(8,128)S(1)} %bitcast.28), channel_id=1, source_target_pairs={{0,1},{1,0},{2,3},{3,2},{4,5},{5,4},{6,7},{7,6},{8,9},{9,8},{10,11... | collective-permute-start | bytes 786440 | tf_op jit(solution)/shard_map/ppermute | solution.py:430
  35.0 5.5 %collective-permute-start.7 = (f32[16,2048]{1,0:T(8,128)S(1)}, f32[16,2048]{1,0:T(8,128)S(1)}, u32[]{:S(2)}, u32[]{:S(2)}) collective-permute-start(f32[16,2048]{1,0:T(8,128)S(1)} %get-tuple-element.59), channel_id=1, source_target_pairs={{0,2},{2,0},{4,6},{6,4},{8,10},{10,8},{12,14},{14,12},{16,18},{18,... | collective-permute-start | bytes 393224 | tf_op jit(solution)/shard_map/ppermute | solution.py:433
  35.2 7.2 %collective-permute-start.8 = (f32[16,2048]{1,0:T(8,128)S(1)}, f32[16,2048]{1,0:T(8,128)S(1)}, u32[]{:S(2)}, u32[]{:S(2)}) collective-permute-start(f32[16,2048]{1,0:T(8,128)S(1)} %get-tuple-element.60), channel_id=1, source_target_pairs={{2,4},{6,8},{10,12},{14,16},{18,20},{22,24},{26,28},{30,0},{4,2},{... | collective-permute-start | bytes 393224 | tf_op jit(solution)/shard_map/ppermute | solution.py:433
  39.7 8.9 %collective-permute-start.9 = (f32[16,2048]{1,0:T(8,128)S(1)}, f32[16,2048]{1,0:T(8,128)S(1)}, u32[]{:S(2)}, u32[]{:S(2)}) collective-permute-start(f32[16,2048]{1,0:T(8,128)S(1)} %bitcast.31), channel_id=1, source_target_pairs={{0,1},{1,0},{2,3},{3,2},{4,5},{5,4},{6,7},{7,6},{8,9},{9,8},{10,11... | collective-permute-start | bytes 393224 | tf_op jit(solution)/shard_map/ppermute | solution.py:430
  44.6 3.8 %collective-permute-start.12 = (f32[24,128]{1,0:T(8,128)S(1)}, f32[24,128]{1,0:T(8,128)S(1)}, u32[]{:S(2)}, u32[]{:S(2)}) collective-permute-start(f32[24,128]{1,0:T(8,128)S(1)} %get-tuple-element.71.here), channel_id=1, source_target_pairs={{0,1},{1,0},{2,3},{3,2},{4,5},{5,4},{6,7},{7,6},{8,9},{9,8},{10,11... | collective-permute-start | bytes 36872 | tf_op jit(solution)/shard_map/ppermute | solution.py:430
  48.6 15.0 %collective-permute-start.17 = (f32[9,8,2048]{2,1,0:T(8,128)S(1)}, f32[9,8,2048]{2,1,0:T(8,128)S(1)}, u32[]{:S(2)}, u32[]{:S(2)}) collective-permute-start(f32[9,8,2048]{2,1,0:T(8,128)S(1)} %bitcast.25), channel_id=1, source_target_pairs={{0,1},{1,0},{2,3},{3,2},{4,5},{5,4},{6,7},{7,6},{8,9},{9,8},{10,11... | collective-permute-start | bytes 1769480 | tf_op jit(solution)/shard_map/ppermute | solution.py:430
  50.2 13.4 %collective-permute-start.18 = (f32[16,2048]{1,0:T(8,128)S(1)}, f32[16,2048]{1,0:T(8,128)S(1)}, u32[]{:S(2)}, u32[]{:S(2)}) collective-permute-start(f32[16,2048]{1,0:T(8,128)S(1)} %bitcast.30), channel_id=1, source_target_pairs={{0,1},{1,0},{2,3},{3,2},{4,5},{5,4},{6,7},{7,6},{8,9},{9,8},{10,11... | collective-permute-start | bytes 393224 | tf_op jit(solution)/shard_map/ppermute | solution.py:430
  50.7 1.2 %collective-permute-start.13 = (f32[8,128]{1,0:T(8,128)S(1)}, f32[8,128]{1,0:T(8,128)S(1)}, u32[]{:S(2)}, u32[]{:S(2)}) collective-permute-start(f32[8,128]{1,0:T(8,128)S(1)} %shard_map.83), channel_id=1, source_target_pairs={{0,2},{2,0},{4,6},{6,4},{8,10},{10,8},{12,14},{14,12},{16,18},{18,... | collective-permute-start | bytes 12296 | tf_op jit(solution)/shard_map/ppermute | solution.py:535
  51.9 3.6 %collective-permute-start.14 = (f32[8,128]{1,0:T(8,128)S(1)}, f32[8,128]{1,0:T(8,128)S(1)}, u32[]{:S(2)}, u32[]{:S(2)}) collective-permute-start(f32[8,128]{1,0:T(8,128)S(1)} %add.12), channel_id=1, source_target_pairs={{0,4},{2,6},{4,0},{6,2},{8,12},{10,14},{12,8},{14,10},{16,20},{18,... | collective-permute-start | bytes 12296 | tf_op jit(solution)/shard_map/ppermute | solution.py:535
  55.5 3.6 %collective-permute-start.15 = (f32[8,128]{1,0:T(8,128)S(1)}, f32[8,128]{1,0:T(8,128)S(1)}, u32[]{:S(2)}, u32[]{:S(2)}) collective-permute-start(f32[8,128]{1,0:T(8,128)S(1)} %add.13), channel_id=1, source_target_pairs={{0,8},{2,10},{4,12},{6,14},{8,0},{10,2},{12,4},{14,6},{16,24},{18,... | collective-permute-start | bytes 12296 | tf_op jit(solution)/shard_map/ppermute | solution.py:535
  59.1 4.5 %collective-permute-start.16 = (f32[8,128]{1,0:T(8,128)S(1)}, f32[8,128]{1,0:T(8,128)S(1)}, u32[]{:S(2)}, u32[]{:S(2)}) collective-permute-start(f32[8,128]{1,0:T(8,128)S(1)} %add.14), channel_id=1, source_target_pairs={{0,16},{2,18},{4,20},{6,22},{8,24},{10,26},{12,28},{14,30},{16,0},... | collective-permute-start | bytes 12296 | tf_op jit(solution)/shard_map/ppermute | solution.py:535
